TPU v7x, 32 devices: a whole 2x2x4 slice. The times are simulated.
32 devices in a mesh: row: 4 (over y, core), col: 8 (over z, x).
Axes of the slice: x: 2, y: 2, z: 4, core: 2. Of those that a mesh axis runs over, the one named last changes fastest.
Arguments:
- rhs: float32 [64, 16384], P(None, ('row', 'col')), may hold values from -6 to 6
- self_term: float32 [16384], P(('row', 'col')), may hold values from 4 to 6
- near_tiles: bfloat16 [4096, 256, 256], P(('row', 'col')), may hold values from -0.0241 to 0.0241
- near_rows: int32 [4096], P(('row', 'col')), may hold values from 0 to 15
- near_cols: int32 [4096], P(('row', 'col')), may hold values from 0 to 7
- near_counts: int32 [32], replicated, may hold values from 1 to 128, as said below
- far_left: bfloat16 [2048, 256, 32], P(('row', 'col')), may hold values from -0.125 to 0.125
- far_right: bfloat16 [2048, 256, 32], P(('row', 'col')), may hold values from -0.125 to 0.125
- far_rows: int32 [2048], P(('row', 'col')), may hold values from 0 to 15
- far_cols: int32 [2048], P(('row', 'col')), may hold values from 0 to 7
- nys_factor: float32 [512, 16384], P(None, ('row', 'col')), may hold values from -0.046875 to 0.046875
- nys_weight: float32 [512], replicated, may hold values from 1 to 16
Outputs:
- solution: float32 [64, 16384], P(None, ('row', 'col'))
- residual: float32 [64, 16384], P(None, ('row', 'col'))
Inputs may be any that keep to these rules, and one draw needn't show every extreme that they name: Owner o uses its first near_counts[o] slots; some owner uses all 128.
All inputs are finite; a program needn't handle non-finite values.
Results may differ from a plain program's by a relative error of at most 0.0003.
Values may be sent and summed in bfloat16 or wider, within the bound.
No kernel may reach another device: no remote copies, remote signals or barrier semaphores. Data moves between devices by JAX's collectives and lax.ppermute only.
A program may use at most 128 MiB of HBM per device.

v0:
```python
import jax
import jax.numpy as jnp
from jax import lax
from jax.sharding import PartitionSpec as P

ITERS = 2


def partner(value, axis, bit):
    mask = 2**bit
    pairs = [(source, source ^ mask) for source in range(lax.axis_size(axis))]
    return lax.ppermute(value, axis, pairs)


def chol_solve(matrix, target):
    return jax.scipy.linalg.cho_solve((jnp.linalg.cholesky(matrix), True), target)


def local(
    rhs,
    self_term,
    near_tiles,
    near_rows,
    near_cols,
    near_counts,
    far_left,
    far_right,
    far_rows,
    far_cols,
    nys_factor,
    nys_weight,
):
    highest = lax.Precision.HIGHEST
    width = near_tiles.shape[1]
    rhs_count = rhs.shape[0]
    slot_total = near_tiles.shape[0]
    group = 8
    n_col = lax.axis_size("col")
    grid_row = lax.axis_index("row")
    grid_col = lax.axis_index("col")
    count = near_counts[grid_row * n_col + grid_col]
    lend = max(slot_total // 40 * 8, 8)
    lend_ids = jnp.arange(lend, dtype=jnp.int32)
    partner_count = near_counts[jnp.bitwise_xor(grid_row, 1) * n_col + grid_col]
    give = jnp.clip(count - partner_count, 0, lend)
    take = jnp.clip(partner_count - count, 0, lend)
    give_start = jnp.maximum(count - lend, 0)
    take_start = jnp.maximum(partner_count - lend, 0)
    given_rows = lax.dynamic_slice_in_dim(near_rows, give_start, lend, 0)
    given_tiles = lax.dynamic_slice_in_dim(near_tiles, give_start, lend, 0)
    given_cols = lax.dynamic_slice_in_dim(near_cols, give_start, lend, 0)
    taken_tiles, taken_cols = partner((given_tiles, given_cols), "row", 0)
    taken_slots = take_start + lend_ids
    taken_valid = (taken_slots >= partner_count - take) & (taken_slots < partner_count)
    own_stop = count - give

    def precondition(resid):
        local_proj = jnp.dot(resid, nys_factor.T, precision=highest)
        proj = lax.psum(local_proj, ("row", "col"))
        precond = resid + jnp.dot(proj * nys_weight, nys_factor, precision=highest)
        rho_value = lax.psum(jnp.dot(resid, precond.T, precision=highest), ("row", "col"))
        return (precond, rho_value)

    solution = jnp.zeros_like(rhs)
    residual = rhs
    precond, rho = precondition(residual)
    direc = precond
    for step in range(ITERS):
        packed = direc.astype(jnp.bfloat16)
        col_side = lax.all_gather(packed, "row", axis=1, tiled=True)
        row_side = lax.all_gather(packed, "col", axis=1, tiled=True)
        col_blocks = col_side.reshape(rhs_count, -1, width).transpose(1, 0, 2)
        row_blocks = row_side.reshape(rhs_count, -1, width).transpose(1, 0, 2)
        ids = jnp.arange(group, dtype=jnp.int32)

        def forward_step(index, acc):
            start = index * group
            tiles = lax.dynamic_slice_in_dim(near_tiles, start, group, 0)
            rows = lax.dynamic_slice_in_dim(near_rows, start, group, 0)
            cols = lax.dynamic_slice_in_dim(near_cols, start, group, 0)
            prod = jnp.einsum(
                "gmk,gnk->gmn", col_blocks[cols], tiles, preferred_element_type=jnp.float32
            )
            valid = (start + ids < count)[:, None, None]
            return acc.at[rows].add(jnp.where(valid, prod, 0.0))

        def transposed_step(index, acc):
            start = index * group
            tiles = lax.dynamic_slice_in_dim(near_tiles, start, group, 0)
            rows = lax.dynamic_slice_in_dim(near_rows, start, group, 0)
            cols = lax.dynamic_slice_in_dim(near_cols, start, group, 0)
            prod = jnp.einsum(
                "gmn,gnk->gmk", row_blocks[rows], tiles, preferred_element_type=jnp.float32
            )
            valid = (start + ids < own_stop)[:, None, None]
            return acc.at[cols].add(jnp.where(valid, prod, 0.0))

        forward = jnp.zeros((row_blocks.shape[0], rhs_count, width), jnp.float32)
        forward = lax.fori_loop(0, (count + group - 1) // group, forward_step, forward)
        transposed = jnp.zeros((col_blocks.shape[0], rhs_count, width), jnp.float32)
        transposed = lax.fori_loop(0, (own_stop + group - 1) // group, transposed_step, transposed)
        half_f = jnp.einsum(
            "fmk,fkr->fmr", col_blocks[far_cols], far_right, preferred_element_type=jnp.float32
        ).astype(jnp.bfloat16)
        half_t = jnp.einsum(
            "fmn,fnr->fmr", row_blocks[far_rows], far_left, preferred_element_type=jnp.float32
        ).astype(jnp.bfloat16)
        forward = forward.at[far_rows].add(
            jnp.einsum("fmr,fnr->fmn", half_f, far_left, preferred_element_type=jnp.float32)
        )
        transposed = transposed.at[far_cols].add(
            jnp.einsum("fmr,fkr->fmk", half_t, far_right, preferred_element_type=jnp.float32)
        )
        sent_inputs = row_blocks[given_rows]
        got_inputs = partner(sent_inputs, "row", 0)
        prod = jnp.einsum(
            "gmn,gnk->gmk", got_inputs, taken_tiles, preferred_element_type=jnp.float32
        )
        transposed = transposed.at[taken_cols].add(jnp.where(taken_valid[:, None, None], prod, 0.0))
        row_terms = forward.transpose(1, 0, 2).reshape(rhs_count, -1)
        col_terms = transposed.transpose(1, 0, 2).reshape(rhs_count, -1)
        row_result = lax.psum_scatter(row_terms, "col", scatter_dimension=1, tiled=True)
        col_result = lax.psum_scatter(col_terms, "row", scatter_dimension=1, tiled=True)
        image = self_term * direc + row_result + col_result
        gram = lax.psum(jnp.dot(direc, image.T, precision=highest), ("row", "col"))
        alpha = chol_solve(gram, rho)
        solution = solution + jnp.dot(alpha.T, direc, precision=highest)
        residual = residual - jnp.dot(alpha.T, image, precision=highest)
        if step + 1 < ITERS:
            precond, rho_next = precondition(residual)
            beta = chol_solve(rho, rho_next)
            direc = precond + jnp.dot(beta.T, direc, precision=highest)
            rho = rho_next
    return (solution, residual)


def solution(mesh):
    in_specs = (
        P(None, ("row", "col")),
        P(("row", "col")),
        P(("row", "col"), None, None),
        P(("row", "col")),
        P(("row", "col")),
        P(),
        P(("row", "col"), None, None),
        P(("row", "col"), None, None),
        P(("row", "col")),
        P(("row", "col")),
        P(None, ("row", "col")),
        P(),
    )
    out_specs = (P(None, ("row", "col")), P(None, ("row", "col")))
    return jax.shard_map(local, mesh=mesh, in_specs=in_specs, out_specs=out_specs, check_vma=False)
```

profile of v0, /device:TPU:0, one launch (start us, length us, event | category | flops | bytes accessed | tf_op | source)
XLA Modules:
  0.0 889.5 jit_solution(8666146536382785415)
XLA Ops:
  13.7 3.9 constant_dynamic-slice_fusion
  26.1 114.1 %all-reduce.4.cloned.1.call-done = f32[64,512]{1,0:T(8,128)} async-done(((f32[64,512]{1,0:T(8,128)}), f32[64,512]{1,0:T(8,128)}) %all-reduce.4.cloned.1.call-update) | async-done | bytes 131088 | tf_op jit(solution)/shard_map/psum | solution.py:59
  141.9 31.3 %all_gather.13 = bf16[64,4096]{1,0:T(8,128)(2,1)S(1)} all-gather(bf16[64,512]{1,0:T(8,128)(2,1)S(1)} %get-tuple-element.352), channel_id=1, replica_groups=mesh['row'=4,'col'=8] {'col'}, dimensions={1}, use_global_device_ids=true | all-gather | bytes 589824 | tf_op jit(solution)/shard_map/all_gather | solution.py:71
  173.2 5.8 all_gather.12
  181.0 4.8 while.44
  187.9 5.0 fusion.20
  192.9 8.8 scatter_fusion.4
  208.4 5.0 fusion.21
  213.4 8.8 scatter_fusion.5
  222.2 4.0 convolution_select_fusion.5
  226.2 4.5 scatter_fusion.6
  231.8 101.5 %reduce-scatter.5.cloned.1.call-done = f32[64,512]{1,0:T(8,128)} async-done(((f32[64,4096]{1,0:T(8,128)}), f32[64,512]{1,0:T(8,128)}) %reduce-scatter.5.cloned.1.call-update) | async-done | bytes 131088 | tf_op jit(solution)/shard_map/reduce_scatter | solution.py:122
  333.3 25.8 %reduce-scatter.7.cloned.1.call-done = f32[64,512]{1,0:T(8,128)} async-done(((f32[64,2048]{1,0:T(8,128)}), f32[64,512]{1,0:T(8,128)}) %reduce-scatter.7.cloned.1.call-update) | async-done | bytes 131088 | tf_op jit(solution)/shard_map/reduce_scatter | solution.py:123
  360.3 40.0 %all-reduce = (f32[64,64]{0,1:T(8,128)S(1)}, f32[64,64]{0,1:T(8,128)S(1)}) all-reduce(f32[64,64]{0,1:T(8,128)S(1)} %convolution_bitcast_fusion, f32[64,64]{0,1:T(8,128)S(1)} %fusion.28), channel_id=1, replica_groups=mesh['row'=4,'col'=8] {'row','col'}, use_global_device_ids=true, to_apply=%region_15.17 | all-reduce | flops 8192 | bytes 65536 | tf_op jit(solution)/shard_map/psum | solution.py:61
  400.6 5.8 cholesky.59
  407.7 4.9 custom-call.9
  416.2 5.8 cholesky.70
  423.4 4.9 custom-call.10
  428.3 111.4 %all-reduce.6.cloned.1.call-done = f32[64,512]{1,0:T(8,128)} async-done(((f32[64,512]{1,0:T(8,128)}), f32[64,512]{1,0:T(8,128)}) %all-reduce.6.cloned.1.call-update) | async-done | bytes 131088 | tf_op jit(solution)/shard_map/psum | solution.py:59
  541.7 39.4 %psum.46 = f32[64,64]{1,0:T(8,128)S(1)} all-reduce(f32[64,64]{1,0:T(8,128)S(1)} %fusion.54), channel_id=1, replica_groups=mesh['row'=4,'col'=8] {'row','col'}, use_global_device_ids=true, to_apply=%region_17.20 | all-reduce | flops 4096 | bytes 32768 | tf_op jit(solution)/shard_map/psum | solution.py:61
  582.5 31.2 %all_gather.15 = bf16[64,4096]{1,0:T(8,128)(2,1)S(1)} all-gather(bf16[64,512]{1,0:T(8,128)(2,1)S(1)} %get-tuple-element.354), channel_id=1, replica_groups=mesh['row'=4,'col'=8] {'col'}, dimensions={1}, use_global_device_ids=true | all-gather | bytes 589824 | tf_op jit(solution)/shard_map/all_gather | solution.py:71
  621.1 21.5 %all_gather.14 = bf16[64,2048]{1,0:T(8,128)(2,1)S(1)} all-gather(bf16[64,512]{1,0:T(8,128)(2,1)S(1)} %copy-done.11), channel_id=1, replica_groups=mesh['row'=4,'col'=8] {'row'}, dimensions={1}, use_global_device_ids=true | all-gather | bytes 327680 | tf_op jit(solution)/shard_map/all_gather | solution.py:70
  642.7 4.7 fusion.23
  647.4 8.8 scatter_fusion.8
  662.8 4.0 while.46
  669.1 4.7 fusion.22
  673.9 8.8 scatter_fusion.7
  684.1 18.7 %reduce-scatter.11.cloned.1.call-done = f32[64,512]{1,0:T(8,128)} async-done(((f32[64,2048]{1,0:T(8,128)}), f32[64,512]{1,0:T(8,128)}) %reduce-scatter.11.cloned.1.call-update) | async-done | bytes 131088 | tf_op jit(solution)/shard_map/reduce_scatter | solution.py:123
  702.8 123.1 %reduce-scatter.9.cloned.1.call-done = f32[64,512]{1,0:T(8,128)} async-done(((f32[64,4096]{1,0:T(8,128)}), f32[64,512]{1,0:T(8,128)}) %reduce-scatter.9.cloned.1.call-update) | async-done | bytes 131088 | tf_op jit(solution)/shard_map/reduce_scatter | solution.py:122
  827.1 40.0 %psum.47 = f32[64,64]{0,1:T(8,128)S(1)} all-reduce(f32[64,64]{0,1:T(8,128)S(1)} %fusion.29), channel_id=1, replica_groups=mesh['row'=4,'col'=8] {'row','col'}, use_global_device_ids=true, to_apply=%region_29.32 | all-reduce | flops 4096 | bytes 32768 | tf_op jit(solution)/shard_map/psum | solution.py:125
  867.2 5.8 cholesky.81
  874.4 4.9 custom-call.11
  (173 shorter events, 72.4 us)
Async XLA Ops:
  7.2 180.8 %copy-start = (bf16[64,256,32]{1,2,0:T(8,128)(2,1)S(1)}, bf16[64,256,32]{1,2,0:T(8,128)(2,1)}, u32[]{:S(2)}) copy-start(bf16[64,256,32]{1,2,0:T(8,128)(2,1)} %param.29) | copy-start | bytes 3145732
  7.2 133.0 %all-reduce.4.cloned.1.call-start = ((), (), s32[]{:S(2)}) async-start(), calls=%async_computation.4 | async-start | bytes 262144 | tf_op jit(solution)/shard_map/psum | solution.py:59
  10.4 322.9 %reduce-scatter.5.cloned.1.call-start = ((), (), s32[]{:S(2)}) async-start(), calls=%async_computation.5 | async-start | bytes 1179648 | tf_op jit(solution)/shard_map/reduce_scatter | solution.py:122
  13.2 9.1 %copy-start.30 = (s32[64]{0:T(128)S(1)}, s32[64]{0:T(128)}, u32[]{:S(2)}) copy-start(s32[64]{0:T(128)} %param.32) | copy-start | bytes 772
  13.2 9.1 %copy-start.31 = (s32[64]{0:T(128)S(1)}, s32[64]{0:T(128)}, u32[]{:S(2)}) copy-start(s32[64]{0:T(128)} %param.31) | copy-start | bytes 772
  13.2 9.8 %copy-start.16 = (s32[128]{0:T(128)S(1)}, s32[128]{0:T(128)}, u32[]{:S(2)}) copy-start(s32[128]{0:T(128)} %param.26) | copy-start | bytes 1540
  13.2 127.0 %copy-start.1 = (f32[512,512]{1,0:T(8,128)S(1)}, f32[512,512]{1,0:T(8,128)}, u32[]{:S(2)}) copy-start(f32[512,512]{1,0:T(8,128)} %param.33) | copy-start | bytes 3145732
  13.2 127.0 %copy-start.8 = (f32[64,512]{1,0:T(8,128)S(1)}, f32[64,512]{1,0:T(8,128)}, u32[]{:S(2)}) copy-start(f32[64,512]{1,0:T(8,128)} %param.23) | copy-start | bytes 393220
  13.2 127.0 %copy-start.19 = (f32[512]{0:T(512)S(1)}, f32[512]{0:T(512)}, u32[]{:S(2)}) copy-start(f32[512]{0:T(512)} %param.34) | copy-start | bytes 6148
  13.2 12.3 %collective-permute-start = (s32[24]{0:T(128)S(1)}, s32[24]{0:T(128)S(1)}, u32[]{:S(2)}, u32[]{:S(2)}) collective-permute-start(s32[24]{0:T(128)S(1)} %dynamic_slice.53), channel_id=1, source_target_pairs={{0,8},{8,0},{16,24},{24,16},{1,9},{9,1},{17,25},{25,17},{2,10},{10... | collective-permute-start | bytes 296 | tf_op jit(solution)/shard_map/ppermute | solution.py:12
  17.7 204.5 %collective-permute-start.2 = (bf16[24,256,256]{2,1,0:T(8,128)(2,1)}, bf16[24,256,256]{2,1,0:T(8,128)(2,1)}, u32[]{:S(2)}, u32[]{:S(2)}) collective-permute-start(bf16[24,256,256]{2,1,0:T(8,128)(2,1)} %constant_dynamic-slice_fusion), channel_id=1, source_target_pairs={{0,8},{8,0},{16,24},{24,16},{1,9},{9,1},{17,25},{25,17},{2,10},{10... | collective-permute-start | bytes 9437192 | tf_op jit(solution)/shard_map/ppermute | solution.py:12
  22.3 119.5 %copy-start.24 = (s32[64]{0:T(128)}, s32[64]{0:T(128)S(1)}, u32[]{:S(2)}) copy-start(s32[64]{0:T(128)S(1)} %compare_select_fusion.10) | copy-start | bytes 772
  22.4 156.6 %copy-start.21 = (s32[64]{0:T(128)}, s32[64]{0:T(128)S(1)}, u32[]{:S(2)}) copy-start(s32[64]{0:T(128)S(1)} %compare_select_fusion.11) | copy-start | bytes 772
  23.0 157.5 %copy-start.20 = (s32[1024]{0:T(1024)}, s32[1024]{0:T(1024)S(1)}, u32[]{:S(2)}) copy-start(s32[1024]{0:T(1024)S(1)} %pad_clamp_fusion.4) | copy-start | bytes 12292
  180.5 41.7 %collective-permute-start.1 = (bf16[24,64,256]{2,1,0:T(8,128)(2,1)}, bf16[24,64,256]{2,1,0:T(8,128)(2,1)}, u32[]{:S(2)}, u32[]{:S(2)}) collective-permute-start(bf16[24,64,256]{2,1,0:T(8,128)(2,1)} %gather_fusion.6), channel_id=1, source_target_pairs={{0,8},{8,0},{16,24},{24,16},{1,9},{9,1},{17,25},{25,17},{2,10},{10... | collective-permute-start | bytes 2359304 | tf_op jit(solution)/shard_map/ppermute | solution.py:12
  202.9 156.2 %reduce-scatter.7.cloned.1.call-start = ((), (), s32[]{:S(2)}) async-start(), calls=%async_computation.6 | async-start | bytes 655360 | tf_op jit(solution)/shard_map/reduce_scatter | solution.py:123
  213.4 8.8 copy-start.27
  226.2 132.9 %copy-start.18 = (f32[512]{0:T(512)S(1)}, f32[512]{0:T(512)}, u32[]{:S(2)}) copy-start(f32[512]{0:T(512)} %param.24) | copy-start | bytes 6148
  230.6 183.7 %copy-start.2 = (f32[512,512]{1,0:T(8,128)S(1)}, f32[512,512]{1,0:T(8,128)}, u32[]{:S(2)}) copy-start(f32[512,512]{1,0:T(8,128)} %param.33) | copy-start | bytes 3145732
  231.5 308.3 %all-reduce.6.cloned.1.call-start = ((), (), s32[]{:S(2)}) async-start(), calls=%async_computation.7 | async-start | bytes 262144 | tf_op jit(solution)/shard_map/psum | solution.py:59
  413.1 15.3 %copy-start.14 = (f32[64,64]{1,0:T(8,128)}, f32[64,64]{1,0:T(8,128)S(1)}, u32[]{:S(2)}) copy-start(f32[64,64]{1,0:T(8,128)S(1)} %fusion.43) | copy-start | bytes 49156
  414.4 199.3 %copy-start.5 = (f32[64,512]{1,0:T(8,128)}, f32[64,512]{1,0:T(8,128)S(1)}, u32[]{:S(2)}) copy-start(f32[64,512]{1,0:T(8,128)S(1)} %convolution_subtract_fusion.1) | copy-start | bytes 393220
  416.2 286.6 %reduce-scatter.11.cloned.1.call-start = ((), (), s32[]{:S(2)}) async-start(), calls=%async_computation.9 | async-start | bytes 655360 | tf_op jit(solution)/shard_map/reduce_scatter | solution.py:123
  581.1 34.4 %copy-start.12 = (f32[64,64]{1,0:T(8,128)}, f32[64,64]{1,0:T(8,128)S(1)}, u32[]{:S(2)}) copy-start(f32[64,64]{1,0:T(8,128)S(1)} %psum.46) | copy-start | bytes 49156
  582.5 33.0 %copy-start.10 = (bf16[64,512]{1,0:T(8,128)(2,1)}, bf16[64,512]{1,0:T(8,128)(2,1)S(1)}, u32[]{:S(2)}) copy-start(bf16[64,512]{1,0:T(8,128)(2,1)S(1)} %get-tuple-element.354) | copy-start | bytes 196612
  615.4 40.8 %collective-permute-start.3 = (bf16[24,64,256]{2,1,0:T(8,128)(2,1)}, bf16[24,64,256]{2,1,0:T(8,128)(2,1)}, u32[]{:S(2)}, u32[]{:S(2)}) collective-permute-start(bf16[24,64,256]{2,1,0:T(8,128)(2,1)} %gather_fusion.9), channel_id=1, source_target_pairs={{0,8},{8,0},{16,24},{24,16},{1,9},{9,1},{17,25},{25,17},{2,10},{10... | collective-permute-start | bytes 2359304 | tf_op jit(solution)/shard_map/ppermute | solution.py:12
  618.8 23.9 %copy-start.3 = (bf16[64,256,32]{1,2,0:T(8,128)(2,1)S(1)}, bf16[64,256,32]{1,2,0:T(8,128)(2,1)}, u32[]{:S(2)}) copy-start(bf16[64,256,32]{1,2,0:T(8,128)(2,1)} %param.30) | copy-start | bytes 3145732
  647.4 8.8 copy-start.28
  662.7 163.2 %reduce-scatter.9.cloned.1.call-start = ((), (), s32[]{:S(2)}) async-start(), calls=%async_computation.8 | async-start | bytes 1179648 | tf_op jit(solution)/shard_map/reduce_scatter | solution.py:122
  682.7 143.2 %copy-start.7 = (f32[64,512]{1,0:T(8,128)S(1)}, f32[64,512]{1,0:T(8,128)}, u32[]{:S(2)}) copy-start(f32[64,512]{1,0:T(8,128)} %get-tuple-element.355) | copy-start | bytes 393220
  682.7 196.7 %copy-start.13 = (f32[64,64]{1,0:T(8,128)S(1)}, f32[64,64]{1,0:T(8,128)}, u32[]{:S(2)}) copy-start(f32[64,64]{1,0:T(8,128)} %copy-done.12) | copy-start | bytes 49156
  682.7 198.1 %copy-start.6 = (f32[64,512]{1,0:T(8,128)S(1)}, f32[64,512]{1,0:T(8,128)}, u32[]{:S(2)}) copy-start(f32[64,512]{1,0:T(8,128)} %copy-done.5) | copy-start | bytes 393220
  (10 other events, 36.8 us)
Sparse Core Ops, SparseCore 0:
  14.1 126.0 all-reduce.3
  203.0 130.2 reduce-scatter.4
  336.0 23.0 reduce-scatter.6
  416.3 123.4 all-reduce.5
  662.8 39.9 reduce-scatter.10
  706.4 119.3 reduce-scatter.8
where the time goes:
time: 895 us; the launch traced here: 890 us
  waiting for transfers between devices  495 us (55%)
  blocking collectives  209 us (23%)
  other arithmetic  87.3 us (10%)
  matrix products  50.6 us (6%)
  local copies, waits for them, and re-layouts  25.7 us (3%)
  between operations  20.6 us (2%)
    psum x2, waiting for transfers between devices, precondition(): proj = lax.psum(local_proj, ('row', 'col'))  226 us
    reduce_scatter x2, waiting for transfers between devices, local(): lax.psum_scatter(row_terms, 'col', scatter_dimension=1, tiled=True)  225 us
    psum x2, blocking collectives, precondition(): lax.psum(jnp.dot(resid, precond.T, precision=highest), ('row', 'col'))  79.4 us
    all_gather x2, blocking collectives, local(): row_side = lax.all_gather(packed, 'col', axis=1, tiled=True)  62.5 us
    reduce_scatter x2, waiting for transfers between devices, local(): lax.psum_scatter(col_terms, 'row', scatter_dimension=1, tiled=True)  44.4 us
    psum x1, blocking collectives, local(): gram = lax.psum(jnp.dot(direc, image.T, precision=highest), ('row', 'col'))  40 us
    all_gather x2, blocking collectives, local(): col_side = lax.all_gather(packed, 'row', axis=1, tiled=True)  27.3 us
    another operation x9, other arithmetic, chol_solve(): jnp.linalg.cholesky(matrix)  19.6 us
  transfers between devices with their start and end apart: 10, of which 6 were waited for; matrix products, arithmetic and copies ran while one was open for 13% of the time, Pallas kernels for 0%

commit v1 on v0

v1 whole, which is shorter than its diff:
```python
import functools

import jax
import jax.numpy as jnp
from jax import lax
from jax.experimental import pallas as pl
from jax.experimental.pallas import tpu as pltpu
from jax.sharding import PartitionSpec as P

F32 = jnp.float32
BF16 = jnp.bfloat16
NN = (((1,), (0,)), ((), ()))
NT = (((1,), (1,)), ((), ()))
TN = (((0,), (0,)), ((), ()))


def exact(left, right, dims):
    return lax.dot_general(
        left, right, dims, precision=lax.Precision.HIGHEST, preferred_element_type=F32
    )


def masks_of(axis):
    return [2**bit for bit in range(lax.axis_size(axis).bit_length() - 1)]


def swap(value, axis, mask):
    pairs = [(source, source ^ mask) for source in range(lax.axis_size(axis))]
    return lax.ppermute(value, axis, pairs)


def place(device, masks):
    spot = jnp.zeros_like(device)
    for mask in masks:
        spot = spot * 2 + (jnp.bitwise_and(device, mask) != 0).astype(jnp.int32)
    return spot


def spread_sum(value):
    axes = ("row", "col")
    devices = lax.axis_size("row") * lax.axis_size("col")
    rows, wanted = value.shape
    step = max(devices * 128 // rows, 128)
    columns = (wanted + step - 1) // step * step
    value = jnp.pad(value, ((0, 0), (0, columns - wanted)))
    tiles = value.reshape(rows // 8, 8, columns // 128, 128).transpose(0, 2, 1, 3)
    pieces = tiles.reshape(devices, -1, 128)
    got = lax.all_to_all(pieces, axes, 0, 0, tiled=True)
    part = jnp.sum(got, axis=0)
    same = jnp.broadcast_to(part[None], pieces.shape)
    full = lax.all_to_all(same, axes, 0, 0, tiled=True)
    tiles = full.reshape(rows // 8, columns // 128, 8, 128).transpose(0, 2, 1, 3)
    return tiles.reshape(rows, columns)[:, :wanted]


def product_kernel(
    forward,
    chunk,
    group,
    count_ref,
    src_ref,
    dst_ref,
    far_src_ref,
    far_dst_ref,
    v_ref,
    inner_ref,
    outer_ref,
    tiles_ref,
    out_ref,
    held,
    arrived,
):
    rhs = v_ref.shape[1]
    depth = held.shape[0]
    count = count_ref[0]
    chunks = lax.div(count + (chunk - 1), chunk)

    def fetch(index):
        slot = lax.rem(index, depth)
        return pltpu.make_async_copy(
            tiles_ref.at[pl.ds(index * chunk, chunk)], held.at[slot], arrived.at[slot]
        )

    for index in range(depth - 1):

        @pl.when(index < chunks)
        def _():
            fetch(index).start()

    out_ref[...] = jnp.zeros_like(out_ref)
    panels = far_src_ref.shape[0]
    prank = inner_ref.shape[0] // panels
    shape = (group * rhs, group * prank)
    of_row = lax.div(lax.broadcasted_iota(jnp.int32, shape, 0), rhs)
    of_lane = lax.div(lax.broadcasted_iota(jnp.int32, shape, 1), prank)
    same = of_row == of_lane

    def far(index, carry):
        start = index * group
        v = jnp.concatenate([v_ref[far_src_ref[start + g]] for g in range(group)], axis=0)
        part = pl.ds(pl.multiple_of(start * prank, group * prank), group * prank)
        half = lax.dot_general(v, inner_ref[part, :], NT, preferred_element_type=F32)
        half = jnp.where(same, half, 0.0).astype(BF16)
        prod = lax.dot_general(half, outer_ref[part, :], NN, preferred_element_type=F32)
        for g in range(group):
            out_ref[far_dst_ref[start + g]] += prod[g * rhs : (g + 1) * rhs]
        return carry

    lax.fori_loop(0, panels // group, far, 0)

    def near(index, carry):
        fetch(index).wait()

        @pl.when(index + (depth - 1) < chunks)
        def _():
            fetch(index + (depth - 1)).start()

        slot = lax.rem(index, depth)
        for s in range(chunk):
            tile = index * chunk + s
            v = v_ref[src_ref[tile]]
            v = jnp.where(tile < count, v, jnp.zeros_like(v))
            out_ref[dst_ref[tile]] += lax.dot_general(
                v, held[slot, s], NT if forward else NN, preferred_element_type=F32
            )
        return carry

    lax.fori_loop(0, chunks, near, 0)


def products(forward, v, tiles, count, src, dst, far_src, far_dst, inner, outer, out_blocks):
    slots, width, _ = tiles.shape
    rhs = v.shape[1]
    chunk, depth, group = 32, 3, 8
    smem = pl.BlockSpec(memory_space=pltpu.SMEM)
    vmem = pl.BlockSpec(memory_space=pltpu.VMEM)
    return pl.pallas_call(
        functools.partial(product_kernel, forward, chunk, group),
        out_shape=jax.ShapeDtypeStruct((out_blocks, rhs, width), F32),
        in_specs=[smem] * 5 + [vmem] * 3 + [pl.BlockSpec(memory_space=pl.ANY)],
        out_specs=vmem,
        scratch_shapes=[
            pltpu.VMEM((depth, chunk, width, width), tiles.dtype),
            pltpu.SemaphoreType.DMA((depth,)),
        ],
        compiler_params=pltpu.CompilerParams(vmem_limit_bytes=40 * 2**20),
        cost_estimate=pl.CostEstimate(
            flops=4 * slots * rhs * width * width,
            bytes_accessed=2 * slots * width * width,
            transcendentals=0,
        ),
        name="forward_products" if forward else "transposed_products",
    )(count.reshape(1), src, dst, far_src, far_dst, v, inner, outer, tiles)


def eliminate(system):
    size = system.shape[0]
    at = lax.broadcasted_iota(jnp.int32, (size, 1), 0)
    for k in range(size):
        pivot_row = system[k : k + 1, :] / system[k : k + 1, k : k + 1]
        system = jnp.where(at == k, pivot_row, system - system[:, k : k + 1] * pivot_row)
    return system[:, size:]


def symmetric(matrix):
    return 0.5 * (matrix + matrix.T)


def project_kernel(rhs_ref, factor_ref, out_ref):
    out_ref[...] = exact(rhs_ref[...], factor_ref[...], NT)


def begin_kernel(rhs_ref, proj_ref, weight_ref, factor_ref, direc_ref, packed_ref):
    direc = rhs_ref[...] + exact(proj_ref[...] * weight_ref[...], factor_ref[...], NN)
    direc_ref[...] = direc
    blocks, _, width = packed_ref.shape
    for b in range(blocks):
        packed_ref[b] = direc[:, b * width : (b + 1) * width].astype(BF16)


def image_of(self_ref, direc_ref, row_ref, col_ref):
    blocks = row_ref.shape[0]
    terms = jnp.concatenate([row_ref[b] + col_ref[b] for b in range(blocks)], axis=1)
    return self_ref[...] * direc_ref[...] + terms


def inner_kernel(
    self_ref, direc_ref, row_ref, col_ref, rhs_ref, factor_ref, image_ref, out_ref
):
    image = image_of(self_ref, direc_ref, row_ref, col_ref)
    image_ref[...] = image
    resid = rhs_ref[...]
    count = resid.shape[0]
    rank = factor_ref.shape[0]
    out_ref[:, :rank] = exact(image, factor_ref[...], NT)
    stack = jnp.concatenate([direc_ref[...], resid, image], axis=0)
    against = exact(stack, image, NT)
    own = exact(resid, resid, NT)
    gram, cross, square = against[:count], against[count : 2 * count], against[2 * count :]
    out_ref[:, rank : rank + 2 * count] = jnp.concatenate([gram, cross], axis=1)
    out_ref[:, rank + 2 * count :] = jnp.concatenate([square, own], axis=1)


def advance_kernel(
    sums_ref,
    proj_ref,
    weight_ref,
    factor_ref,
    rhs_ref,
    direc_ref,
    image_ref,
    solution_ref,
    resid_ref,
    next_ref,
    packed_ref,
    rho_ref,
):
    count = rhs_ref.shape[0]
    rank = factor_ref.shape[0]
    image_proj = sums_ref[:, :rank]
    pair = sums_ref[:, rank : rank + 2 * count]
    gram, cross = pair[:, :count], pair[:, count:]
    pair = sums_ref[:, rank + 2 * count :]
    square, own = pair[:, :count], pair[:, count:]
    weight = weight_ref[...]
    proj = proj_ref[...]
    rho = own + exact(proj * weight, proj, NT)
    unit = (
        lax.broadcasted_iota(jnp.int32, (count, count), 0)
        == lax.broadcasted_iota(jnp.int32, (count, count), 1)
    ).astype(F32)
    alpha = eliminate(jnp.concatenate([symmetric(gram), rho], axis=1))
    inverse = eliminate(jnp.concatenate([symmetric(rho), unit], axis=1))
    alpha_t = alpha.T
    proj = proj - exact(alpha_t, image_proj, NN)
    mixed = exact(cross, alpha, NN)
    new = own - mixed - mixed.T + exact(exact(alpha_t, square, NN), alpha, NN)
    new = new + exact(proj * weight, proj, NT)
    beta = exact(inverse, new, NN)
    direc = direc_ref[...]
    resid = rhs_ref[...] - exact(alpha_t, image_ref[...], NN)
    after = resid + exact(proj * weight, factor_ref[...], NN) + exact(beta.T, direc, NN)
    solution_ref[...] = exact(alpha_t, direc, NN)
    resid_ref[...] = resid
    next_ref[...] = after
    rho_ref[...] = new
    blocks, _, width = packed_ref.shape
    for b in range(blocks):
        packed_ref[b] = after[:, b * width : (b + 1) * width].astype(BF16)


def last_image_kernel(self_ref, direc_ref, row_ref, col_ref, image_ref, gram_ref):
    image = image_of(self_ref, direc_ref, row_ref, col_ref)
    image_ref[...] = image
    gram = exact(direc_ref[...], image, NT)
    gram_ref[...] = jnp.concatenate([gram, jnp.zeros_like(gram)], axis=1)


def finish_kernel(
    gram_ref, rho_ref, solution_ref, resid_ref, direc_ref, image_ref, out_ref, left_ref
):
    count = rho_ref.shape[0]
    gram = gram_ref[:, :count]
    alpha = eliminate(jnp.concatenate([symmetric(gram), rho_ref[...]], axis=1))
    alpha_t = alpha.T
    out_ref[...] = solution_ref[...] + exact(alpha_t, direc_ref[...], NN)
    left_ref[...] = resid_ref[...] - exact(alpha_t, image_ref[...], NN)


def call(kernel, outs, name, *operands):
    return pl.pallas_call(
        kernel,
        out_shape=[jax.ShapeDtypeStruct(shape, dtype) for shape, dtype in outs],
        compiler_params=pltpu.CompilerParams(vmem_limit_bytes=40 * 2**20),
        name=name,
    )(*operands)


def local(
    rhs,
    self_term,
    near_tiles,
    near_rows,
    near_cols,
    near_counts,
    far_left,
    far_right,
    far_rows,
    far_cols,
    nys_factor,
    nys_weight,
):
    width = near_tiles.shape[1]
    count_rhs, columns = rhs.shape
    blocks = columns // width
    n_row, n_col = lax.axis_size("row"), lax.axis_size("col")
    grid_row, grid_col = lax.axis_index("row"), lax.axis_index("col")
    count = near_counts[grid_row * n_col + grid_col]
    rank = nys_factor.shape[0]
    self_row = self_term.reshape(1, columns)
    weight = nys_weight.reshape(1, rank)
    prank = far_left.shape[2]
    left = far_left.transpose(0, 2, 1).reshape(-1, width)
    right = far_right.transpose(0, 2, 1).reshape(-1, width)

    col_masks, row_masks = masks_of("col"), masks_of("row")
    gather_col, gather_row = col_masks[::-1], row_masks[::-1]
    path_a = col_masks[-2::-1] + col_masks[-1:]
    path_b = col_masks
    scatter_row = row_masks

    def relative(ids, me):
        return jnp.bitwise_xor(ids // blocks, me), ids % blocks

    def gathered(ids, me, masks):
        device, block = relative(ids, me)
        return place(device, masks[::-1]) * blocks + block

    def scattered_col(ids):
        device, block = relative(ids, grid_col)
        path = jnp.where(block % 2 == 0, place(device, path_a), place(device, path_b))
        return block * n_col + path

    def scattered_row(ids):
        device, block = relative(ids, grid_row)
        return place(device, scatter_row) * blocks + block

    row_src = gathered(near_rows, grid_col, gather_col)
    col_src = gathered(near_cols, grid_row, gather_row)
    far_row_src = gathered(far_rows, grid_col, gather_col)
    far_col_src = gathered(far_cols, grid_row, gather_row)
    row_dst, far_row_dst = scattered_col(near_rows), scattered_col(far_rows)
    col_dst, far_col_dst = scattered_row(near_cols), scattered_row(far_cols)

    def operate(packed):
        col_side = row_side = packed
        for axis_step in range(max(len(gather_col), len(gather_row))):
            if axis_step < len(gather_row):
                got = swap(col_side, "row", gather_row[axis_step])
                col_side = jnp.concatenate([col_side, got], axis=0)
            if axis_step < len(gather_col):
                got = swap(row_side, "col", gather_col[axis_step])
                row_side = jnp.concatenate([row_side, got], axis=0)
        forward = products(
            True, col_side, near_tiles, count, col_src, row_dst,
            far_col_src, far_row_dst, right, left, n_col * blocks,
        )
        transposed = products(
            False, row_side, near_tiles, count, row_src, col_dst,
            far_row_src, far_col_dst, left, right, n_row * blocks,
        )
        parts = [forward[b * n_col : (b + 1) * n_col] for b in range(blocks)]
        for step in range(len(col_masks)):
            for b in range(blocks):
                mask = (path_a if b % 2 == 0 else path_b)[step]
                half = parts[b].shape[0] // 2
                parts[b] = parts[b][:half] + swap(parts[b][half:], "col", mask)
        for mask in scatter_row:
            half = transposed.shape[0] // 2
            transposed = transposed[:half] + swap(transposed[half:], "row", mask)
        return jnp.concatenate(parts, axis=0), transposed

    full, pack = (count_rhs, columns), (blocks, count_rhs, width)
    square = (count_rhs, count_rhs)
    (partial,) = call(
        project_kernel, [((count_rhs, rank), F32)], "project", rhs, nys_factor
    )
    proj = spread_sum(partial)
    direc, packed = call(
        begin_kernel, [(full, F32), (pack, BF16)], "begin", rhs, proj, weight, nys_factor
    )
    row_part, col_part = operate(packed)
    image, partial = call(
        inner_kernel, [(full, F32), ((count_rhs, rank + 4 * count_rhs), F32)], "inner",
        self_row, direc, row_part, col_part, rhs, nys_factor,
    )
    sums = spread_sum(partial)
    solution, residual, direc, packed, rho = call(
        advance_kernel, [(full, F32), (full, F32), (full, F32), (pack, BF16), (square, F32)],
        "advance", sums, proj, weight, nys_factor, rhs, direc, image,
    )
    row_part, col_part = operate(packed)
    image, partial = call(
        last_image_kernel, [(full, F32), ((count_rhs, 2 * count_rhs), F32)], "last_image",
        self_row, direc, row_part, col_part,
    )
    gram = spread_sum(partial)
    return tuple(
        call(
            finish_kernel, [(full, F32), (full, F32)], "finish",
            gram, rho, solution, residual, direc, image,
        )
    )


def solution(mesh):
    in_specs = (
        P(None, ("row", "col")),
        P(("row", "col")),
        P(("row", "col"), None, None),
        P(("row", "col")),
        P(("row", "col")),
        P(),
        P(("row", "col"), None, None),
        P(("row", "col"), None, None),
        P(("row", "col")),
        P(("row", "col")),
        P(None, ("row", "col")),
        P(),
    )
    out_specs = (P(None, ("row", "col")), P(None, ("row", "col")))
    return jax.shard_map(local, mesh=mesh, in_specs=in_specs, out_specs=out_specs, check_vma=False)
```

time: 895 us -> 227 us (0.25)
  waiting for transfers between devices: 495 us -> 70.3 us
  blocking collectives: 209 us -> 45.5 us
  other arithmetic: 87.3 us -> 5.29 us
  Pallas kernels: 0 us -> 52.9 us
  matrix products: 50.6 us -> 0 us
  starting transfers between devices: 1.28 us -> 27.1 us
  between operations: 20.6 us -> 1.4 us
    reduce_scatter x4 -> x0, waiting for transfers between devices: 269 us -> none  [the longest x2 225 us: local(): lax.psum_scatter(row_terms, 'col', scatter_dimension=1, tiled=True)]
    psum x2 -> x0, waiting for transfers between devices: 226 us -> none  [precondition(): proj = lax.psum(local_proj, ('row', 'col'))]
    psum x3 -> x0, blocking collectives: 119 us -> none  [the longest x2 79.4 us: precondition(): lax.psum(jnp.dot(resid, precond.T, precision=highest), ('row', 'col'))]
    all_gather x4 -> x0, blocking collectives: 89.8 us -> none  [the longest x2 62.5 us: local(): row_side = lax.all_gather(packed, 'col', axis=1, tiled=True)]
    ppermute x4 -> x26, waiting for transfers between devices: 0.01 us -> 56.3 us  [swap(): return lax.ppermute(value, axis, pairs)]
    pallas_call x0 -> x10, Pallas kernels: none -> 52.9 us  [the longest x4 33.6 us: products(): pl.pallas_call(functools.partial(product_kernel, forward, chunk, group),...]
    dot_general x23 -> x0, matrix products: 49.4 us -> none  [the longest x2 9.74 us: local(): jnp.einsum('fmr,fnr->fmn', half_f, far_left, preferred_element_type=jnp.f...]
    scatter-add x10 -> x0, other arithmetic: 46.5 us -> none  [the longest x2 17.6 us: local(): forward.at[far_rows]]
  transfers between devices with their start and end apart: 10 -> 28, of which waited for: 6 -> 16; matrix products, arithmetic and copies ran while one was open for 13% -> 2% of each run, Pallas kernels for 0% -> 7%
where the time goes in v1:
time: 227 us; the launch traced here: 225 us
  waiting for transfers between devices  70.3 us (31%)
  Pallas kernels  52.9 us (23%)
  blocking collectives  45.5 us (20%)
  starting transfers between devices  27.1 us (12%)
  local copies, waits for them, and re-layouts  23 us (10%)
  other arithmetic  5.29 us (2%)
    ppermute x26, waiting for transfers between devices, swap(): return lax.ppermute(value, axis, pairs)  56.3 us
    pallas_call x4, Pallas kernels, products(): pl.pallas_call(functools.partial(product_kernel, forward, chunk, group),...  33.6 us
    all_to_all x2, blocking collectives, spread_sum(): got = lax.all_to_all(pieces, axes, 0, 0, tiled=True)  23.6 us
    all_to_all x2, blocking collectives, spread_sum(): full = lax.all_to_all(same, axes, 0, 0, tiled=True)  21.9 us
    pallas_call x6, Pallas kernels, call(): pl.pallas_call(kernel, out_shape=[jax.ShapeDtypeStruct(shape, dtype) for...  19.2 us
    unnamed x70, local copies, waits for them, and re-layouts  17.5 us
    ppermute x26, starting transfers between devices, swap(): return lax.ppermute(value, axis, pairs)  17.2 us
    all_to_all x1, waiting for transfers between devices, spread_sum(): full = lax.all_to_all(same, axes, 0, 0, tiled=True)  7.67 us
  transfers between devices with their start and end apart: 28, of which 16 were waited for; matrix products, arithmetic and copies ran while one was open for 2% of the time, Pallas kernels for 7%

profile of v1, /device:TPU:0, one launch (start us, length us, event | category | flops | bytes accessed | tf_op | source)
XLA Modules:
  0.0 225.4 jit_solution(3448676498984158395)
XLA Ops:
  2.9 1.8 project.1
  4.7 7.3 %all-to-all-start = ((f32[32,8,128]{2,1,0:T(8,128)}), f32[32,8,128]{2,1,0:T(8,128)S(1)}, u32[]{:S(2)}, u32[]{:S(2)}) async-start(f32[32,8,128]{2,1,0:T(8,128)} %bitcast.3), calls=%async_computation | async-start | bytes 262144 | tf_op jit(solution)/shard_map/all_to_all | solution.py:48
  13.4 6.4 %all-to-all-done = f32[32,8,128]{2,1,0:T(8,128)S(1)} async-done(((f32[32,8,128]{2,1,0:T(8,128)}), f32[32,8,128]{2,1,0:T(8,128)S(1)}, u32[]{:S(2)}, u32[]{:S(2)}) %all-to-all-start) | async-done | bytes 131104 | tf_op jit(solution)/shard_map/all_to_all | solution.py:48
  20.4 2.6 %all-to-all-start.1 = ((f32[32,8,128]{2,1,0:T(8,128)}), f32[32,8,128]{2,1,0:T(8,128)S(1)}, u32[]{:S(2)}, u32[]{:S(2)}) async-start(f32[32,8,128]{2,1,0:T(8,128)} %broadcast_in_dim.6), calls=%async_computation.1 | async-start | bytes 262144 | tf_op jit(solution)/shard_map/all_to_all | solution.py:51
  23.1 7.7 %all-to-all-done.1 = f32[32,8,128]{2,1,0:T(8,128)S(1)} async-done(((f32[32,8,128]{2,1,0:T(8,128)}), f32[32,8,128]{2,1,0:T(8,128)S(1)}, u32[]{:S(2)}, u32[]{:S(2)}) %all-to-all-start.1) | async-done | bytes 131104 | tf_op jit(solution)/shard_map/all_to_all | solution.py:51
  38.8 2.5 %collective-permute-done.8 = bf16[2,64,256]{2,1,0:T(8,128)(2,1)S(1)} collective-permute-done((bf16[2,64,256]{2,1,0:T(8,128)(2,1)S(1)}, bf16[2,64,256]{2,1,0:T(8,128)(2,1)S(1)}, u32[]{:S(2)}, u32[]{:S(2)}) %collective-permute-start.8) | collective-permute-done | bytes 65568 | tf_op jit(solution)/shard_map/ppermute | solution.py:29
  42.2 4.6 %collective-permute-done.9 = bf16[4,64,256]{2,1,0:T(8,128)(2,1)S(1)} collective-permute-done((bf16[4,64,256]{2,1,0:T(8,128)(2,1)S(1)}, bf16[4,64,256]{2,1,0:T(8,128)(2,1)S(1)}, u32[]{:S(2)}, u32[]{:S(2)}) %collective-permute-start.9) | collective-permute-done | bytes 131104 | tf_op jit(solution)/shard_map/ppermute | solution.py:29
  49.3 9.0 %forward_products.2 = f32[16,64,256]{2,1,0:T(8,128)S(1)} custom-call(s32[1]{0:T(128)} %dynamic_slice.3.count_ref, s32[128]{0:T(128)S(1)} %fusion.4.src_ref.dst_ref, s32[128]{0:T(128)S(1)} %multiply_add_fusion.3.dst_ref, s32[64]{0:T(128)S(1)} %fusion.5.far_src_ref.far_dst_ref, s32[64]{0:T(128)S(1)} %multiply_add_fusion.2.far_dst_ref, ...), custom_call_target="tpu_custom_call" | custom-call | flops 2147483648 | bytes 16777216 | tf_op jit(solution)/shard_map/forward_products/pallas_call | solution.py:137
  58.6 7.2 %collective-permute-done.2 = f32[4,64,256]{2,1,0:T(8,128)S(1)} collective-permute-done((f32[4,64,256]{2,1,0:T(8,128)S(1)}, f32[4,64,256]{2,1,0:T(8,128)S(1)}, u32[]{:S(2)}, u32[]{:S(2)}) %collective-permute-start.2) | collective-permute-done | bytes 262176 | tf_op jit(solution)/shard_map/ppermute | solution.py:29
  66.0 2.0 collective-permute-start.5
  68.9 3.5 %collective-permute-done.3 = f32[2,64,256]{2,1,0:T(8,128)S(1)} collective-permute-done((f32[2,64,256]{2,1,0:T(8,128)S(1)}, f32[2,64,256]{2,1,0:T(8,128)S(1)}, u32[]{:S(2)}, u32[]{:S(2)}) %collective-permute-start.3) | collective-permute-done | bytes 131104 | tf_op jit(solution)/shard_map/ppermute | solution.py:29
  73.3 7.8 %transposed_products.2 = f32[8,64,256]{2,1,0:T(8,128)S(1)} custom-call(s32[1]{0:T(128)} %dynamic_slice.3.count_ref, s32[128]{0:T(128)S(1)} %get-tuple-element.28.src_ref, s32[128]{0:T(128)S(1)} %fusion.4.src_ref.dst_ref, s32[64]{0:T(128)S(1)} %get-tuple-element.24.far_src_ref, s32[64]{0:T(128)S(1)} %fusion.5.far_src_ref.far_dst_ref, ...), custom_call_target="tpu_custom_call" | custom-call | flops 2147483648 | bytes 16777216 | tf_op jit(solution)/shard_map/transposed_products/pallas_call | solution.py:137
  82.9 4.4 %collective-permute-done.6 = f32[2,64,256]{2,1,0:T(8,128)S(1)} collective-permute-done((f32[2,64,256]{2,1,0:T(8,128)S(1)}, f32[2,64,256]{2,1,0:T(8,128)S(1)}, u32[]{:S(2)}, u32[]{:S(2)}) %collective-permute-start.6) | collective-permute-done | bytes 131104 | tf_op jit(solution)/shard_map/ppermute | solution.py:29
  87.4 3.6 %collective-permute-start.7 = (f32[1,64,256]{2,1,0:T(8,128)S(1)}, f32[1,64,256]{2,1,0:T(8,128)S(1)}, u32[]{:S(2)}, u32[]{:S(2)}) collective-permute-start(f32[1,64,256]{2,1,0:T(8,128)S(1)} %slice.151), channel_id=1, source_target_pairs={{0,4},{1,5},{2,6},{3,7},{4,0},{5,1},{6,2},{7,3},{8,12},{9,13},{10,... | collective-permute-start | bytes 196616 | tf_op jit(solution)/shard_map/ppermute | solution.py:29
  91.0 3.3 %collective-permute-done.7 = f32[1,64,256]{2,1,0:T(8,128)S(1)} collective-permute-done((f32[1,64,256]{2,1,0:T(8,128)S(1)}, f32[1,64,256]{2,1,0:T(8,128)S(1)}, u32[]{:S(2)}, u32[]{:S(2)}) %collective-permute-start.7) | collective-permute-done | bytes 65568 | tf_op jit(solution)/shard_map/ppermute | solution.py:29
  98.9 14.0 %all_to_all.30 = f32[32,12,128]{2,1,0:T(8,128)} all-to-all(f32[32,12,128]{2,1,0:T(8,128)} %reshape.52), channel_id=1, replica_groups=mesh['row'=4,'col'=8] {'row','col'}, dimensions={0} | all-to-all | bytes 393216 | tf_op jit(solution)/shard_map/all_to_all | solution.py:48
  114.0 13.0 %all_to_all.31 = f32[32,12,128]{2,1,0:T(8,128)} all-to-all(f32[32,12,128]{2,1,0:T(8,128)S(1)} %broadcast_in_dim.7), channel_id=1, replica_groups=mesh['row'=4,'col'=8] {'row','col'}, dimensions={0} | all-to-all | bytes 393216 | tf_op jit(solution)/shard_map/all_to_all | solution.py:51
  131.4 8.3 %advance.1 = (f32[64,512]{1,0:T(8,128)S(1)}, f32[64,512]{1,0:T(8,128)S(1)}, f32[64,512]{1,0:T(8,128)S(1)}, bf16[2,64,256]{2,1,0:T(8,128)(2,1)S(1)}, f32[64,64]{1,0:T(8,128)S(1)}) custom-call(f32[64,768]{1,0:T(8,128)S(1)} %bitcast.38, f32[64,512]{1,0:T(8,128)S(1)} %bitcast.37, f32[1,512]{1,0:T(1,128)S(1)} %bitcast.45, f32[512,512]{1,0:T(8,128)S(1)} %copy-done.6, ...), custom_call_target="tpu_custom_call" | custom-call | tf_op jit(solution)/shard_map/advance/pallas_call | solution.py:271
  140.7 5.1 %collective-permute-done.21 = bf16[2,64,256]{2,1,0:T(8,128)(2,1)S(1)} collective-permute-done((bf16[2,64,256]{2,1,0:T(8,128)(2,1)S(1)}, bf16[2,64,256]{2,1,0:T(8,128)(2,1)S(1)}, u32[]{:S(2)}, u32[]{:S(2)}) %collective-permute-start.21) | collective-permute-done | bytes 65568 | tf_op jit(solution)/shard_map/ppermute | solution.py:29
  146.1 4.9 %collective-permute-done.22 = bf16[4,64,256]{2,1,0:T(8,128)(2,1)S(1)} collective-permute-done((bf16[4,64,256]{2,1,0:T(8,128)(2,1)S(1)}, bf16[4,64,256]{2,1,0:T(8,128)(2,1)S(1)}, u32[]{:S(2)}, u32[]{:S(2)}) %collective-permute-start.22) | collective-permute-done | bytes 131104 | tf_op jit(solution)/shard_map/ppermute | solution.py:29
  152.3 9.0 %forward_products.3 = f32[16,64,256]{2,1,0:T(8,128)S(1)} custom-call(s32[1]{0:T(128)} %dynamic_slice.3.count_ref, s32[128]{0:T(128)S(1)} %fusion.4.src_ref.dst_ref, s32[128]{0:T(128)S(1)} %copy-done.27, s32[64]{0:T(128)S(1)} %fusion.5.far_src_ref.far_dst_ref, s32[64]{0:T(128)S(1)} %copy-done.29, bf16[8,64,256]{2,1,0:T(8,128)(2,1)S(1)} %get-tuple-element.37.v_ref, ...), custom_call_target="tpu_custom_call" | custom-call | flops 2147483648 | bytes 16777216 | tf_op jit(solution)/shard_map/forward_products/pallas_call | solution.py:137
  161.5 6.3 %collective-permute-done.15 = f32[4,64,256]{2,1,0:T(8,128)S(1)} collective-permute-done((f32[4,64,256]{2,1,0:T(8,128)S(1)}, f32[4,64,256]{2,1,0:T(8,128)S(1)}, u32[]{:S(2)}, u32[]{:S(2)}) %collective-permute-start.15) | collective-permute-done | bytes 262176 | tf_op jit(solution)/shard_map/ppermute | solution.py:29
  167.9 2.0 collective-permute-start.18
  170.0 3.5 %collective-permute-done.16 = f32[2,64,256]{2,1,0:T(8,128)S(1)} collective-permute-done((f32[2,64,256]{2,1,0:T(8,128)S(1)}, f32[2,64,256]{2,1,0:T(8,128)S(1)}, u32[]{:S(2)}, u32[]{:S(2)}) %collective-permute-start.16) | collective-permute-done | bytes 131104 | tf_op jit(solution)/shard_map/ppermute | solution.py:29
  173.5 2.5 %collective-permute-start.17 = (f32[1,64,256]{2,1,0:T(8,128)S(1)}, f32[1,64,256]{2,1,0:T(8,128)S(1)}, u32[]{:S(2)}, u32[]{:S(2)}) collective-permute-start(f32[1,64,256]{2,1,0:T(8,128)S(1)} %slice.161), channel_id=1, source_target_pairs={{0,4},{1,5},{2,6},{3,7},{4,0},{5,1},{6,2},{7,3},{8,12},{9,13},{10,... | collective-permute-start | bytes 196616 | tf_op jit(solution)/shard_map/ppermute | solution.py:29
  177.4 7.8 %transposed_products.3 = f32[8,64,256]{2,1,0:T(8,128)S(1)} custom-call(s32[1]{0:T(128)} %dynamic_slice.3.count_ref, s32[128]{0:T(128)S(1)} %copy-done.31, s32[128]{0:T(128)S(1)} %fusion.4.src_ref.dst_ref, s32[64]{0:T(128)S(1)} %copy-done.33, s32[64]{0:T(128)S(1)} %fusion.5.far_src_ref.far_dst_ref, bf16[16,64,256]{2,1,0:T(8,128)(2,1)S(1)} %pad_maximum_fusion.1.v_ref, ...), custom_call_target="tpu_custom_call" | custom-call | flops 2147483648 | bytes 16777216 | tf_op jit(solution)/shard_map/transposed_products/pallas_call | solution.py:137
  187.0 4.4 %collective-permute-done.19 = f32[2,64,256]{2,1,0:T(8,128)S(1)} collective-permute-done((f32[2,64,256]{2,1,0:T(8,128)S(1)}, f32[2,64,256]{2,1,0:T(8,128)S(1)}, u32[]{:S(2)}, u32[]{:S(2)}) %collective-permute-start.19) | collective-permute-done | bytes 131104 | tf_op jit(solution)/shard_map/ppermute | solution.py:29
  191.4 2.0 collective-permute-start.20
  193.4 4.0 %collective-permute-done.20 = f32[1,64,256]{2,1,0:T(8,128)S(1)} collective-permute-done((f32[1,64,256]{2,1,0:T(8,128)S(1)}, f32[1,64,256]{2,1,0:T(8,128)S(1)}, u32[]{:S(2)}, u32[]{:S(2)}) %collective-permute-start.20) | collective-permute-done | bytes 65568 | tf_op jit(solution)/shard_map/ppermute | solution.py:29
  197.7 9.6 %all_to_all.32 = f32[32,2,128]{2,1,0:T(2,128)S(1)} all-to-all(f32[32,2,128]{2,1,0:T(2,128)S(1)} %bitcast.41), channel_id=1, replica_groups=mesh['row'=4,'col'=8] {'row','col'}, dimensions={0} | all-to-all | bytes 65536 | tf_op jit(solution)/shard_map/all_to_all | solution.py:48
  207.3 8.9 %all_to_all.33 = f32[32,2,128]{2,1,0:T(2,128)S(1)} all-to-all(f32[32,2,128]{2,1,0:T(2,128)S(1)} %broadcast_in_dim.8), channel_id=1, replica_groups=mesh['row'=4,'col'=8] {'row','col'}, dimensions={0} | all-to-all | bytes 65536 | tf_op jit(solution)/shard_map/all_to_all | solution.py:51
  218.8 6.6 %finish.1 = (f32[64,512]{1,0:T(8,128)}, f32[64,512]{1,0:T(8,128)}) custom-call(f32[64,128]{1,0:T(8,128)S(1)} %bitcast.40, f32[64,64]{1,0:T(8,128)S(1)} %copy-done.22, f32[64,512]{1,0:T(8,128)S(1)} %copy-done.16, f32[64,512]{1,0:T(8,128)S(1)} %copy-done.18, f32[64,512]{1,0:T(8,128)S(1)} %get-tuple-element.17.direc_ref, f32[64,512]{1,0:T(8,128)S(1)} %get-tuple-element.23.image_ref), custom_call_target="tpu_custom_call" | custom-call | tf_op jit(solution)/shard_map/finish/pallas_call | solution.py:271
  (161 shorter events, 38.5 us)
Async XLA Ops:
  0.6 72.7 %copy-start.1 = (bf16[64,256,32]{1,2,0:T(8,128)(2,1)S(1)}, bf16[64,256,32]{1,2,0:T(8,128)(2,1)}, u32[]{:S(2)}) copy-start(bf16[64,256,32]{1,2,0:T(8,128)(2,1)} %param.19) | copy-start | bytes 3145732
  0.6 72.7 %copy-start.3 = (bf16[64,256,32]{1,2,0:T(8,128)(2,1)S(1)}, bf16[64,256,32]{1,2,0:T(8,128)(2,1)}, u32[]{:S(2)}) copy-start(bf16[64,256,32]{1,2,0:T(8,128)(2,1)} %param.18) | copy-start | bytes 3145732
  4.7 15.0 %all-to-all-start = ((f32[32,8,128]{2,1,0:T(8,128)}), f32[32,8,128]{2,1,0:T(8,128)S(1)}, u32[]{:S(2)}, u32[]{:S(2)}) async-start(f32[32,8,128]{2,1,0:T(8,128)} %bitcast.3), calls=%async_computation | async-start | bytes 262144 | tf_op jit(solution)/shard_map/all_to_all | solution.py:48
  12.7 68.5 %copy-start.30 = (s32[128]{0:T(128)}, s32[128]{0:T(128)S(1)}, u32[]{:S(2)}) copy-start(s32[128]{0:T(128)S(1)} %get-tuple-element.28.src_ref) | copy-start | bytes 1540
  20.4 10.3 %all-to-all-start.1 = ((f32[32,8,128]{2,1,0:T(8,128)}), f32[32,8,128]{2,1,0:T(8,128)S(1)}, u32[]{:S(2)}, u32[]{:S(2)}) async-start(f32[32,8,128]{2,1,0:T(8,128)} %broadcast_in_dim.6), calls=%async_computation.1 | async-start | bytes 262144 | tf_op jit(solution)/shard_map/all_to_all | solution.py:51
  35.0 6.4 %collective-permute-start.8 = (bf16[2,64,256]{2,1,0:T(8,128)(2,1)S(1)}, bf16[2,64,256]{2,1,0:T(8,128)(2,1)S(1)}, u32[]{:S(2)}, u32[]{:S(2)}) collective-permute-start(bf16[2,64,256]{2,1,0:T(8,128)(2,1)S(1)} %get-tuple-element.14), channel_id=1, source_target_pairs={{0,4},{1,5},{2,6},{3,7},{4,0},{5,1},{6,2},{7,3},{8,12},{9,13},{10,... | collective-permute-start | bytes 196616 | tf_op jit(solution)/shard_map/ppermute | solution.py:29
  36.3 5.1 %collective-permute-start = (bf16[2,64,256]{2,1,0:T(8,128)(2,1)S(1)}, bf16[2,64,256]{2,1,0:T(8,128)(2,1)S(1)}, u32[]{:S(2)}, u32[]{:S(2)}) collective-permute-start(bf16[2,64,256]{2,1,0:T(8,128)(2,1)S(1)} %get-tuple-element.14), channel_id=1, source_target_pairs={{0,16},{8,24},{16,0},{24,8},{1,17},{9,25},{17,1},{25,9},{2,18},{10... | collective-permute-start | bytes 196616 | tf_op jit(solution)/shard_map/ppermute | solution.py:29
  41.4 5.4 %collective-permute-start.9 = (bf16[4,64,256]{2,1,0:T(8,128)(2,1)S(1)}, bf16[4,64,256]{2,1,0:T(8,128)(2,1)S(1)}, u32[]{:S(2)}, u32[]{:S(2)}) collective-permute-start(bf16[4,64,256]{2,1,0:T(8,128)(2,1)S(1)} %get-tuple-element.42), channel_id=1, source_target_pairs={{0,2},{1,3},{2,0},{3,1},{4,6},{5,7},{6,4},{7,5},{8,10},{9,11},{10,... | collective-permute-start | bytes 393224 | tf_op jit(solution)/shard_map/ppermute | solution.py:29
  41.5 5.3 %collective-permute-start.1 = (bf16[4,64,256]{2,1,0:T(8,128)(2,1)S(1)}, bf16[4,64,256]{2,1,0:T(8,128)(2,1)S(1)}, u32[]{:S(2)}, u32[]{:S(2)}) collective-permute-start(bf16[4,64,256]{2,1,0:T(8,128)(2,1)S(1)} %get-tuple-element.43), channel_id=1, source_target_pairs={{0,8},{8,0},{16,24},{24,16},{1,9},{9,1},{17,25},{25,17},{2,10},{10... | collective-permute-start | bytes 393224 | tf_op jit(solution)/shard_map/ppermute | solution.py:29
  58.4 70.3 %copy-start.25 = (f32[512]{0:T(512)S(1)}, f32[512]{0:T(512)}, u32[]{:S(2)}) copy-start(f32[512]{0:T(512)} %param.23) | copy-start | bytes 6148
  58.4 7.4 %collective-permute-start.2 = (f32[4,64,256]{2,1,0:T(8,128)S(1)}, f32[4,64,256]{2,1,0:T(8,128)S(1)}, u32[]{:S(2)}, u32[]{:S(2)}) collective-permute-start(f32[4,64,256]{2,1,0:T(8,128)S(1)} %slice.141), channel_id=1, source_target_pairs={{0,2},{1,3},{2,0},{3,1},{4,6},{5,7},{6,4},{7,5},{8,10},{9,11},{10,... | collective-permute-start | bytes 786440 | tf_op jit(solution)/shard_map/ppermute | solution.py:29
  58.5 9.5 %collective-permute-start.10 = (bf16[8,64,256]{2,1,0:T(8,128)(2,1)S(1)}, bf16[8,64,256]{2,1,0:T(8,128)(2,1)S(1)}, u32[]{:S(2)}, u32[]{:S(2)}) collective-permute-start(bf16[8,64,256]{2,1,0:T(8,128)(2,1)S(1)} %get-tuple-element.40), channel_id=1, source_target_pairs={{0,1},{1,0},{2,3},{3,2},{4,5},{5,4},{6,7},{7,6},{8,9},{9,8},{10,11... | collective-permute-start | bytes 786440 | tf_op jit(solution)/shard_map/ppermute | solution.py:29
  65.9 6.4 %collective-permute-start.3 = (f32[2,64,256]{2,1,0:T(8,128)S(1)}, f32[2,64,256]{2,1,0:T(8,128)S(1)}, u32[]{:S(2)}, u32[]{:S(2)}) collective-permute-start(f32[2,64,256]{2,1,0:T(8,128)S(1)} %slice.143), channel_id=1, source_target_pairs={{0,1},{1,0},{2,3},{3,2},{4,5},{5,4},{6,7},{7,6},{8,9},{9,8},{10,11... | collective-permute-start | bytes 393224 | tf_op jit(solution)/shard_map/ppermute | solution.py:29
  66.0 15.3 %collective-permute-start.5 = (f32[4,64,256]{2,1,0:T(8,128)S(1)}, f32[4,64,256]{2,1,0:T(8,128)S(1)}, u32[]{:S(2)}, u32[]{:S(2)}) collective-permute-start(f32[4,64,256]{2,1,0:T(8,128)S(1)} %get-tuple-element.35), channel_id=1, source_target_pairs={{0,1},{1,0},{2,3},{3,2},{4,5},{5,4},{6,7},{7,6},{8,9},{9,8},{10,11... | collective-permute-start | bytes 786440 | tf_op jit(solution)/shard_map/ppermute | solution.py:29
  72.4 8.9 %collective-permute-start.4 = (f32[1,64,256]{2,1,0:T(8,128)S(1)}, f32[1,64,256]{2,1,0:T(8,128)S(1)}, u32[]{:S(2)}, u32[]{:S(2)}) collective-permute-start(f32[1,64,256]{2,1,0:T(8,128)S(1)} %slice.145), channel_id=1, source_target_pairs={{0,4},{1,5},{2,6},{3,7},{4,0},{5,1},{6,2},{7,3},{8,12},{9,13},{10,... | collective-permute-start | bytes 196616 | tf_op jit(solution)/shard_map/ppermute | solution.py:29
  81.2 1.6 collective-permute-start.11
  81.4 6.0 %collective-permute-start.6 = (f32[2,64,256]{2,1,0:T(8,128)S(1)}, f32[2,64,256]{2,1,0:T(8,128)S(1)}, u32[]{:S(2)}, u32[]{:S(2)}) collective-permute-start(f32[2,64,256]{2,1,0:T(8,128)S(1)} %slice.149), channel_id=1, source_target_pairs={{0,2},{1,3},{2,0},{3,1},{4,6},{5,7},{6,4},{7,5},{8,10},{9,11},{10,... | collective-permute-start | bytes 393224 | tf_op jit(solution)/shard_map/ppermute | solution.py:29
  82.9 8.1 %collective-permute-start.12 = (f32[2,64,256]{2,1,0:T(8,128)S(1)}, f32[2,64,256]{2,1,0:T(8,128)S(1)}, u32[]{:S(2)}, u32[]{:S(2)}) collective-permute-start(f32[2,64,256]{2,1,0:T(8,128)S(1)} %slice.155), channel_id=1, source_target_pairs={{0,16},{8,24},{16,0},{24,8},{1,17},{9,25},{17,1},{25,9},{2,18},{10... | collective-permute-start | bytes 393224 | tf_op jit(solution)/shard_map/ppermute | solution.py:29
  87.4 6.9 %collective-permute-start.7 = (f32[1,64,256]{2,1,0:T(8,128)S(1)}, f32[1,64,256]{2,1,0:T(8,128)S(1)}, u32[]{:S(2)}, u32[]{:S(2)}) collective-permute-start(f32[1,64,256]{2,1,0:T(8,128)S(1)} %slice.151), channel_id=1, source_target_pairs={{0,4},{1,5},{2,6},{3,7},{4,0},{5,1},{6,2},{7,3},{8,12},{9,13},{10,... | collective-permute-start | bytes 196616 | tf_op jit(solution)/shard_map/ppermute | solution.py:29
  139.7 6.2 %collective-permute-start.21 = (bf16[2,64,256]{2,1,0:T(8,128)(2,1)S(1)}, bf16[2,64,256]{2,1,0:T(8,128)(2,1)S(1)}, u32[]{:S(2)}, u32[]{:S(2)}) collective-permute-start(bf16[2,64,256]{2,1,0:T(8,128)(2,1)S(1)} %get-tuple-element.18), channel_id=1, source_target_pairs={{0,4},{1,5},{2,6},{3,7},{4,0},{5,1},{6,2},{7,3},{8,12},{9,13},{10,... | collective-permute-start | bytes 196616 | tf_op jit(solution)/shard_map/ppermute | solution.py:29
  140.2 5.7 %collective-permute-start.13 = (bf16[2,64,256]{2,1,0:T(8,128)(2,1)S(1)}, bf16[2,64,256]{2,1,0:T(8,128)(2,1)S(1)}, u32[]{:S(2)}, u32[]{:S(2)}) collective-permute-start(bf16[2,64,256]{2,1,0:T(8,128)(2,1)S(1)} %get-tuple-element.18), channel_id=1, source_target_pairs={{0,16},{8,24},{16,0},{24,8},{1,17},{9,25},{17,1},{25,9},{2,18},{10... | collective-permute-start | bytes 196616 | tf_op jit(solution)/shard_map/ppermute | solution.py:29
  145.9 5.0 %collective-permute-start.22 = (bf16[4,64,256]{2,1,0:T(8,128)(2,1)S(1)}, bf16[4,64,256]{2,1,0:T(8,128)(2,1)S(1)}, u32[]{:S(2)}, u32[]{:S(2)}) collective-permute-start(bf16[4,64,256]{2,1,0:T(8,128)(2,1)S(1)} %get-tuple-element.38), channel_id=1, source_target_pairs={{0,2},{1,3},{2,0},{3,1},{4,6},{5,7},{6,4},{7,5},{8,10},{9,11},{10,... | collective-permute-start | bytes 393224 | tf_op jit(solution)/shard_map/ppermute | solution.py:29
  146.0 5.0 %collective-permute-start.14 = (bf16[4,64,256]{2,1,0:T(8,128)(2,1)S(1)}, bf16[4,64,256]{2,1,0:T(8,128)(2,1)S(1)}, u32[]{:S(2)}, u32[]{:S(2)}) collective-permute-start(bf16[4,64,256]{2,1,0:T(8,128)(2,1)S(1)} %get-tuple-element.39), channel_id=1, source_target_pairs={{0,8},{8,0},{16,24},{24,16},{1,9},{9,1},{17,25},{25,17},{2,10},{10... | collective-permute-start | bytes 393224 | tf_op jit(solution)/shard_map/ppermute | solution.py:29
  161.3 6.4 %collective-permute-start.15 = (f32[4,64,256]{2,1,0:T(8,128)S(1)}, f32[4,64,256]{2,1,0:T(8,128)S(1)}, u32[]{:S(2)}, u32[]{:S(2)}) collective-permute-start(f32[4,64,256]{2,1,0:T(8,128)S(1)} %slice.157), channel_id=1, source_target_pairs={{0,2},{1,3},{2,0},{3,1},{4,6},{5,7},{6,4},{7,5},{8,10},{9,11},{10,... | collective-permute-start | bytes 786440 | tf_op jit(solution)/shard_map/ppermute | solution.py:29
  161.4 8.5 %collective-permute-start.23 = (bf16[8,64,256]{2,1,0:T(8,128)(2,1)S(1)}, bf16[8,64,256]{2,1,0:T(8,128)(2,1)S(1)}, u32[]{:S(2)}, u32[]{:S(2)}) collective-permute-start(bf16[8,64,256]{2,1,0:T(8,128)(2,1)S(1)} %get-tuple-element.36), channel_id=1, source_target_pairs={{0,1},{1,0},{2,3},{3,2},{4,5},{5,4},{6,7},{7,6},{8,9},{9,8},{10,11... | collective-permute-start | bytes 786440 | tf_op jit(solution)/shard_map/ppermute | solution.py:29
  167.9 5.6 %collective-permute-start.16 = (f32[2,64,256]{2,1,0:T(8,128)S(1)}, f32[2,64,256]{2,1,0:T(8,128)S(1)}, u32[]{:S(2)}, u32[]{:S(2)}) collective-permute-start(f32[2,64,256]{2,1,0:T(8,128)S(1)} %slice.159), channel_id=1, source_target_pairs={{0,1},{1,0},{2,3},{3,2},{4,5},{5,4},{6,7},{7,6},{8,9},{9,8},{10,11... | collective-permute-start | bytes 393224 | tf_op jit(solution)/shard_map/ppermute | solution.py:29
  167.9 17.4 %collective-permute-start.18 = (f32[4,64,256]{2,1,0:T(8,128)S(1)}, f32[4,64,256]{2,1,0:T(8,128)S(1)}, u32[]{:S(2)}, u32[]{:S(2)}) collective-permute-start(f32[4,64,256]{2,1,0:T(8,128)S(1)} %get-tuple-element.33), channel_id=1, source_target_pairs={{0,1},{1,0},{2,3},{3,2},{4,5},{5,4},{6,7},{7,6},{8,9},{9,8},{10,11... | collective-permute-start | bytes 786440 | tf_op jit(solution)/shard_map/ppermute | solution.py:29
  173.5 11.8 %collective-permute-start.17 = (f32[1,64,256]{2,1,0:T(8,128)S(1)}, f32[1,64,256]{2,1,0:T(8,128)S(1)}, u32[]{:S(2)}, u32[]{:S(2)}) collective-permute-start(f32[1,64,256]{2,1,0:T(8,128)S(1)} %slice.161), channel_id=1, source_target_pairs={{0,4},{1,5},{2,6},{3,7},{4,0},{5,1},{6,2},{7,3},{8,12},{9,13},{10,... | collective-permute-start | bytes 196616 | tf_op jit(solution)/shard_map/ppermute | solution.py:29
  185.2 1.6 collective-permute-start.24
  185.4 6.0 %collective-permute-start.19 = (f32[2,64,256]{2,1,0:T(8,128)S(1)}, f32[2,64,256]{2,1,0:T(8,128)S(1)}, u32[]{:S(2)}, u32[]{:S(2)}) collective-permute-start(f32[2,64,256]{2,1,0:T(8,128)S(1)} %slice.165), channel_id=1, source_target_pairs={{0,2},{1,3},{2,0},{3,1},{4,6},{5,7},{6,4},{7,5},{8,10},{9,11},{10,... | collective-permute-start | bytes 393224 | tf_op jit(solution)/shard_map/ppermute | solution.py:29
  186.9 6.5 %collective-permute-start.25 = (f32[2,64,256]{2,1,0:T(8,128)S(1)}, f32[2,64,256]{2,1,0:T(8,128)S(1)}, u32[]{:S(2)}, u32[]{:S(2)}) collective-permute-start(f32[2,64,256]{2,1,0:T(8,128)S(1)} %slice.171), channel_id=1, source_target_pairs={{0,16},{8,24},{16,0},{24,8},{1,17},{9,25},{17,1},{25,9},{2,18},{10... | collective-permute-start | bytes 393224 | tf_op jit(solution)/shard_map/ppermute | solution.py:29
  191.4 6.0 %collective-permute-start.20 = (f32[1,64,256]{2,1,0:T(8,128)S(1)}, f32[1,64,256]{2,1,0:T(8,128)S(1)}, u32[]{:S(2)}, u32[]{:S(2)}) collective-permute-start(f32[1,64,256]{2,1,0:T(8,128)S(1)} %slice.167), channel_id=1, source_target_pairs={{0,4},{1,5},{2,6},{3,7},{4,0},{5,1},{6,2},{7,3},{8,12},{9,13},{10,... | collective-permute-start | bytes 196616 | tf_op jit(solution)/shard_map/ppermute | solution.py:29
  (31 other events, 487.3 us)

commit v2 on v1

v2 whole, which is shorter than its diff:
```python
import functools

import jax
import jax.numpy as jnp
from jax import lax
from jax.experimental import pallas as pl
from jax.experimental.pallas import tpu as pltpu
from jax.sharding import PartitionSpec as P

F32 = jnp.float32
BF16 = jnp.bfloat16
NN = (((1,), (0,)), ((), ()))
NT = (((1,), (1,)), ((), ()))
VMEM_LIMIT = 44 * 2**20


def exact(left, right, dims):
    return lax.dot_general(
        left, right, dims, precision=lax.Precision.HIGHEST, preferred_element_type=F32
    )


def masks_of(axis):
    return [2**bit for bit in range(lax.axis_size(axis).bit_length() - 1)]


def swap(value, axis, mask):
    pairs = [(source, source ^ mask) for source in range(lax.axis_size(axis))]
    return lax.ppermute(value, axis, pairs)


def place(device, masks):
    spot = jnp.zeros_like(device)
    for mask in masks:
        spot = spot * 2 + (jnp.bitwise_and(device, mask) != 0).astype(jnp.int32)
    return spot


def pieces_shape(rows, columns, devices):
    return (devices, 2 * rows // devices, columns // 2)


def to_pieces(value, pieces_ref):
    pieces, depth, width = pieces_ref.shape
    for piece in range(pieces):
        row, half = piece // 2 * depth, piece % 2 * width
        pieces_ref[piece] = value[row : row + depth, half : half + width]


def from_pieces(pieces_ref):
    pieces = pieces_ref.shape[0]
    halves = [[pieces_ref[p] for p in range(side, pieces, 2)] for side in (0, 1)]
    return jnp.concatenate([jnp.concatenate(half, axis=0) for half in halves], axis=1)


def total_kernel(got_ref, out_ref):
    total = got_ref[0]
    for piece in range(1, got_ref.shape[0]):
        total = total + got_ref[piece]
    for piece in range(got_ref.shape[0]):
        out_ref[piece] = total


def spread_sum(pieces):
    axes = ("row", "col")
    got = lax.all_to_all(pieces, axes, 0, 0, tiled=True)
    (same,) = call(total_kernel, [(pieces.shape, F32)], "total", [], [got])
    return lax.all_to_all(same, axes, 0, 0, tiled=True)


def product_kernel(
    forward,
    chunk,
    group,
    count_ref,
    src_ref,
    dst_ref,
    far_src_ref,
    far_dst_ref,
    v_ref,
    inner_hbm,
    outer_hbm,
    tiles_ref,
    out_ref,
    inner_ref,
    outer_ref,
    held,
    far_arrived,
    arrived,
):
    rhs = v_ref.shape[1]
    depth = held.shape[0]
    count = count_ref[0]
    chunks = lax.div(count + (chunk - 1), chunk)

    def fetch(index):
        slot = lax.rem(index, depth)
        return pltpu.make_async_copy(
            tiles_ref.at[pl.ds(index * chunk, chunk)], held.at[slot], arrived.at[slot]
        )

    far_copies = [
        pltpu.make_async_copy(inner_hbm, inner_ref, far_arrived.at[0]),
        pltpu.make_async_copy(outer_hbm, outer_ref, far_arrived.at[1]),
    ]
    for copy in far_copies:
        copy.start()
    for index in range(depth - 1):

        @pl.when(index < chunks)
        def _():
            fetch(index).start()

    out_ref[...] = jnp.zeros_like(out_ref)
    panels = far_src_ref.shape[0]
    prank = inner_ref.shape[0] // panels
    shape = (group * rhs, group * prank)
    of_row = lax.div(lax.broadcasted_iota(jnp.int32, shape, 0), rhs)
    of_lane = lax.div(lax.broadcasted_iota(jnp.int32, shape, 1), prank)
    same = of_row == of_lane

    for copy in far_copies:
        copy.wait()
    for start in range(0, panels, group):
        v = jnp.concatenate([v_ref[far_src_ref[start + g]] for g in range(group)], axis=0)
        part = pl.ds(start * prank, group * prank)
        half = lax.dot_general(v, inner_ref[part, :], NT, preferred_element_type=F32)
        half = jnp.where(same, half, 0.0).astype(BF16)
        prod = lax.dot_general(half, outer_ref[part, :], NN, preferred_element_type=F32)
        for g in range(group):
            out_ref[far_dst_ref[start + g]] += prod[g * rhs : (g + 1) * rhs]

    def near(index, carry):
        fetch(index).wait()

        @pl.when(index + (depth - 1) < chunks)
        def _():
            fetch(index + (depth - 1)).start()

        slot = lax.rem(index, depth)
        for s in range(chunk):
            tile = index * chunk + s
            v = v_ref[src_ref[tile]]
            v = jnp.where(tile < count, v, jnp.zeros_like(v))
            out_ref[dst_ref[tile]] += lax.dot_general(
                v, held[slot, s], NT if forward else NN, preferred_element_type=F32
            )
        return carry

    lax.fori_loop(0, chunks, near, 0)


def products(forward, v, tiles, count, src, dst, far_src, far_dst, inner, outer, out_blocks):
    slots, width, _ = tiles.shape
    rhs = v.shape[1]
    chunk, depth, group = 32, 3, 8
    smem = pl.BlockSpec(memory_space=pltpu.SMEM)
    vmem = pl.BlockSpec(memory_space=pltpu.VMEM)
    return pl.pallas_call(
        functools.partial(product_kernel, forward, chunk, group),
        out_shape=jax.ShapeDtypeStruct((out_blocks, rhs, width), F32),
        in_specs=[smem] * 5 + [vmem] + [pl.BlockSpec(memory_space=pltpu.HBM)] * 3,
        out_specs=vmem,
        scratch_shapes=[
            pltpu.VMEM(inner.shape, inner.dtype),
            pltpu.VMEM(outer.shape, outer.dtype),
            pltpu.VMEM((depth, chunk, width, width), tiles.dtype),
            pltpu.SemaphoreType.DMA((2,)),
            pltpu.SemaphoreType.DMA((depth,)),
        ],
        compiler_params=pltpu.CompilerParams(vmem_limit_bytes=VMEM_LIMIT),
        cost_estimate=pl.CostEstimate(
            flops=4 * slots * rhs * width * width,
            bytes_accessed=2 * slots * width * width,
            transcendentals=0,
        ),
        name="forward_products" if forward else "transposed_products",
    )(count.reshape(1), src, dst, far_src, far_dst, v, inner, outer, tiles)


def eliminate(systems, block=4):
    size, lanes = systems[0].shape
    parts = [[s[t : t + 8, :] for t in range(0, size, 8)] for s in systems]
    sub = lax.broadcasted_iota(jnp.int32, (8, lanes), 0)
    every = range(block)
    for k in range(0, size, block):
        home, offset = k // 8, k % 8
        for n, part in enumerate(parts):
            cols = [[jnp.broadcast_to(p[:, k + j : k + j + 1], p.shape) for p in part] for j in every]
            head = part[home]
            rows = [jnp.broadcast_to(head[offset + i : offset + i + 1, :], head.shape) for i in every]
            small = [
                [jnp.broadcast_to(cols[j][home][offset + i : offset + i + 1, :], head.shape) for j in every]
                for i in every
            ]
            for p in every:
                inverse = 1.0 / small[p][p]
                rows[p] = rows[p] * inverse
                for j in range(p + 1, block):
                    small[p][j] = small[p][j] * inverse
                for i in every:
                    if i != p:
                        factor = small[i][p]
                        rows[i] = rows[i] - factor * rows[p]
                        for j in range(p + 1, block):
                            small[i][j] = small[i][j] - factor * small[p][j]
            for t in range(len(part)):
                value = part[t]
                for j in every:
                    value = value - cols[j][t] * rows[j]
                part[t] = value
            for i in every:
                part[home] = jnp.where(sub == offset + i, rows[i], part[home])
    return [jnp.concatenate(part, axis=0)[:, size:] for part in parts]


def symmetric(matrix):
    return 0.5 * (matrix + matrix.T)


def call(kernel, outs, name, far, near, after=()):
    def body(*refs):
        refs = refs[len(after) :]
        sources, refs = refs[: len(far)], refs[len(far) :]
        given, refs = refs[: len(near)], refs[len(near) :]
        results, refs = refs[: len(outs)], refs[len(outs) :]
        held = refs[: len(far)]
        copies = [
            pltpu.make_async_copy(source, target, refs[-1].at[index])
            for index, (source, target) in enumerate(zip(sources, held))
        ]
        for copy in copies:
            copy.start()

        def reader(index):
            def read():
                copies[index].wait()
                return held[index][...]

            return read

        kernel(*[reader(index) for index in range(len(far))], *given, *results)

    vmem = pl.BlockSpec(memory_space=pltpu.VMEM)
    return pl.pallas_call(
        body,
        out_shape=[jax.ShapeDtypeStruct(shape, dtype) for shape, dtype in outs],
        in_specs=[pl.BlockSpec(memory_space=pl.ANY)] * len(after)
        + [pl.BlockSpec(memory_space=pltpu.HBM)] * len(far)
        + [vmem] * len(near),
        out_specs=[vmem] * len(outs),
        scratch_shapes=[pltpu.VMEM(value.shape, value.dtype) for value in far]
        + [pltpu.SemaphoreType.DMA((max(len(far), 1),))],
        compiler_params=pltpu.CompilerParams(vmem_limit_bytes=VMEM_LIMIT),
        name=name,
    )(*after, *far, *near)


def pack(direc, packed_ref):
    blocks, _, width = packed_ref.shape
    for b in range(blocks):
        packed_ref[b] = direc[:, b * width : (b + 1) * width].astype(BF16)


def project_kernel(rhs, factor, out_ref):
    to_pieces(exact(rhs(), factor(), NT), out_ref)


def begin_kernel(rhs, weight, factor, proj_ref, direc_ref, packed_ref):
    proj = from_pieces(proj_ref)
    direc = rhs() + exact(proj * weight(), factor(), NN)
    direc_ref[...] = direc
    pack(direc, packed_ref)


def image_of(self_term, direc, terms):
    sums = [own[...] + got[...] for own, got in terms]
    row_terms, col_terms = jnp.concatenate(sums[:-1], axis=0), sums[-1]
    both = row_terms + col_terms
    return self_term * direc + jnp.concatenate([both[b] for b in range(both.shape[0])], axis=1)


def paired(refs):
    return list(zip(refs[::2], refs[1::2]))


def fold_kernel(forward_ref, *refs):
    blocks = len(refs) // 3
    half, width = refs[0].shape[0], refs[0].shape[0] // 2
    for b in range(blocks):
        start = 2 * half * b
        for part in range(2):
            mine = forward_ref[start + part * width : start + (part + 1) * width]
            got = refs[b][part * width : (part + 1) * width]
            refs[blocks + 2 * b + part][...] = mine + got


def inner_kernel(self_term, rhs, factor, direc_ref, *refs):
    terms, (image_ref, out_ref) = paired(refs[:-2]), refs[-2:]
    direc = direc_ref[...]
    image = image_of(self_term(), direc, terms)
    image_ref[...] = image
    resid = rhs()
    count = resid.shape[0]
    stack = jnp.concatenate([direc, resid, image], axis=0)
    against = exact(stack, image, NT)
    own = exact(resid, resid, NT)
    pairs = jnp.concatenate(
        [against[:count], against[count : 2 * count], against[2 * count :], own], axis=1
    )
    to_pieces(jnp.concatenate([exact(image, factor(), NT), pairs], axis=1), out_ref)


def advance_kernel(
    weight_of,
    factor,
    rhs,
    sums_ref,
    proj_ref,
    direc_ref,
    image_ref,
    solution_ref,
    resid_ref,
    next_ref,
    packed_ref,
    rho_ref,
):
    count = rho_ref.shape[0]
    weight, proj, sums = weight_of(), from_pieces(proj_ref), from_pieces(sums_ref)
    rank = proj.shape[1]
    image_proj = sums[:, :rank]
    gram, cross, square, own = (
        sums[:, rank + count * index : rank + count * (index + 1)] for index in range(4)
    )
    rho = own + exact(proj * weight, proj, NT)
    unit = (
        lax.broadcasted_iota(jnp.int32, (count, count), 0)
        == lax.broadcasted_iota(jnp.int32, (count, count), 1)
    ).astype(F32)
    alpha, inverse = eliminate(
        [
            jnp.concatenate([symmetric(gram), rho], axis=1),
            jnp.concatenate([symmetric(rho), unit], axis=1),
        ]
    )
    alpha_t = alpha.T
    proj = proj - exact(alpha_t, image_proj, NN)
    mixed = exact(cross, alpha, NN)
    new = own - mixed - mixed.T + exact(exact(alpha_t, square, NN), alpha, NN)
    new = new + exact(proj * weight, proj, NT)
    beta = exact(inverse, new, NN)
    direc = direc_ref[...]
    resid = rhs() - exact(alpha_t, image_ref[...], NN)
    after = resid + exact(proj * weight, factor(), NN) + exact(beta.T, direc, NN)
    pack(after, packed_ref)
    solution_ref[...] = exact(alpha_t, direc, NN)
    resid_ref[...] = resid
    next_ref[...] = after
    rho_ref[...] = new


def last_image_kernel(self_term, direc_ref, *refs):
    terms, (image_ref, gram_ref) = paired(refs[:-2]), refs[-2:]
    direc = direc_ref[...]
    image = image_of(self_term(), direc, terms)
    image_ref[...] = image
    gram = exact(direc, image, NT)
    to_pieces(jnp.concatenate([gram] + [jnp.zeros_like(gram)] * 3, axis=1), gram_ref)


def finish_kernel(
    gram_ref, rho_ref, solution_ref, resid_ref, direc_ref, image_ref, out_ref, left_ref
):
    count = rho_ref.shape[0]
    gram = from_pieces(gram_ref)[:, :count]
    (alpha,) = eliminate([jnp.concatenate([symmetric(gram), rho_ref[...]], axis=1)])
    alpha_t = alpha.T
    out_ref[...] = solution_ref[...] + exact(alpha_t, direc_ref[...], NN)
    left_ref[...] = resid_ref[...] - exact(alpha_t, image_ref[...], NN)


def local(
    rhs,
    self_term,
    near_tiles,
    near_rows,
    near_cols,
    near_counts,
    far_left,
    far_right,
    far_rows,
    far_cols,
    nys_factor,
    nys_weight,
):
    width = near_tiles.shape[1]
    count_rhs, columns = rhs.shape
    blocks = columns // width
    n_row, n_col = lax.axis_size("row"), lax.axis_size("col")
    grid_row, grid_col = lax.axis_index("row"), lax.axis_index("col")
    count = near_counts[grid_row * n_col + grid_col]
    rank = nys_factor.shape[0]
    self_row = self_term.reshape(1, columns)
    weight = nys_weight.reshape(1, rank)
    prank = far_left.shape[2]
    left = far_left.transpose(0, 2, 1).reshape(-1, width)
    right = far_right.transpose(0, 2, 1).reshape(-1, width)

    col_masks, row_masks = masks_of("col"), masks_of("row")
    gather_col, gather_row = col_masks[::-1], row_masks[::-1]
    path_a = col_masks[-2::-1] + col_masks[-1:]
    path_b = col_masks
    scatter_row = row_masks

    def relative(ids, me):
        return jnp.bitwise_xor(ids // blocks, me), ids % blocks

    def gathered(ids, me, masks):
        device, block = relative(ids, me)
        return place(device, masks[::-1]) * blocks + block

    def scattered_col(ids):
        device, block = relative(ids, grid_col)
        path = jnp.where(block % 2 == 0, place(device, path_a), place(device, path_b))
        return block * n_col + path

    def scattered_row(ids):
        device, block = relative(ids, grid_row)
        return place(device, scatter_row) * blocks + block

    row_src = gathered(near_rows, grid_col, gather_col)
    col_src = gathered(near_cols, grid_row, gather_row)
    far_row_src = gathered(far_rows, grid_col, gather_col)
    far_col_src = gathered(far_cols, grid_row, gather_row)
    row_dst, far_row_dst = scattered_col(near_rows), scattered_col(far_rows)
    col_dst, far_col_dst = scattered_row(near_cols), scattered_row(far_cols)

    def operate(packed):
        col_side = row_side = packed
        for axis_step in range(max(len(gather_col), len(gather_row))):
            if axis_step < len(gather_row):
                got = swap(col_side, "row", gather_row[axis_step])
                col_side = jnp.concatenate([col_side, got], axis=0)
            if axis_step < len(gather_col):
                got = swap(row_side, "col", gather_col[axis_step])
                row_side = jnp.concatenate([row_side, got], axis=0)
        forward = products(
            True, col_side, near_tiles, count, col_src, row_dst,
            far_col_src, far_row_dst, right, left, n_col * blocks,
        )
        transposed = products(
            False, row_side, near_tiles, count, row_src, col_dst,
            far_row_src, far_col_dst, left, right, n_row * blocks,
        )

        def halve(value, axis, mask):
            half = value.shape[0] // 2
            return value[:half], swap(value[half:], axis, mask)

        half = n_col // 2
        sends = [forward[b * n_col + half : (b + 1) * n_col] for b in range(blocks)]
        paths = [path_a if b % 2 == 0 else path_b for b in range(blocks)]
        got = [swap(sends[b], "col", paths[b][0]) for b in range(blocks)]
        quarter = (half // 2, count_rhs, width)
        folded = call(
            fold_kernel, [(quarter, F32)] * (2 * blocks), "fold", [], [forward, *got], [transposed]
        )
        pairs = [
            (folded[2 * b], swap(folded[2 * b + 1], "col", paths[b][1])) for b in range(blocks)
        ]
        for step in range(2, len(col_masks)):
            parts = [own + other for own, other in pairs]
            pairs = [halve(parts[b], "col", paths[b][step]) for b in range(blocks)]
        for mask in scatter_row:
            last = halve(transposed, "row", mask)
            transposed = last[0] + last[1]
        return [term for pair in pairs + [last] for term in pair]

    devices = n_row * n_col
    full, packs = (count_rhs, columns), (blocks, count_rhs, width)
    shape_of = lambda wanted: pieces_shape(count_rhs, wanted, devices)
    (partial,) = call(
        project_kernel, [(shape_of(rank), F32)], "project", [rhs, nys_factor], []
    )
    proj = spread_sum(partial)
    direc, packed = call(
        begin_kernel, [(full, F32), (packs, BF16)], "begin", [rhs, weight, nys_factor], [proj]
    )
    terms = operate(packed)
    image, partial = call(
        inner_kernel, [(full, F32), (shape_of(rank + 4 * count_rhs), F32)], "inner",
        [self_row, rhs, nys_factor], [direc, *terms],
    )
    sums = spread_sum(partial)
    solution, residual, direc, packed, rho = call(
        advance_kernel,
        [(full, F32), (full, F32), (full, F32), (packs, BF16), ((count_rhs, count_rhs), F32)],
        "advance", [weight, nys_factor, rhs], [sums, proj, direc, image],
    )
    terms = operate(packed)
    image, partial = call(
        last_image_kernel, [(full, F32), (shape_of(4 * count_rhs), F32)], "last_image",
        [self_row], [direc, *terms],
    )
    gram = spread_sum(partial)
    return tuple(
        call(
            finish_kernel, [(full, F32), (full, F32)], "finish",
            [], [gram, rho, solution, residual, direc, image],
        )
    )


def solution(mesh):
    in_specs = (
        P(None, ("row", "col")),
        P(("row", "col")),
        P(("row", "col"), None, None),
        P(("row", "col")),
        P(("row", "col")),
        P(),
        P(("row", "col"), None, None),
        P(("row", "col"), None, None),
        P(("row", "col")),
        P(("row", "col")),
        P(None, ("row", "col")),
        P(),
    )
    out_specs = (P(None, ("row", "col")), P(None, ("row", "col")))
    return jax.shard_map(local, mesh=mesh, in_specs=in_specs, out_specs=out_specs, check_vma=False)
```

time: 227 us -> 185 us (0.81)
  waiting for transfers between devices: 70.3 us -> 51.9 us
  local copies, waits for them, and re-layouts: 23 us -> 8.95 us
  Pallas kernels: 52.9 us -> 42.3 us
  starting transfers between devices: 27.1 us -> 33.7 us
    ppermute x26, waiting for transfers between devices: 56.3 us -> 37.8 us  [swap(): return lax.ppermute(value, axis, pairs)]
    unnamed x70 -> x26, local copies, waits for them, and re-layouts: 17.5 us -> 7.51 us
    pallas_call x4, Pallas kernels: 33.6 us -> 24.5 us  [products(): pl.pallas_call(functools.partial(product_kernel, forward, chunk, group),...]
    ppermute x26, starting transfers between devices: 17.2 us -> 23.8 us  [swap(): return lax.ppermute(value, axis, pairs)]
    reshape x2 -> x0, local copies, waits for them, and re-layouts: 3.31 us -> none  [the longest x1 1.67 us: spread_sum(): full.reshape(rows // 8, columns // 128, 8, 128).transpose(0, 2, 1, 3)]
    add x4 -> x2, other arithmetic: 2.7 us -> 0.01 us  [gathered(): return place(device, masks[::-1]) * blocks + block]
    pallas_call x6 -> x11, Pallas kernels: 19.2 us -> 17.8 us  [call(): pl.pallas_call(body, out_shape=[jax.ShapeDtypeStruct(shape, dtype) for sh...]
  transfers between devices with their start and end apart: 28 -> 28, of which waited for: 16 -> 20; matrix products, arithmetic and copies ran while one was open for 2% -> 2% of each run, Pallas kernels for 7% -> 13%
where the time goes in v2:
time: 185 us; the launch traced here: 186 us
  waiting for transfers between devices  51.9 us (28%)
  blocking collectives  44.5 us (24%)
  Pallas kernels  42.3 us (23%)
  starting transfers between devices  33.7 us (18%)
  local copies, waits for them, and re-layouts  8.95 us (5%)
  other arithmetic  3.11 us (2%)
    ppermute x26, waiting for transfers between devices, swap(): return lax.ppermute(value, axis, pairs)  37.8 us
    pallas_call x4, Pallas kernels, products(): pl.pallas_call(functools.partial(product_kernel, forward, chunk, group),...  24.5 us
    all_to_all x2, blocking collectives, spread_sum(): got = lax.all_to_all(pieces, axes, 0, 0, tiled=True)  24.1 us
    ppermute x26, starting transfers between devices, swap(): return lax.ppermute(value, axis, pairs)  23.8 us
    all_to_all x2, blocking collectives, spread_sum(): return lax.all_to_all(same, axes, 0, 0, tiled=True)  20.4 us
    pallas_call x11, Pallas kernels, call(): pl.pallas_call(body, out_shape=[jax.ShapeDtypeStruct(shape, dtype) for sh...  17.8 us
    all_to_all x1, waiting for transfers between devices, spread_sum(): return lax.all_to_all(same, axes, 0, 0, tiled=True)  7.71 us
    unnamed x26, local copies, waits for them, and re-layouts  7.51 us
  transfers between devices with their start and end apart: 28, of which 20 were waited for; matrix products, arithmetic and copies ran while one was open for 2% of the time, Pallas kernels for 13%

profile of v2, /device:TPU:0, one launch (start us, length us, event | category | flops | bytes accessed | tf_op | source)
XLA Modules:
  0.0 185.7 jit_solution(910544649951841650)
XLA Ops:
  2.9 2.0 %project.1 = f32[32,4,256]{2,1,0:T(4,128)} custom-call(f32[64,512]{1,0:T(8,128)S(1)} %copy-done.7, f32[512,512]{1,0:T(8,128)S(1)} %copy-done.4), custom_call_target="tpu_custom_call" | custom-call | tf_op jit(solution)/shard_map/project/pallas_call | solution.py:245
  4.9 7.3 %all-to-all-start = ((f32[32,4,256]{2,1,0:T(4,128)}), f32[32,4,256]{2,1,0:T(4,128)S(1)}, u32[]{:S(2)}, u32[]{:S(2)}) async-start(f32[32,4,256]{2,1,0:T(4,128)} %project.1), calls=%async_computation | async-start | bytes 262144 | tf_op jit(solution)/shard_map/all_to_all | solution.py:66
  13.5 6.4 %all-to-all-done.refs_0_ = f32[32,4,256]{2,1,0:T(4,128)S(1)} async-done(((f32[32,4,256]{2,1,0:T(4,128)}), f32[32,4,256]{2,1,0:T(4,128)S(1)}, u32[]{:S(2)}, u32[]{:S(2)}) %all-to-all-start) | async-done | bytes 131104 | tf_op jit(solution)/shard_map/all_to_all | solution.py:66
  20.6 2.6 %all-to-all-start.1 = ((f32[32,4,256]{2,1,0:T(4,128)}), f32[32,4,256]{2,1,0:T(4,128)S(1)}, u32[]{:S(2)}, u32[]{:S(2)}) async-start(f32[32,4,256]{2,1,0:T(4,128)} %total.3), calls=%async_computation.1 | async-start | bytes 262144 | tf_op jit(solution)/shard_map/all_to_all | solution.py:68
  23.2 7.7 %all-to-all-done.1.refs_3_.refs_4_ = f32[32,4,256]{2,1,0:T(4,128)S(1)} async-done(((f32[32,4,256]{2,1,0:T(4,128)}), f32[32,4,256]{2,1,0:T(4,128)S(1)}, u32[]{:S(2)}, u32[]{:S(2)}) %all-to-all-start.1) | async-done | bytes 131104 | tf_op jit(solution)/shard_map/all_to_all | solution.py:68
  39.1 2.6 %collective-permute-done = bf16[2,64,256]{2,1,0:T(8,128)(2,1)S(1)} collective-permute-done((bf16[2,64,256]{2,1,0:T(8,128)(2,1)S(1)}, bf16[2,64,256]{2,1,0:T(8,128)(2,1)S(1)}, u32[]{:S(2)}, u32[]{:S(2)}) %collective-permute-start) | collective-permute-done | bytes 65568 | tf_op jit(solution)/shard_map/ppermute | solution.py:29
  43.1 4.6 %collective-permute-done.1 = bf16[4,64,256]{2,1,0:T(8,128)(2,1)S(1)} collective-permute-done((bf16[4,64,256]{2,1,0:T(8,128)(2,1)S(1)}, bf16[4,64,256]{2,1,0:T(8,128)(2,1)S(1)}, u32[]{:S(2)}, u32[]{:S(2)}) %collective-permute-start.1) | collective-permute-done | bytes 131104 | tf_op jit(solution)/shard_map/ppermute | solution.py:29
  51.3 6.4 %forward_products.2.refs_1_ = f32[16,64,256]{2,1,0:T(8,128)S(1)} custom-call(s32[1]{0:T(128)} %dynamic_slice.3.count_ref, s32[128]{0:T(128)S(1)} %fusion.4.dst_ref.src_ref, s32[128]{0:T(128)S(1)} %get-tuple-element.42.dst_ref, s32[64]{0:T(128)S(1)} %fusion.5.far_dst_ref.far_src_ref, s32[64]{0:T(128)S(1)} %get-tuple-element.40.far_dst_ref, ...), custom_call_target="tpu_custom_call" | custom-call | flops 2147483648 | bytes 16777216 | tf_op jit(solution)/shard_map/forward_products/pallas_call | solution.py:159
  58.3 5.9 %transposed_products.2.refs_0_ = f32[8,64,256]{2,1,0:T(8,128)S(1)} custom-call(s32[1]{0:T(128)} %dynamic_slice.3.count_ref, s32[128]{0:T(128)S(1)} %multiply_add_fusion.4.src_ref, s32[128]{0:T(128)S(1)} %fusion.4.dst_ref.src_ref, s32[64]{0:T(128)S(1)} %multiply_add_fusion.2.far_src_ref, s32[64]{0:T(128)S(1)} %fusion.5.far_dst_ref.far_src_ref, ...), custom_call_target="tpu_custom_call" | custom-call | flops 2147483648 | bytes 16777216 | tf_op jit(solution)/shard_map/transposed_products/pallas_call | solution.py:159
  64.3 1.4 collective-permute-done.6.refs_3_
  67.3 3.5 %collective-permute-done.7 = f32[2,64,256]{2,1,0:T(8,128)S(1)} collective-permute-done((f32[2,64,256]{2,1,0:T(8,128)S(1)}, f32[2,64,256]{2,1,0:T(8,128)S(1)}, u32[]{:S(2)}, u32[]{:S(2)}) %collective-permute-start.7) | collective-permute-done | bytes 131104 | tf_op jit(solution)/shard_map/ppermute | solution.py:29
  70.8 5.2 %collective-permute-start.8 = (f32[1,64,256]{2,1,0:T(8,128)S(1)}, f32[1,64,256]{2,1,0:T(8,128)S(1)}, u32[]{:S(2)}, u32[]{:S(2)}) collective-permute-start(f32[1,64,256]{2,1,0:T(8,128)S(1)} %get-tuple-element.62), channel_id=1, source_target_pairs={{0,4},{1,5},{2,6},{3,7},{4,0},{5,1},{6,2},{7,3},{8,12},{9,13},{10,... | collective-permute-start | bytes 196616 | tf_op jit(solution)/shard_map/ppermute | solution.py:29
  77.4 2.7 %collective-permute-done.8.refs_5_ = f32[1,64,256]{2,1,0:T(8,128)S(1)} collective-permute-done((f32[1,64,256]{2,1,0:T(8,128)S(1)}, f32[1,64,256]{2,1,0:T(8,128)S(1)}, u32[]{:S(2)}, u32[]{:S(2)}) %collective-permute-start.8) | collective-permute-done | bytes 65568 | tf_op jit(solution)/shard_map/ppermute | solution.py:29
  80.1 1.8 collective-permute-done.10.refs_7_
  81.9 2.3 %inner.1 = (f32[64,512]{1,0:T(8,128)S(1)}, f32[32,4,384]{2,1,0:T(4,128)S(1)}) custom-call(f32[1,512]{1,0:T(1,128)S(1)} %bitcast.18, f32[64,512]{1,0:T(8,128)S(1)} %copy-done.9, f32[512,512]{1,0:T(8,128)S(1)} %copy-done.6, f32[64,512]{1,0:T(8,128)S(1)} %get-tuple-element.21.refs_3_.refs_5_, f32[1,64,256]{2,1,0:T(8,128)S(1)} %get-tuple-element.63.refs_4_, ...), custom_call_target="tpu_custom_call" | custom-call | tf_op jit(solution)/shard_map/inner/pallas_call | solution.py:245
  84.2 12.6 %all_to_all.30.refs_0_ = f32[32,4,384]{2,1,0:T(4,128)S(1)} all-to-all(f32[32,4,384]{2,1,0:T(4,128)S(1)} %get-tuple-element.27), channel_id=1, replica_groups=mesh['row'=4,'col'=8] {'row','col'}, dimensions={0} | all-to-all | bytes 393216 | tf_op jit(solution)/shard_map/all_to_all | solution.py:66
  96.9 11.4 %all_to_all.31.refs_3_ = f32[32,4,384]{2,1,0:T(4,128)S(1)} all-to-all(f32[32,4,384]{2,1,0:T(4,128)S(1)} %total.4), channel_id=1, replica_groups=mesh['row'=4,'col'=8] {'row','col'}, dimensions={0} | all-to-all | bytes 393216 | tf_op jit(solution)/shard_map/all_to_all | solution.py:68
  108.3 6.7 %advance.1 = (f32[64,512]{1,0:T(8,128)S(1)}, f32[64,512]{1,0:T(8,128)S(1)}, f32[64,512]{1,0:T(8,128)S(1)}, bf16[2,64,256]{2,1,0:T(8,128)(2,1)S(1)}, f32[64,64]{1,0:T(8,128)S(1)}) custom-call(f32[1,512]{1,0:T(1,128)S(1)} %bitcast.17, f32[512,512]{1,0:T(8,128)S(1)} %copy-done.6, f32[64,512]{1,0:T(8,128)S(1)} %copy-done.9, ...), custom_call_target="tpu_custom_call" | custom-call | tf_op jit(solution)/shard_map/advance/pallas_call | solution.py:245
  117.2 2.2 %collective-permute-done.16 = bf16[2,64,256]{2,1,0:T(8,128)(2,1)S(1)} collective-permute-done((bf16[2,64,256]{2,1,0:T(8,128)(2,1)S(1)}, bf16[2,64,256]{2,1,0:T(8,128)(2,1)S(1)}, u32[]{:S(2)}, u32[]{:S(2)}) %collective-permute-start.16) | collective-permute-done | bytes 65568 | tf_op jit(solution)/shard_map/ppermute | solution.py:29
  119.4 3.4 %collective-permute-done.13 = bf16[2,64,256]{2,1,0:T(8,128)(2,1)S(1)} collective-permute-done((bf16[2,64,256]{2,1,0:T(8,128)(2,1)S(1)}, bf16[2,64,256]{2,1,0:T(8,128)(2,1)S(1)}, u32[]{:S(2)}, u32[]{:S(2)}) %collective-permute-start.13) | collective-permute-done | bytes 65568 | tf_op jit(solution)/shard_map/ppermute | solution.py:29
  124.2 4.6 %collective-permute-done.14 = bf16[4,64,256]{2,1,0:T(8,128)(2,1)S(1)} collective-permute-done((bf16[4,64,256]{2,1,0:T(8,128)(2,1)S(1)}, bf16[4,64,256]{2,1,0:T(8,128)(2,1)S(1)}, u32[]{:S(2)}, u32[]{:S(2)}) %collective-permute-start.14) | collective-permute-done | bytes 131104 | tf_op jit(solution)/shard_map/ppermute | solution.py:29
  129.4 6.4 %forward_products.3.refs_1_ = f32[16,64,256]{2,1,0:T(8,128)S(1)} custom-call(s32[1]{0:T(128)} %dynamic_slice.3.count_ref, s32[128]{0:T(128)S(1)} %fusion.4.dst_ref.src_ref, s32[128]{0:T(128)S(1)} %get-tuple-element.42.dst_ref, s32[64]{0:T(128)S(1)} %fusion.5.far_dst_ref.far_src_ref, s32[64]{0:T(128)S(1)} %get-tuple-element.40.far_dst_ref, ...), custom_call_target="tpu_custom_call" | custom-call | flops 2147483648 | bytes 16777216 | tf_op jit(solution)/shard_map/forward_products/pallas_call | solution.py:159
  136.8 5.7 %transposed_products.3.refs_0_ = f32[8,64,256]{2,1,0:T(8,128)S(1)} custom-call(s32[1]{0:T(128)} %dynamic_slice.3.count_ref, s32[128]{0:T(128)S(1)} %multiply_add_fusion.4.src_ref, s32[128]{0:T(128)S(1)} %fusion.4.dst_ref.src_ref, s32[64]{0:T(128)S(1)} %multiply_add_fusion.2.far_src_ref, s32[64]{0:T(128)S(1)} %fusion.5.far_dst_ref.far_src_ref, ...), custom_call_target="tpu_custom_call" | custom-call | flops 2147483648 | bytes 16777216 | tf_op jit(solution)/shard_map/transposed_products/pallas_call | solution.py:159
  143.8 1.5 collective-permute-start.20
  145.9 3.0 %collective-permute-done.20 = f32[2,64,256]{2,1,0:T(8,128)S(1)} collective-permute-done((f32[2,64,256]{2,1,0:T(8,128)S(1)}, f32[2,64,256]{2,1,0:T(8,128)S(1)}, u32[]{:S(2)}, u32[]{:S(2)}) %collective-permute-start.20) | collective-permute-done | bytes 131104 | tf_op jit(solution)/shard_map/ppermute | solution.py:29
  148.9 5.4 %collective-permute-start.21 = (f32[1,64,256]{2,1,0:T(8,128)S(1)}, f32[1,64,256]{2,1,0:T(8,128)S(1)}, u32[]{:S(2)}, u32[]{:S(2)}) collective-permute-start(f32[1,64,256]{2,1,0:T(8,128)S(1)} %get-tuple-element.58), channel_id=1, source_target_pairs={{0,4},{1,5},{2,6},{3,7},{4,0},{5,1},{6,2},{7,3},{8,12},{9,13},{10,... | collective-permute-start | bytes 196616 | tf_op jit(solution)/shard_map/ppermute | solution.py:29
  154.6 1.5 collective-permute-start.23
  156.0 2.2 %collective-permute-done.21.refs_3_ = f32[1,64,256]{2,1,0:T(8,128)S(1)} collective-permute-done((f32[1,64,256]{2,1,0:T(8,128)S(1)}, f32[1,64,256]{2,1,0:T(8,128)S(1)}, u32[]{:S(2)}, u32[]{:S(2)}) %collective-permute-start.21) | collective-permute-done | bytes 65568 | tf_op jit(solution)/shard_map/ppermute | solution.py:29
  158.3 1.8 collective-permute-done.23.refs_5_
  160.4 11.5 %all_to_all.32.refs_0_ = f32[32,4,128]{2,1,0:T(4,128)S(1)} all-to-all(f32[32,4,128]{2,1,0:T(4,128)S(1)} %get-tuple-element.35), channel_id=1, replica_groups=mesh['row'=4,'col'=8] {'row','col'}, dimensions={0} | all-to-all | bytes 131072 | tf_op jit(solution)/shard_map/all_to_all | solution.py:66
  171.9 9.0 %all_to_all.33.refs_0_ = f32[32,4,128]{2,1,0:T(4,128)S(1)} all-to-all(f32[32,4,128]{2,1,0:T(4,128)S(1)} %total.5), channel_id=1, replica_groups=mesh['row'=4,'col'=8] {'row','col'}, dimensions={0} | all-to-all | bytes 131072 | tf_op jit(solution)/shard_map/all_to_all | solution.py:68
  180.9 4.6 %finish.1 = (f32[64,512]{1,0:T(8,128)}, f32[64,512]{1,0:T(8,128)}) custom-call(f32[32,4,128]{2,1,0:T(4,128)S(1)} %all_to_all.33.refs_0_, f32[64,64]{1,0:T(8,128)S(1)} %get-tuple-element.36.refs_1_, f32[64,512]{1,0:T(8,128)S(1)} %get-tuple-element.37.refs_2_, f32[64,512]{1,0:T(8,128)S(1)} %get-tuple-element.38.refs_3_, ...), custom_call_target="tpu_custom_call" | custom-call | tf_op jit(solution)/shard_map/finish/pallas_call | solution.py:245
  (100 shorter events, 28.5 us)
Async XLA Ops:
  0.6 57.6 %copy-start.1 = (bf16[64,256,32]{1,2,0:T(8,128)(2,1)S(1)}, bf16[64,256,32]{1,2,0:T(8,128)(2,1)}, u32[]{:S(2)}) copy-start(bf16[64,256,32]{1,2,0:T(8,128)(2,1)} %param.18) | copy-start | bytes 3145732
  4.9 15.1 %all-to-all-start = ((f32[32,4,256]{2,1,0:T(4,128)}), f32[32,4,256]{2,1,0:T(4,128)S(1)}, u32[]{:S(2)}, u32[]{:S(2)}) async-start(f32[32,4,256]{2,1,0:T(4,128)} %project.1), calls=%async_computation | async-start | bytes 262144 | tf_op jit(solution)/shard_map/all_to_all | solution.py:66
  20.6 10.3 %all-to-all-start.1 = ((f32[32,4,256]{2,1,0:T(4,128)}), f32[32,4,256]{2,1,0:T(4,128)S(1)}, u32[]{:S(2)}, u32[]{:S(2)}) async-start(f32[32,4,256]{2,1,0:T(4,128)} %total.3), calls=%async_computation.1 | async-start | bytes 262144 | tf_op jit(solution)/shard_map/all_to_all | solution.py:68
  34.8 4.3 %collective-permute-start.3 = (bf16[2,64,256]{2,1,0:T(8,128)(2,1)S(1)}, bf16[2,64,256]{2,1,0:T(8,128)(2,1)S(1)}, u32[]{:S(2)}, u32[]{:S(2)}) collective-permute-start(bf16[2,64,256]{2,1,0:T(8,128)(2,1)S(1)} %get-tuple-element.22), channel_id=1, source_target_pairs={{0,16},{8,24},{16,0},{24,8},{1,17},{9,25},{17,1},{25,9},{2,18},{10... | collective-permute-start | bytes 196616 | tf_op jit(solution)/shard_map/ppermute | solution.py:29
  35.9 5.8 %collective-permute-start = (bf16[2,64,256]{2,1,0:T(8,128)(2,1)S(1)}, bf16[2,64,256]{2,1,0:T(8,128)(2,1)S(1)}, u32[]{:S(2)}, u32[]{:S(2)}) collective-permute-start(bf16[2,64,256]{2,1,0:T(8,128)(2,1)S(1)} %get-tuple-element.22), channel_id=1, source_target_pairs={{0,4},{1,5},{2,6},{3,7},{4,0},{5,1},{6,2},{7,3},{8,12},{9,13},{10,... | collective-permute-start | bytes 196616 | tf_op jit(solution)/shard_map/ppermute | solution.py:29
  41.7 1.4 collective-permute-start.4
  41.8 5.9 %collective-permute-start.1 = (bf16[4,64,256]{2,1,0:T(8,128)(2,1)S(1)}, bf16[4,64,256]{2,1,0:T(8,128)(2,1)S(1)}, u32[]{:S(2)}, u32[]{:S(2)}) collective-permute-start(bf16[4,64,256]{2,1,0:T(8,128)(2,1)S(1)} %get-tuple-element.71), channel_id=1, source_target_pairs={{0,2},{1,3},{2,0},{3,1},{4,6},{5,7},{6,4},{7,5},{8,10},{9,11},{10,... | collective-permute-start | bytes 393224 | tf_op jit(solution)/shard_map/ppermute | solution.py:29
  47.7 10.5 %collective-permute-start.2 = (bf16[8,64,256]{2,1,0:T(8,128)(2,1)S(1)}, bf16[8,64,256]{2,1,0:T(8,128)(2,1)S(1)}, u32[]{:S(2)}, u32[]{:S(2)}) collective-permute-start(bf16[8,64,256]{2,1,0:T(8,128)(2,1)S(1)} %get-tuple-element.69), channel_id=1, source_target_pairs={{0,1},{1,0},{2,3},{3,2},{4,5},{5,4},{6,7},{7,6},{8,9},{9,8},{10,11... | collective-permute-start | bytes 786440 | tf_op jit(solution)/shard_map/ppermute | solution.py:29
  57.7 24.2 %copy-start.6 = (f32[512,512]{1,0:T(8,128)S(1)}, f32[512,512]{1,0:T(8,128)}, u32[]{:S(2)}) copy-start(f32[512,512]{1,0:T(8,128)} %refs_1_.5) | copy-start | bytes 3145732
  57.8 50.5 %copy-start.11 = (f32[512]{0:T(512)S(1)}, f32[512]{0:T(512)}, u32[]{:S(2)}) copy-start(f32[512]{0:T(512)} %param.23) | copy-start | bytes 6148
  57.8 71.7 %copy-start.3 = (bf16[64,256,32]{1,2,0:T(8,128)(2,1)S(1)}, bf16[64,256,32]{1,2,0:T(8,128)(2,1)}, u32[]{:S(2)}) copy-start(bf16[64,256,32]{1,2,0:T(8,128)(2,1)} %param.19) | copy-start | bytes 3145732
  57.8 6.4 %collective-permute-start.5 = (f32[4,64,256]{2,1,0:T(8,128)S(1)}, f32[4,64,256]{2,1,0:T(8,128)S(1)}, u32[]{:S(2)}, u32[]{:S(2)}) collective-permute-start(f32[4,64,256]{2,1,0:T(8,128)S(1)} %get-tuple-element.51), channel_id=1, source_target_pairs={{0,2},{1,3},{2,0},{3,1},{4,6},{5,7},{6,4},{7,5},{8,10},{9,11},{10,... | collective-permute-start | bytes 786440 | tf_op jit(solution)/shard_map/ppermute | solution.py:29
  58.2 7.5 %collective-permute-start.6 = (f32[4,64,256]{2,1,0:T(8,128)S(1)}, f32[4,64,256]{2,1,0:T(8,128)S(1)}, u32[]{:S(2)}, u32[]{:S(2)}) collective-permute-start(f32[4,64,256]{2,1,0:T(8,128)S(1)} %get-tuple-element.50), channel_id=1, source_target_pairs={{0,1},{1,0},{2,3},{3,2},{4,5},{5,4},{6,7},{7,6},{8,9},{9,8},{10,11... | collective-permute-start | bytes 786440 | tf_op jit(solution)/shard_map/ppermute | solution.py:29
  65.8 5.0 %collective-permute-start.7 = (f32[2,64,256]{2,1,0:T(8,128)S(1)}, f32[2,64,256]{2,1,0:T(8,128)S(1)}, u32[]{:S(2)}, u32[]{:S(2)}) collective-permute-start(f32[2,64,256]{2,1,0:T(8,128)S(1)} %get-tuple-element.24), channel_id=1, source_target_pairs={{0,1},{1,0},{2,3},{3,2},{4,5},{5,4},{6,7},{7,6},{8,9},{9,8},{10,11... | collective-permute-start | bytes 393224 | tf_op jit(solution)/shard_map/ppermute | solution.py:29
  66.8 9.3 %collective-permute-start.11 = (f32[4,64,256]{2,1,0:T(8,128)S(1)}, f32[4,64,256]{2,1,0:T(8,128)S(1)}, u32[]{:S(2)}, u32[]{:S(2)}) collective-permute-start(f32[4,64,256]{2,1,0:T(8,128)S(1)} %slice.87), channel_id=1, source_target_pairs={{0,8},{8,0},{16,24},{24,16},{1,9},{9,1},{17,25},{25,17},{2,10},{10... | collective-permute-start | bytes 786440 | tf_op jit(solution)/shard_map/ppermute | solution.py:29
  66.9 9.2 %collective-permute-start.9 = (f32[2,64,256]{2,1,0:T(8,128)S(1)}, f32[2,64,256]{2,1,0:T(8,128)S(1)}, u32[]{:S(2)}, u32[]{:S(2)}) collective-permute-start(f32[2,64,256]{2,1,0:T(8,128)S(1)} %get-tuple-element.26), channel_id=1, source_target_pairs={{0,2},{1,3},{2,0},{3,1},{4,6},{5,7},{6,4},{7,5},{8,10},{9,11},{10,... | collective-permute-start | bytes 393224 | tf_op jit(solution)/shard_map/ppermute | solution.py:29
  70.8 9.2 %collective-permute-start.8 = (f32[1,64,256]{2,1,0:T(8,128)S(1)}, f32[1,64,256]{2,1,0:T(8,128)S(1)}, u32[]{:S(2)}, u32[]{:S(2)}) collective-permute-start(f32[1,64,256]{2,1,0:T(8,128)S(1)} %get-tuple-element.62), channel_id=1, source_target_pairs={{0,4},{1,5},{2,6},{3,7},{4,0},{5,1},{6,2},{7,3},{8,12},{9,13},{10,... | collective-permute-start | bytes 196616 | tf_op jit(solution)/shard_map/ppermute | solution.py:29
  76.2 5.7 %collective-permute-start.12 = (f32[2,64,256]{2,1,0:T(8,128)S(1)}, f32[2,64,256]{2,1,0:T(8,128)S(1)}, u32[]{:S(2)}, u32[]{:S(2)}) collective-permute-start(f32[2,64,256]{2,1,0:T(8,128)S(1)} %get-tuple-element.54), channel_id=1, source_target_pairs={{0,16},{8,24},{16,0},{24,8},{1,17},{9,25},{17,1},{25,9},{2,18},{10... | collective-permute-start | bytes 393224 | tf_op jit(solution)/shard_map/ppermute | solution.py:29
  76.3 5.6 %collective-permute-start.10 = (f32[1,64,256]{2,1,0:T(8,128)S(1)}, f32[1,64,256]{2,1,0:T(8,128)S(1)}, u32[]{:S(2)}, u32[]{:S(2)}) collective-permute-start(f32[1,64,256]{2,1,0:T(8,128)S(1)} %get-tuple-element.60), channel_id=1, source_target_pairs={{0,4},{1,5},{2,6},{3,7},{4,0},{5,1},{6,2},{7,3},{8,12},{9,13},{10,... | collective-permute-start | bytes 196616 | tf_op jit(solution)/shard_map/ppermute | solution.py:29
  115.0 4.3 %collective-permute-start.16 = (bf16[2,64,256]{2,1,0:T(8,128)(2,1)S(1)}, bf16[2,64,256]{2,1,0:T(8,128)(2,1)S(1)}, u32[]{:S(2)}, u32[]{:S(2)}) collective-permute-start(bf16[2,64,256]{2,1,0:T(8,128)(2,1)S(1)} %get-tuple-element.30), channel_id=1, source_target_pairs={{0,16},{8,24},{16,0},{24,8},{1,17},{9,25},{17,1},{25,9},{2,18},{10... | collective-permute-start | bytes 196616 | tf_op jit(solution)/shard_map/ppermute | solution.py:29
  116.0 6.8 %collective-permute-start.13 = (bf16[2,64,256]{2,1,0:T(8,128)(2,1)S(1)}, bf16[2,64,256]{2,1,0:T(8,128)(2,1)S(1)}, u32[]{:S(2)}, u32[]{:S(2)}) collective-permute-start(bf16[2,64,256]{2,1,0:T(8,128)(2,1)S(1)} %get-tuple-element.30), channel_id=1, source_target_pairs={{0,4},{1,5},{2,6},{3,7},{4,0},{5,1},{6,2},{7,3},{8,12},{9,13},{10,... | collective-permute-start | bytes 196616 | tf_op jit(solution)/shard_map/ppermute | solution.py:29
  122.8 1.4 collective-permute-start.17
  122.9 5.9 %collective-permute-start.14 = (bf16[4,64,256]{2,1,0:T(8,128)(2,1)S(1)}, bf16[4,64,256]{2,1,0:T(8,128)(2,1)S(1)}, u32[]{:S(2)}, u32[]{:S(2)}) collective-permute-start(bf16[4,64,256]{2,1,0:T(8,128)(2,1)S(1)} %get-tuple-element.67), channel_id=1, source_target_pairs={{0,2},{1,3},{2,0},{3,1},{4,6},{5,7},{6,4},{7,5},{8,10},{9,11},{10,... | collective-permute-start | bytes 393224 | tf_op jit(solution)/shard_map/ppermute | solution.py:29
  128.8 7.9 %collective-permute-start.15 = (bf16[8,64,256]{2,1,0:T(8,128)(2,1)S(1)}, bf16[8,64,256]{2,1,0:T(8,128)(2,1)S(1)}, u32[]{:S(2)}, u32[]{:S(2)}) collective-permute-start(bf16[8,64,256]{2,1,0:T(8,128)(2,1)S(1)} %get-tuple-element.65), channel_id=1, source_target_pairs={{0,1},{1,0},{2,3},{3,2},{4,5},{5,4},{6,7},{7,6},{8,9},{9,8},{10,11... | collective-permute-start | bytes 786440 | tf_op jit(solution)/shard_map/ppermute | solution.py:29
  135.9 6.7 %collective-permute-start.18 = (f32[4,64,256]{2,1,0:T(8,128)S(1)}, f32[4,64,256]{2,1,0:T(8,128)S(1)}, u32[]{:S(2)}, u32[]{:S(2)}) collective-permute-start(f32[4,64,256]{2,1,0:T(8,128)S(1)} %get-tuple-element.49), channel_id=1, source_target_pairs={{0,2},{1,3},{2,0},{3,1},{4,6},{5,7},{6,4},{7,5},{8,10},{9,11},{10,... | collective-permute-start | bytes 786440 | tf_op jit(solution)/shard_map/ppermute | solution.py:29
  136.3 7.5 %collective-permute-start.19 = (f32[4,64,256]{2,1,0:T(8,128)S(1)}, f32[4,64,256]{2,1,0:T(8,128)S(1)}, u32[]{:S(2)}, u32[]{:S(2)}) collective-permute-start(f32[4,64,256]{2,1,0:T(8,128)S(1)} %get-tuple-element.48), channel_id=1, source_target_pairs={{0,1},{1,0},{2,3},{3,2},{4,5},{5,4},{6,7},{7,6},{8,9},{9,8},{10,11... | collective-permute-start | bytes 786440 | tf_op jit(solution)/shard_map/ppermute | solution.py:29
  143.8 5.1 %collective-permute-start.20 = (f32[2,64,256]{2,1,0:T(8,128)S(1)}, f32[2,64,256]{2,1,0:T(8,128)S(1)}, u32[]{:S(2)}, u32[]{:S(2)}) collective-permute-start(f32[2,64,256]{2,1,0:T(8,128)S(1)} %get-tuple-element.32), channel_id=1, source_target_pairs={{0,1},{1,0},{2,3},{3,2},{4,5},{5,4},{6,7},{7,6},{8,9},{9,8},{10,11... | collective-permute-start | bytes 393224 | tf_op jit(solution)/shard_map/ppermute | solution.py:29
  145.4 9.0 %collective-permute-start.24 = (f32[4,64,256]{2,1,0:T(8,128)S(1)}, f32[4,64,256]{2,1,0:T(8,128)S(1)}, u32[]{:S(2)}, u32[]{:S(2)}) collective-permute-start(f32[4,64,256]{2,1,0:T(8,128)S(1)} %slice.97), channel_id=1, source_target_pairs={{0,8},{8,0},{16,24},{24,16},{1,9},{9,1},{17,25},{25,17},{2,10},{10... | collective-permute-start | bytes 786440 | tf_op jit(solution)/shard_map/ppermute | solution.py:29
  145.5 8.9 %collective-permute-start.22 = (f32[2,64,256]{2,1,0:T(8,128)S(1)}, f32[2,64,256]{2,1,0:T(8,128)S(1)}, u32[]{:S(2)}, u32[]{:S(2)}) collective-permute-start(f32[2,64,256]{2,1,0:T(8,128)S(1)} %get-tuple-element.34), channel_id=1, source_target_pairs={{0,2},{1,3},{2,0},{3,1},{4,6},{5,7},{6,4},{7,5},{8,10},{9,11},{10,... | collective-permute-start | bytes 393224 | tf_op jit(solution)/shard_map/ppermute | solution.py:29
  148.9 9.4 %collective-permute-start.21 = (f32[1,64,256]{2,1,0:T(8,128)S(1)}, f32[1,64,256]{2,1,0:T(8,128)S(1)}, u32[]{:S(2)}, u32[]{:S(2)}) collective-permute-start(f32[1,64,256]{2,1,0:T(8,128)S(1)} %get-tuple-element.58), channel_id=1, source_target_pairs={{0,4},{1,5},{2,6},{3,7},{4,0},{5,1},{6,2},{7,3},{8,12},{9,13},{10,... | collective-permute-start | bytes 196616 | tf_op jit(solution)/shard_map/ppermute | solution.py:29
  154.5 5.6 %collective-permute-start.25 = (f32[2,64,256]{2,1,0:T(8,128)S(1)}, f32[2,64,256]{2,1,0:T(8,128)S(1)}, u32[]{:S(2)}, u32[]{:S(2)}) collective-permute-start(f32[2,64,256]{2,1,0:T(8,128)S(1)} %get-tuple-element.52), channel_id=1, source_target_pairs={{0,16},{8,24},{16,0},{24,8},{1,17},{9,25},{17,1},{25,9},{2,18},{10... | collective-permute-start | bytes 393224 | tf_op jit(solution)/shard_map/ppermute | solution.py:29
  154.6 5.5 %collective-permute-start.23 = (f32[1,64,256]{2,1,0:T(8,128)S(1)}, f32[1,64,256]{2,1,0:T(8,128)S(1)}, u32[]{:S(2)}, u32[]{:S(2)}) collective-permute-start(f32[1,64,256]{2,1,0:T(8,128)S(1)} %get-tuple-element.56), channel_id=1, source_target_pairs={{0,4},{1,5},{2,6},{3,7},{4,0},{5,1},{6,2},{7,3},{8,12},{9,13},{10,... | collective-permute-start | bytes 196616 | tf_op jit(solution)/shard_map/ppermute | solution.py:29
  (9 other events, 55.8 us)

commit v3 on v2

v3 whole, which is shorter than its diff:
```python
import functools

import jax
import jax.numpy as jnp
from jax import lax
from jax.experimental import pallas as pl
from jax.experimental.pallas import tpu as pltpu
from jax.sharding import PartitionSpec as P

F32 = jnp.float32
BF16 = jnp.bfloat16
NN = (((1,), (0,)), ((), ()))
NT = (((1,), (1,)), ((), ()))
VMEM_LIMIT = 18 * 2**20
PROJECT_LIMIT = 62 * 2**20
STREAM_LIMIT = 36 * 2**20
GROUP = 8


def exact(left, right, dims):
    return lax.dot_general(
        left, right, dims, precision=lax.Precision.HIGHEST, preferred_element_type=F32
    )


def masks_of(axis):
    return [2**bit for bit in range(lax.axis_size(axis).bit_length() - 1)]


def swap(value, axis, mask):
    pairs = [(source, source ^ mask) for source in range(lax.axis_size(axis))]
    return lax.ppermute(value, axis, pairs)


def place(device, masks):
    spot = jnp.zeros_like(device)
    for mask in masks:
        spot = spot * 2 + (jnp.bitwise_and(device, mask) != 0).astype(jnp.int32)
    return spot


def pieces_shape(rows, columns, devices):
    return (devices, 2 * rows // devices, columns // 2)


def to_pieces(value, pieces_ref):
    pieces, depth, width = pieces_ref.shape
    for piece in range(pieces):
        row, half = piece // 2 * depth, piece % 2 * width
        pieces_ref[piece] = value[row : row + depth, half : half + width]


def from_pieces(pieces_ref):
    pieces = pieces_ref.shape[0]
    halves = [[pieces_ref[p] for p in range(side, pieces, 2)] for side in (0, 1)]
    return jnp.concatenate([jnp.concatenate(half, axis=0) for half in halves], axis=1)


def total_kernel(got_ref, out_ref):
    total = got_ref[0]
    for piece in range(1, got_ref.shape[0]):
        total = total + got_ref[piece]
    for piece in range(got_ref.shape[0]):
        out_ref[piece] = total


def spread_sum(pieces):
    axes = ("row", "col")
    got = lax.all_to_all(pieces, axes, 0, 0, tiled=True)
    (same,) = call(total_kernel, [(pieces.shape, F32)], "total", [got])
    return lax.all_to_all(same, axes, 0, 0, tiled=True)


def near_kernel(forward, chunk, stream, part, count_ref, src_ref, dst_ref, v_ref, tiles_ref, *refs):
    count = count_ref[0]
    chunks = lax.div(count + (chunk - 1), chunk)
    slots = tiles_ref.shape[0]
    if stream:
        out_ref, held_ref, arrived = refs

        def fetch(index):
            part = pl.ds(index * chunk, chunk)
            return pltpu.make_async_copy(
                tiles_ref.at[part], held_ref.at[part], arrived.at[index]
            )

        for index in range(slots // chunk):

            @pl.when(index < chunks)
            def _():
                fetch(index).start()

    else:
        out_ref, held_ref = refs[-1], tiles_ref
    out_ref[...] = jnp.zeros_like(out_ref) if stream or len(refs) == 1 else refs[0][...]

    first, last = (lax.min(chunks, slots // chunk * (part[0] + end) // part[1]) for end in (0, 1))

    def near(index, carry):
        if stream:
            fetch(index).wait()
        for s in range(chunk):
            tile = index * chunk + s
            v = v_ref[src_ref[tile]]
            v = jnp.where(tile < count, v, jnp.zeros_like(v))
            out_ref[dst_ref[tile]] += lax.dot_general(
                v, held_ref[tile], NT if forward else NN, preferred_element_type=F32
            )
        return carry

    lax.fori_loop(first, last, near, 0)
    if stream:

        def rest(index, carry):
            fetch(index).wait()
            return carry

        lax.fori_loop(last, chunks, rest, 0)


def near_products(
    forward, v, tiles, count, src, dst, part=(0, 1), out_blocks=None, start=None, stream=False, after=(),
    far=(),
):
    slots, width, _ = tiles.shape
    rhs = v.shape[1]
    chunk = 32

    def body(*refs):
        far_refs, refs = refs[len(after) : len(after) + len(far)], refs[len(after) + len(far) :]
        near_kernel(forward, chunk, stream, part, *refs)
        if far:
            src, dst, inner, outer = far_refs
            add_far(GROUP, src, dst, refs[3], inner, outer, refs[-1])

    extra = [] if start is None else [start]
    total = jax.ShapeDtypeStruct((out_blocks, rhs, width) if start is None else start.shape, F32)
    smem = pl.BlockSpec(memory_space=pltpu.SMEM)
    vmem = pl.BlockSpec(memory_space=pltpu.VMEM)
    hbm = pl.BlockSpec(memory_space=pltpu.HBM)
    return pl.pallas_call(
        body,
        out_shape=[total, jax.ShapeDtypeStruct(tiles.shape, tiles.dtype)] if stream else [total],
        in_specs=[pl.BlockSpec(memory_space=pl.ANY)] * len(after)
        + ([smem] * 2 + [vmem] * 2 if far else [])
        + [smem] * 3
        + [vmem]
        + [hbm if stream else vmem]
        + [vmem] * len(extra),
        out_specs=[vmem, vmem] if stream else [vmem],
        scratch_shapes=[pltpu.SemaphoreType.DMA((slots // chunk,))] if stream else [],
        compiler_params=pltpu.CompilerParams(vmem_limit_bytes=STREAM_LIMIT if stream else VMEM_LIMIT),
        cost_estimate=pl.CostEstimate(
            flops=4 * slots * rhs * width * width,
            bytes_accessed=2 * slots * width * width,
            transcendentals=0,
        ),
        name="near_forward" if forward else "near_transposed",
    )(*after, *far, count, src, dst, v, tiles, *extra)


def add_far(group, src_ref, dst_ref, v_ref, inner_ref, outer_ref, out_ref):
    rhs = v_ref.shape[1]
    panels = src_ref.shape[0]
    prank = inner_ref.shape[0] // panels
    shape = (group * rhs, group * prank)
    of_row = lax.div(lax.broadcasted_iota(jnp.int32, shape, 0), rhs)
    of_lane = lax.div(lax.broadcasted_iota(jnp.int32, shape, 1), prank)
    same = of_row == of_lane
    for start in range(0, panels, group):
        v = jnp.concatenate([v_ref[src_ref[start + g]] for g in range(group)], axis=0)
        part = pl.ds(start * prank, group * prank)
        half = lax.dot_general(v, inner_ref[part, :], NT, preferred_element_type=F32)
        half = jnp.where(same, half, 0.0).astype(BF16)
        prod = lax.dot_general(half, outer_ref[part, :], NN, preferred_element_type=F32)
        for g in range(group):
            out_ref[dst_ref[start + g]] += prod[g * rhs : (g + 1) * rhs]


def far_kernel(group, src_ref, dst_ref, v_ref, inner_ref, outer_ref, out_ref):
    out_ref[...] = jnp.zeros_like(out_ref)
    add_far(group, src_ref, dst_ref, v_ref, inner_ref, outer_ref, out_ref)


def far_products(v, src, dst, inner, outer, out_blocks):
    _, rhs, width = v.shape
    smem = pl.BlockSpec(memory_space=pltpu.SMEM)
    vmem = pl.BlockSpec(memory_space=pltpu.VMEM)
    return pl.pallas_call(
        functools.partial(far_kernel, GROUP),
        out_shape=jax.ShapeDtypeStruct((out_blocks, rhs, width), F32),
        in_specs=[smem] * 2 + [vmem] * 3,
        out_specs=vmem,
        compiler_params=pltpu.CompilerParams(vmem_limit_bytes=VMEM_LIMIT),
        cost_estimate=pl.CostEstimate(
            flops=4 * rhs * width * inner.shape[0],
            bytes_accessed=2 * inner.size,
            transcendentals=0,
        ),
        name="far_transposed",
    )(src, dst, v, inner, outer)


def eliminate(systems, block=8):
    size, lanes = systems[0].shape
    parts = [[s[t : t + 8, :] for t in range(0, size, 8)] for s in systems]
    sub = lax.broadcasted_iota(jnp.int32, (8, lanes), 0)
    every = range(block)
    for k in range(0, size, block):
        home, offset = k // 8, k % 8
        for n, part in enumerate(parts):
            cols = [[jnp.broadcast_to(p[:, k + j : k + j + 1], p.shape) for p in part] for j in every]
            head = part[home]
            rows = [jnp.broadcast_to(head[offset + i : offset + i + 1, :], head.shape) for i in every]
            small = [
                [jnp.broadcast_to(cols[j][home][offset + i : offset + i + 1, :], head.shape) for j in every]
                for i in every
            ]
            for p in every:
                inverse = 1.0 / small[p][p]
                rows[p] = rows[p] * inverse
                for j in range(p + 1, block):
                    small[p][j] = small[p][j] * inverse
                for i in every:
                    if i != p:
                        factor = small[i][p]
                        rows[i] = rows[i] - factor * rows[p]
                        for j in range(p + 1, block):
                            small[i][j] = small[i][j] - factor * small[p][j]
            for t in range(len(part)):
                value = part[t]
                for j in every:
                    value = value - cols[j][t] * rows[j]
                part[t] = value
            for i in every:
                part[home] = jnp.where(sub == offset + i, rows[i], part[home])
    return [jnp.concatenate(part, axis=0)[:, size:] for part in parts]


def symmetric(matrix):
    return 0.5 * (matrix + matrix.T)


def call(kernel, outs, name, operands, after=(), limit=VMEM_LIMIT):
    vmem = pl.BlockSpec(memory_space=pltpu.VMEM)

    def body(*refs):
        kernel(*refs[len(after) :])

    return pl.pallas_call(
        body,
        out_shape=[jax.ShapeDtypeStruct(shape, dtype) for shape, dtype in outs],
        in_specs=[pl.BlockSpec(memory_space=pl.ANY)] * len(after) + [vmem] * len(operands),
        out_specs=[vmem] * len(outs),
        compiler_params=pltpu.CompilerParams(vmem_limit_bytes=limit),
        name=name,
    )(*after, *operands)


def pack(direc, packed_ref):
    blocks, _, width = packed_ref.shape
    for b in range(blocks):
        packed_ref[b] = direc[:, b * width : (b + 1) * width].astype(BF16)


def project_kernel(rhs_hbm, factor_hbm, out_ref, rhs, factor, arrived):
    parts = arrived.shape[0] - 1
    ranks = factor.shape[0] // parts
    copies = [pltpu.make_async_copy(rhs_hbm, rhs, arrived.at[parts])]
    for p in range(parts):
        part = pl.ds(p * ranks, ranks)
        copies.append(
            pltpu.make_async_copy(factor_hbm.at[part], factor.at[part], arrived.at[p])
        )
    for copy in copies:
        copy.start()
    copies[0].wait()
    resid = rhs[...]
    done = []
    for p in range(parts):
        copies[1 + p].wait()
        done.append(exact(factor[p * ranks : (p + 1) * ranks], resid, NT).T)
    to_pieces(jnp.concatenate(done, axis=1), out_ref)


def project(shape, rhs, factor):
    parts = 2
    return pl.pallas_call(
        project_kernel,
        out_shape=jax.ShapeDtypeStruct(shape, F32),
        in_specs=[pl.BlockSpec(memory_space=pltpu.HBM)] * 2,
        out_specs=pl.BlockSpec(memory_space=pltpu.VMEM),
        scratch_shapes=[
            pltpu.VMEM(rhs.shape, F32),
            pltpu.VMEM(factor.shape, F32),
            pltpu.SemaphoreType.DMA((parts + 1,)),
        ],
        compiler_params=pltpu.CompilerParams(vmem_limit_bytes=PROJECT_LIMIT),
        name="project",
    )(rhs, factor)


def stage_kernel(*refs):
    sources, held, arrived = refs[: len(refs) // 2], refs[len(refs) // 2 : -1], refs[-1]
    copies = [
        pltpu.make_async_copy(source, target, arrived.at[index])
        for index, (source, target) in enumerate(zip(sources, held))
    ]
    for copy in copies:
        copy.start()
    for copy in copies:
        copy.wait()


def stage(operands):
    return pl.pallas_call(
        stage_kernel,
        out_shape=[jax.ShapeDtypeStruct(value.shape, value.dtype) for value in operands],
        in_specs=[pl.BlockSpec(memory_space=pltpu.HBM)] * len(operands),
        out_specs=[pl.BlockSpec(memory_space=pltpu.VMEM)] * len(operands),
        scratch_shapes=[pltpu.SemaphoreType.DMA((len(operands),))],
        compiler_params=pltpu.CompilerParams(vmem_limit_bytes=VMEM_LIMIT),
        cost_estimate=pl.CostEstimate(flops=0, bytes_accessed=2**24, transcendentals=0),
        name="stage",
    )(*operands)


def begin_kernel(rhs, weight, factor, proj_ref, direc_ref, packed_ref):
    proj = from_pieces(proj_ref)
    direc = rhs[...] + exact(proj * weight[...], factor[...], NN)
    direc_ref[...] = direc
    pack(direc, packed_ref)


def image_of(self_term, direc, terms):
    both = terms[0][...] + terms[1][...] + terms[2][...] + terms[3][...]
    return self_term * direc + jnp.concatenate([both[b] for b in range(both.shape[0])], axis=1)


def copy_kernel(value_ref, out_ref):
    out_ref[...] = value_ref[...]


def fold_kernel(*refs):
    paths = len(refs) // 4
    own, got, keep, send = (refs[paths * index : paths * (index + 1)] for index in range(4))
    for p in range(paths):
        half = own[p].shape[0] // 2
        keep[p][...] = own[p][:half] + got[p][:half]
        send[p][...] = own[p][half:] + got[p][half:]


def join_kernel(transposed_ref, *refs):
    paths = len(refs) // 2 - 2
    keep, send, col_keep, col_send = refs[-4:]
    for p in range(paths):
        own, got = refs[p], refs[paths + p]
        half = own.shape[0] // 2
        part = pl.ds(p * half, half)
        keep[part] = own[:half] + got[:half]
        send[part] = own[half:] + got[half:]
    half = col_keep.shape[0]
    col_keep[...] = transposed_ref[:half]
    col_send[...] = transposed_ref[half:]


def inner_kernel(self_term, rhs, factor, direc_ref, *refs):
    terms, (image_ref, out_ref) = refs[:-2], refs[-2:]
    direc = direc_ref[...]
    image = image_of(self_term[...], direc, terms)
    image_ref[...] = image
    resid = rhs[...]
    count = resid.shape[0]
    stack = jnp.concatenate([direc, resid, image], axis=0)
    against = exact(stack, image, NT)
    own = exact(resid, resid, NT)
    pairs = jnp.concatenate(
        [against[:count], against[count : 2 * count], against[2 * count :], own], axis=1
    )
    to_pieces(jnp.concatenate([exact(image, factor[...], NT), pairs], axis=1), out_ref)


def advance_kernel(
    weight_ref,
    factor,
    rhs,
    sums_ref,
    proj_ref,
    direc_ref,
    image_ref,
    solution_ref,
    resid_ref,
    next_ref,
    packed_ref,
    rho_ref,
):
    count = rho_ref.shape[0]
    weight, proj, sums = weight_ref[...], from_pieces(proj_ref), from_pieces(sums_ref)
    rank = proj.shape[1]
    image_proj = sums[:, :rank]
    gram, cross, square, own = (
        sums[:, rank + count * index : rank + count * (index + 1)] for index in range(4)
    )
    rho = own + exact(proj * weight, proj, NT)
    unit = (
        lax.broadcasted_iota(jnp.int32, (count, count), 0)
        == lax.broadcasted_iota(jnp.int32, (count, count), 1)
    ).astype(F32)
    alpha, inverse = eliminate(
        [
            jnp.concatenate([symmetric(gram), rho], axis=1),
            jnp.concatenate([symmetric(rho), unit], axis=1),
        ]
    )
    alpha_t = alpha.T
    proj = proj - exact(alpha_t, image_proj, NN)
    mixed = exact(cross, alpha, NN)
    new = own - mixed - mixed.T + exact(exact(alpha_t, square, NN), alpha, NN)
    new = new + exact(proj * weight, proj, NT)
    beta = exact(inverse, new, NN)
    direc = direc_ref[...]
    resid = rhs[...] - exact(alpha_t, image_ref[...], NN)
    after = resid + exact(proj * weight, factor[...], NN) + exact(beta.T, direc, NN)
    pack(after, packed_ref)
    solution_ref[...] = exact(alpha_t, direc, NN)
    resid_ref[...] = resid
    next_ref[...] = after
    rho_ref[...] = new


def last_image_kernel(self_term, direc_ref, *refs):
    terms, (image_ref, gram_ref) = refs[:-2], refs[-2:]
    direc = direc_ref[...]
    image = image_of(self_term[...], direc, terms)
    image_ref[...] = image
    gram = exact(direc, image, NT)
    half = gram.shape[0] // 2
    gram_ref[...] = jnp.concatenate([gram[:half], gram[half:]], axis=1)


def finish_kernel(
    gram_ref, rho_ref, solution_ref, resid_ref, direc_ref, image_ref, out_ref, left_ref
):
    count = rho_ref.shape[0]
    gram = gram_ref[0]
    for index in range(1, gram_ref.shape[0]):
        gram = gram + gram_ref[index]
    gram = jnp.concatenate([gram[:, :count], gram[:, count:]], axis=0)
    (alpha,) = eliminate([jnp.concatenate([symmetric(gram), rho_ref[...]], axis=1)])
    alpha_t = alpha.T
    out_ref[...] = solution_ref[...] + exact(alpha_t, direc_ref[...], NN)
    left_ref[...] = resid_ref[...] - exact(alpha_t, image_ref[...], NN)


def local(
    rhs,
    self_term,
    near_tiles,
    near_rows,
    near_cols,
    near_counts,
    far_left,
    far_right,
    far_rows,
    far_cols,
    nys_factor,
    nys_weight,
):
    width = near_tiles.shape[1]
    count_rhs, columns = rhs.shape
    blocks = columns // width
    n_row, n_col = lax.axis_size("row"), lax.axis_size("col")
    grid_row, grid_col = lax.axis_index("row"), lax.axis_index("col")
    count = near_counts[grid_row * n_col + grid_col]
    rank = nys_factor.shape[0]
    self_row = self_term.reshape(1, columns)
    weight = nys_weight.reshape(1, rank)
    prank = far_left.shape[2]
    left = far_left.transpose(0, 2, 1).reshape(-1, width)
    right = far_right.transpose(0, 2, 1).reshape(-1, width)

    col_masks, row_masks = masks_of("col"), masks_of("row")
    gather_col, gather_row = col_masks[::-1], row_masks[::-1]
    path_a = col_masks[-2::-1] + col_masks[-1:]
    path_b = col_masks
    scatter_row = row_masks

    def relative(ids, me):
        return jnp.bitwise_xor(ids // blocks, me), ids % blocks

    def gathered(ids, me, masks):
        device, block = relative(ids, me)
        return place(device, masks[::-1]) * blocks + block

    def scattered_col(ids):
        device, block = relative(ids, grid_col)
        path = jnp.where(block % 2 == 0, place(device, path_a), place(device, path_b))
        return block * n_col + path

    def scattered_row(ids):
        device, block = relative(ids, grid_row)
        return place(device, scatter_row) * blocks + block

    row_src = gathered(near_rows, grid_col, gather_col)
    col_src = gathered(near_cols, grid_row, gather_row)
    far_row_src = gathered(far_rows, grid_col, gather_col)
    far_col_src = gathered(far_cols, grid_row, gather_row)
    row_dst, far_row_dst = scattered_col(near_rows), scattered_col(far_rows)
    col_dst, far_col_dst = scattered_row(near_cols), scattered_row(far_cols)

    def operate(packed, tiles, first):
        col_side = row_side = packed
        for mask in gather_row:
            col_side = jnp.concatenate([col_side, swap(col_side, "row", mask)], axis=0)
        for mask in gather_col[:-1]:
            row_side = jnp.concatenate([row_side, swap(row_side, "col", mask)], axis=0)
        near = (count, col_src, row_dst)
        forward, *streamed = near_products(
            True, col_side, tiles, *near, part=(0, 2), out_blocks=n_col * blocks, stream=first
        )
        held = streamed[0] if first else tiles
        (row_side,) = call(
            copy_kernel, [(row_side.shape, BF16)], "gathered", [row_side], [forward]
        )
        (forward,) = near_products(
            True, col_side, held, *near, part=(1, 2), start=forward, after=[row_side],
            far=(far_col_src, far_row_dst, right, left),
        )
        other_side = swap(row_side, "col", gather_col[-1])
        row_side = jnp.concatenate([row_side, other_side], axis=0)

        half = n_col // 2
        sends = [forward[b * n_col + half : (b + 1) * n_col] for b in range(blocks)]
        paths = [path_a if b % 2 == 0 else path_b for b in range(blocks)]
        got = [swap(sends[b], "col", paths[b][0]) for b in range(blocks)]
        transposed = far_products(
            row_side, far_row_src, far_col_dst, left, right, n_row * blocks
        )
        own = [forward[b * n_col : b * n_col + half] for b in range(blocks)]
        for step in range(1, len(col_masks) - 1):
            size = (own[0].shape[0] // 2, count_rhs, width)
            folded = call(
                fold_kernel, [(size, F32)] * (2 * blocks), "fold", [*own, *got], [transposed]
            )
            own = folded[:blocks]
            got = [swap(folded[blocks + b], "col", paths[b][step]) for b in range(blocks)]
            if step == 1:
                (transposed,) = near_products(
                    False, row_side, held, count, row_src, col_dst, start=transposed,
                    after=[folded[blocks]],
                )
        size = (own[0].shape[0] // 2 * blocks, count_rhs, width)
        col_size = (n_row * blocks // 2, count_rhs, width)
        own, send, col_own, col_send = call(
            join_kernel, [(size, F32)] * 2 + [(col_size, F32)] * 2, "join", [transposed, *own, *got]
        )
        row_terms = (own, swap(send, "col", col_masks[-1]))
        for step, mask in enumerate(scatter_row):
            if step:
                transposed = col_own + col_got
                half = transposed.shape[0] // 2
                col_own, col_send = transposed[:half], transposed[half:]
            col_got = swap(col_send, "row", mask)
        col_terms = (col_own, col_got)
        return [*row_terms, *col_terms], held

    devices = n_row * n_col
    full, packs = (count_rhs, columns), (blocks, count_rhs, width)
    shape_of = lambda wanted: pieces_shape(count_rhs, wanted, devices)
    partial = project(shape_of(rank), rhs, nys_factor)
    count = count.reshape(1)
    rhs, nys_factor, weight, self_row = stage([rhs, nys_factor, weight, self_row])
    proj = spread_sum(partial)
    direc, packed = call(
        begin_kernel, [(full, F32), (packs, BF16)], "begin", [rhs, weight, nys_factor, proj]
    )
    terms, tiles = operate(packed, near_tiles, True)
    image, partial = call(
        inner_kernel, [(full, F32), (shape_of(rank + 4 * count_rhs), F32)], "inner",
        [self_row, rhs, nys_factor, direc, *terms],
    )
    sums = spread_sum(partial)
    solution, residual, direc, packed, rho = call(
        advance_kernel,
        [(full, F32), (full, F32), (full, F32), (packs, BF16), ((count_rhs, count_rhs), F32)],
        "advance", [weight, nys_factor, rhs, sums, proj, direc, image],
    )
    terms, _ = operate(packed, tiles, False)
    image, partial = call(
        last_image_kernel, [(full, F32), ((count_rhs // 2, 2 * count_rhs), F32)], "last_image",
        [self_row, direc, *terms],
    )
    for mask in row_masks:
        partial = partial + swap(partial, "row", mask)
    gram = lax.all_to_all(
        jnp.broadcast_to(partial, (n_col, *partial.shape)), "col", 0, 0, tiled=True
    )
    return tuple(
        call(
            finish_kernel, [(full, F32), (full, F32)], "finish",
            [gram, rho, solution, residual, direc, image],
        )
    )


def solution(mesh):
    in_specs = (
        P(None, ("row", "col")),
        P(("row", "col")),
        P(("row", "col"), None, None),
        P(("row", "col")),
        P(("row", "col")),
        P(),
        P(("row", "col"), None, None),
        P(("row", "col"), None, None),
        P(("row", "col")),
        P(("row", "col")),
        P(None, ("row", "col")),
        P(),
    )
    out_specs = (P(None, ("row", "col")), P(None, ("row", "col")))
    return jax.shard_map(local, mesh=mesh, in_specs=in_specs, out_specs=out_specs, check_vma=False)
```

time: 185 us -> 173 us (0.935)
  blocking collectives: 44.5 us -> 33.4 us
  waiting for transfers between devices: 51.9 us -> 59.2 us
  starting transfers between devices: 33.7 us -> 29.4 us
  Pallas kernels: 42.3 us -> 38.8 us
    all_to_all x2 -> x1, blocking collectives: 24.1 us -> 11 us  [spread_sum(): got = lax.all_to_all(pieces, axes, 0, 0, tiled=True)]
    ppermute x26, waiting for transfers between devices: 37.8 us -> 50.6 us  [swap(): return lax.ppermute(value, axis, pairs)]
    all_to_all x0 -> x1, blocking collectives: none -> 11 us  [local(): lax.all_to_all(jnp.broadcast_to(partial, (n_col, *partial.shape)), 'col',...]
    all_to_all x2 -> x1, blocking collectives: 20.4 us -> 11.4 us  [spread_sum(): return lax.all_to_all(same, axes, 0, 0, tiled=True)]
    all_to_all x1, waiting for transfers between devices: 7.71 us -> 2.26 us  [spread_sum(): return lax.all_to_all(same, axes, 0, 0, tiled=True)]
    pallas_call x11 -> x13, Pallas kernels: 17.8 us -> 13.2 us  [call(): pl.pallas_call(body, out_shape=[jax.ShapeDtypeStruct(shape, dtype) for sh...]
    ppermute x26, starting transfers between devices: 23.8 us -> 19.5 us  [swap(): return lax.ppermute(value, axis, pairs)]
    unnamed x26 -> x22, local copies, waits for them, and re-layouts: 7.51 us -> 5.77 us
  transfers between devices with their start and end apart: 28 -> 28, of which waited for: 20 -> 20; matrix products, arithmetic and copies ran while one was open for 2% -> 3% of each run, Pallas kernels for 13% -> 11%
where the time goes in v3:
time: 173 us; the launch traced here: 172 us
  waiting for transfers between devices  59.2 us (34%)
  Pallas kernels  38.8 us (22%)
  blocking collectives  33.4 us (19%)
  starting transfers between devices  29.4 us (17%)
  local copies, waits for them, and re-layouts  7.27 us (4%)
  other arithmetic  2.97 us (2%)
    ppermute x26, waiting for transfers between devices, swap(): return lax.ppermute(value, axis, pairs)  50.6 us
    ppermute x26, starting transfers between devices, swap(): return lax.ppermute(value, axis, pairs)  19.5 us
    pallas_call x6, Pallas kernels, near_products(): pl.pallas_call(body, out_shape=[total, jax.ShapeDtypeStruct(tiles.shape,...  17.3 us
    pallas_call x13, Pallas kernels, call(): pl.pallas_call(body, out_shape=[jax.ShapeDtypeStruct(shape, dtype) for sh...  13.2 us
    all_to_all x1, blocking collectives, spread_sum(): return lax.all_to_all(same, axes, 0, 0, tiled=True)  11.4 us
    all_to_all x1, blocking collectives, spread_sum(): got = lax.all_to_all(pieces, axes, 0, 0, tiled=True)  11 us
    all_to_all x1, blocking collectives, local(): lax.all_to_all(jnp.broadcast_to(partial, (n_col, *partial.shape)), 'col',...  11 us
    all_to_all x1, starting transfers between devices, spread_sum(): got = lax.all_to_all(pieces, axes, 0, 0, tiled=True)  7.3 us
  transfers between devices with their start and end apart: 28, of which 20 were waited for; matrix products, arithmetic and copies ran while one was open for 3% of the time, Pallas kernels for 11%

profile of v3, /device:TPU:0, one launch (start us, length us, event | category | flops | bytes accessed | tf_op | source)
XLA Modules:
  0.0 172.0 jit_solution(10074058517079618314)
XLA Ops:
  0.6 3.9 %project.1 = f32[32,4,256]{2,1,0:T(4,128)} custom-call(f32[64,512]{1,0:T(8,128)} %rhs_hbm.1, f32[512,512]{1,0:T(8,128)} %factor_hbm.1), custom_call_target="tpu_custom_call" | custom-call | tf_op jit(solution)/shard_map/project/pallas_call | solution.py:288
  4.5 7.3 %all-to-all-start = ((f32[32,4,256]{2,1,0:T(4,128)}), f32[32,4,256]{2,1,0:T(4,128)S(1)}, u32[]{:S(2)}, u32[]{:S(2)}) async-start(f32[32,4,256]{2,1,0:T(4,128)} %project.1), calls=%async_computation | async-start | bytes 262144 | tf_op jit(solution)/shard_map/all_to_all | solution.py:69
  13.2 6.4 %all-to-all-done.refs_0_ = f32[32,4,256]{2,1,0:T(4,128)S(1)} async-done(((f32[32,4,256]{2,1,0:T(4,128)}), f32[32,4,256]{2,1,0:T(4,128)S(1)}, u32[]{:S(2)}, u32[]{:S(2)}) %all-to-all-start) | async-done | bytes 131104 | tf_op jit(solution)/shard_map/all_to_all | solution.py:69
  20.3 2.6 %all-to-all-start.1 = ((f32[32,4,256]{2,1,0:T(4,128)}), f32[32,4,256]{2,1,0:T(4,128)S(1)}, u32[]{:S(2)}, u32[]{:S(2)}) async-start(f32[32,4,256]{2,1,0:T(4,128)} %total.2), calls=%async_computation.1 | async-start | bytes 262144 | tf_op jit(solution)/shard_map/all_to_all | solution.py:71
  28.3 2.3 %all-to-all-done.1.refs_3_.refs_4_ = f32[32,4,256]{2,1,0:T(4,128)S(1)} async-done(((f32[32,4,256]{2,1,0:T(4,128)}), f32[32,4,256]{2,1,0:T(4,128)S(1)}, u32[]{:S(2)}, u32[]{:S(2)}) %all-to-all-start.1) | async-done | bytes 131104 | tf_op jit(solution)/shard_map/all_to_all | solution.py:71
  36.4 2.6 %collective-permute-done.2 = bf16[2,64,256]{2,1,0:T(8,128)(2,1)S(1)} collective-permute-done((bf16[2,64,256]{2,1,0:T(8,128)(2,1)S(1)}, bf16[2,64,256]{2,1,0:T(8,128)(2,1)S(1)}, u32[]{:S(2)}, u32[]{:S(2)}) %collective-permute-start.2) | collective-permute-done | bytes 65568 | tf_op jit(solution)/shard_map/ppermute | solution.py:32
  40.5 4.8 %near_forward.4 = (f32[16,64,256]{2,1,0:T(8,128)S(1)}, bf16[128,256,256]{2,1,0:T(8,128)(2,1)S(1)}) custom-call(s32[1]{0:T(128)} %dynamic_slice.3.refs_0_.refs_5_.refs_1_, s32[128]{0:T(128)S(1)} %get-tuple-element.92.refs_1_.refs_6_.refs_3_, s32[128]{0:T(128)S(1)} %get-tuple-element.93.refs_2_.refs_7_, ...), custom_call_target="tpu_custom_call" | custom-call | flops 2147483648 | bytes 16777216 | tf_op jit(solution)/shard_map/near_forward/pallas_call | solution.py:141
  46.7 2.8 %near_forward.5 = f32[16,64,256]{2,1,0:T(8,128)S(1)} custom-call(bf16[8,64,256]{2,1,0:T(8,128)(2,1)S(1)} %gathered.2.refs_0_, s32[64]{0:T(128)S(1)} %fusion.dst_ref.refs_1_, s32[64]{0:T(128)S(1)} %get-tuple-element.72.refs_2_, bf16[2048,256]{1,0:T(8,128)(2,1)S(1)} %bitcast.12, bf16[2048,256]{1,0:T(8,128)(2,1)S(1)} %bitcast.8, ...), custom_call_target="tpu_custom_call" | custom-call | flops 2147483648 | bytes 16777216 | tf_op jit(solution)/shard_map/near_forward/pallas_call | solution.py:141
  51.9 2.6 %collective-permute-done.4 = bf16[8,64,256]{2,1,0:T(8,128)(2,1)S(1)} collective-permute-done((bf16[8,64,256]{2,1,0:T(8,128)(2,1)S(1)}, bf16[8,64,256]{2,1,0:T(8,128)(2,1)S(1)}, u32[]{:S(2)}, u32[]{:S(2)}) %collective-permute-start.4) | collective-permute-done | bytes 262176 | tf_op jit(solution)/shard_map/ppermute | solution.py:32
  54.6 2.1 %far_transposed.2.refs_0_.refs_6_ = f32[8,64,256]{2,1,0:T(8,128)S(1)} custom-call(s32[64]{0:T(128)S(1)} %multiply_add_fusion.3.src_ref, s32[64]{0:T(128)S(1)} %fusion.dst_ref.refs_1_, bf16[16,64,256]{2,1,0:T(8,128)(2,1)S(1)} %pad_maximum_fusion.v_ref.refs_4_, bf16[2048,256]{1,0:T(8,128)(2,1)S(1)} %bitcast.9, bf16[2048,256]{1,0:T(8,128)(2,1)S(1)} %bitcast.13), custom_call_target="tpu_custom_call" | custom-call | flops 134217728 | bytes 1048576 | tf_op jit(solution)/shard_map/far_transposed/pallas_call | solution.py:189
  56.7 3.5 %collective-permute-done.6.refs_4_ = f32[4,64,256]{2,1,0:T(8,128)S(1)} collective-permute-done((f32[4,64,256]{2,1,0:T(8,128)S(1)}, f32[4,64,256]{2,1,0:T(8,128)S(1)}, u32[]{:S(2)}, u32[]{:S(2)}) %collective-permute-start.6) | collective-permute-done | bytes 262176 | tf_op jit(solution)/shard_map/ppermute | solution.py:32
  62.0 2.1 %near_transposed.2.refs_0_ = f32[8,64,256]{2,1,0:T(8,128)S(1)} custom-call(f32[2,64,256]{2,1,0:T(8,128)S(1)} %get-tuple-element.43.refs_0_, s32[1]{0:T(128)} %dynamic_slice.3.refs_0_.refs_5_.refs_1_, s32[128]{0:T(128)S(1)} %get-tuple-element.68.refs_2_, s32[128]{0:T(128)S(1)} %get-tuple-element.92.refs_1_.refs_6_.refs_3_, ...), custom_call_target="tpu_custom_call" | custom-call | flops 2147483648 | bytes 16777216 | tf_op jit(solution)/shard_map/near_transposed/pallas_call | solution.py:141
  64.1 1.7 collective-permute-done.8.refs_4_
  69.6 7.0 %collective-permute-done.9.refs_5_ = f32[2,64,256]{2,1,0:T(8,128)S(1)} collective-permute-done((f32[2,64,256]{2,1,0:T(8,128)S(1)}, f32[2,64,256]{2,1,0:T(8,128)S(1)}, u32[]{:S(2)}, u32[]{:S(2)}) %collective-permute-start.9) | collective-permute-done | bytes 131104 | tf_op jit(solution)/shard_map/ppermute | solution.py:32
  78.2 11.0 %all_to_all.25.refs_0_ = f32[32,4,384]{2,1,0:T(4,128)S(1)} all-to-all(f32[32,4,384]{2,1,0:T(4,128)S(1)} %get-tuple-element.51), channel_id=1, replica_groups=mesh['row'=4,'col'=8] {'row','col'}, dimensions={0} | all-to-all | bytes 393216 | tf_op jit(solution)/shard_map/all_to_all | solution.py:69
  89.3 11.4 %all_to_all.26.refs_3_ = f32[32,4,384]{2,1,0:T(4,128)S(1)} all-to-all(f32[32,4,384]{2,1,0:T(4,128)S(1)} %total.3), channel_id=1, replica_groups=mesh['row'=4,'col'=8] {'row','col'}, dimensions={0} | all-to-all | bytes 393216 | tf_op jit(solution)/shard_map/all_to_all | solution.py:71
  100.7 5.8 %advance.1 = (f32[64,512]{1,0:T(8,128)S(1)}, f32[64,512]{1,0:T(8,128)S(1)}, f32[64,512]{1,0:T(8,128)S(1)}, bf16[2,64,256]{2,1,0:T(8,128)(2,1)S(1)}, f32[64,64]{1,0:T(8,128)S(1)}) custom-call(f32[1,512]{1,0:T(1,128)S(1)} %get-tuple-element.36.refs_1_.refs_0_, f32[512,512]{1,0:T(8,128)S(1)} %copy-done.4, ...), custom_call_target="tpu_custom_call" | custom-call | tf_op jit(solution)/shard_map/advance/pallas_call | solution.py:250
  106.5 1.6 collective-permute-start.14
  108.7 4.5 %collective-permute-done.14 = bf16[2,64,256]{2,1,0:T(8,128)(2,1)S(1)} collective-permute-done((bf16[2,64,256]{2,1,0:T(8,128)(2,1)S(1)}, bf16[2,64,256]{2,1,0:T(8,128)(2,1)S(1)}, u32[]{:S(2)}, u32[]{:S(2)}) %collective-permute-start.14) | collective-permute-done | bytes 65568 | tf_op jit(solution)/shard_map/ppermute | solution.py:32
  114.6 2.7 %near_forward.6.refs_0_.refs_10_ = f32[16,64,256]{2,1,0:T(8,128)S(1)} custom-call(s32[1]{0:T(128)} %dynamic_slice.3.refs_0_.refs_5_.refs_1_, s32[128]{0:T(128)S(1)} %get-tuple-element.92.refs_1_.refs_6_.refs_3_, s32[128]{0:T(128)S(1)} %get-tuple-element.93.refs_2_.refs_7_, bf16[8,64,256]{2,1,0:T(8,128)(2,1)S(1)} %constant_dynamic-update-slice_fusion.3.refs_3_.refs_8_, ...), custom_call_target="tpu_custom_call" | custom-call | flops 2147483648 | bytes 16777216 | tf_op jit(solution)/shard_map/near_forward/pallas_call | solution.py:141
  117.3 1.9 %collective-permute-done.15 = bf16[4,64,256]{2,1,0:T(8,128)(2,1)S(1)} collective-permute-done((bf16[4,64,256]{2,1,0:T(8,128)(2,1)S(1)}, bf16[4,64,256]{2,1,0:T(8,128)(2,1)S(1)}, u32[]{:S(2)}, u32[]{:S(2)}) %collective-permute-start.15) | collective-permute-done | bytes 131104 | tf_op jit(solution)/shard_map/ppermute | solution.py:32
  119.2 2.8 %near_forward.7 = f32[16,64,256]{2,1,0:T(8,128)S(1)} custom-call(bf16[8,64,256]{2,1,0:T(8,128)(2,1)S(1)} %gathered.3.refs_0_, s32[64]{0:T(128)S(1)} %fusion.dst_ref.refs_1_, s32[64]{0:T(128)S(1)} %get-tuple-element.72.refs_2_, bf16[2048,256]{1,0:T(8,128)(2,1)S(1)} %bitcast.14, bf16[2048,256]{1,0:T(8,128)(2,1)S(1)} %bitcast.10, ...), custom_call_target="tpu_custom_call" | custom-call | flops 2147483648 | bytes 16777216 | tf_op jit(solution)/shard_map/near_forward/pallas_call | solution.py:141
  124.6 6.7 %collective-permute-done.16 = bf16[8,64,256]{2,1,0:T(8,128)(2,1)S(1)} collective-permute-done((bf16[8,64,256]{2,1,0:T(8,128)(2,1)S(1)}, bf16[8,64,256]{2,1,0:T(8,128)(2,1)S(1)}, u32[]{:S(2)}, u32[]{:S(2)}) %collective-permute-start.16) | collective-permute-done | bytes 262176 | tf_op jit(solution)/shard_map/ppermute | solution.py:32
  131.4 2.1 %far_transposed.3.refs_0_.refs_6_ = f32[8,64,256]{2,1,0:T(8,128)S(1)} custom-call(s32[64]{0:T(128)S(1)} %multiply_add_fusion.3.src_ref, s32[64]{0:T(128)S(1)} %fusion.dst_ref.refs_1_, bf16[16,64,256]{2,1,0:T(8,128)(2,1)S(1)} %pad_maximum_fusion.1.v_ref.refs_4_, bf16[2048,256]{1,0:T(8,128)(2,1)S(1)} %bitcast.11, bf16[2048,256]{1,0:T(8,128)(2,1)S(1)} %bitcast.15), custom_call_target="tpu_custom_call" | custom-call | flops 134217728 | bytes 1048576 | tf_op jit(solution)/shard_map/far_transposed/pallas_call | solution.py:189
  133.5 3.2 %collective-permute-done.18.refs_4_ = f32[4,64,256]{2,1,0:T(8,128)S(1)} collective-permute-done((f32[4,64,256]{2,1,0:T(8,128)S(1)}, f32[4,64,256]{2,1,0:T(8,128)S(1)}, u32[]{:S(2)}, u32[]{:S(2)}) %collective-permute-start.18) | collective-permute-done | bytes 262176 | tf_op jit(solution)/shard_map/ppermute | solution.py:32
  138.4 2.1 %near_transposed.3.refs_0_ = f32[8,64,256]{2,1,0:T(8,128)S(1)} custom-call(f32[2,64,256]{2,1,0:T(8,128)S(1)} %get-tuple-element.55.refs_0_, s32[1]{0:T(128)} %dynamic_slice.3.refs_0_.refs_5_.refs_1_, s32[128]{0:T(128)S(1)} %get-tuple-element.68.refs_2_, s32[128]{0:T(128)S(1)} %get-tuple-element.92.refs_1_.refs_6_.refs_3_, ...), custom_call_target="tpu_custom_call" | custom-call | flops 2147483648 | bytes 16777216 | tf_op jit(solution)/shard_map/near_transposed/pallas_call | solution.py:141
  140.5 1.6 collective-permute-done.20.refs_4_
  142.3 2.3 %collective-permute-start.21 = (f32[2,64,256]{2,1,0:T(8,128)S(1)}, f32[2,64,256]{2,1,0:T(8,128)S(1)}, u32[]{:S(2)}, u32[]{:S(2)}) collective-permute-start(f32[2,64,256]{2,1,0:T(8,128)S(1)} %get-tuple-element.60), channel_id=1, source_target_pairs={{0,4},{1,5},{2,6},{3,7},{4,0},{5,1},{6,2},{7,3},{8,12},{9,13},{10,... | collective-permute-start | bytes 393224 | tf_op jit(solution)/shard_map/ppermute | solution.py:32
  144.8 7.2 %collective-permute-done.21.refs_3_ = f32[2,64,256]{2,1,0:T(8,128)S(1)} collective-permute-done((f32[2,64,256]{2,1,0:T(8,128)S(1)}, f32[2,64,256]{2,1,0:T(8,128)S(1)}, u32[]{:S(2)}, u32[]{:S(2)}) %collective-permute-start.21) | collective-permute-done | bytes 131104 | tf_op jit(solution)/shard_map/ppermute | solution.py:32
  154.3 3.0 %collective-permute-done.25 = f32[32,128]{1,0:T(8,128)S(1)} collective-permute-done((f32[32,128]{1,0:T(8,128)S(1)}, f32[32,128]{1,0:T(8,128)S(1)}, u32[]{:S(2)}, u32[]{:S(2)}) %collective-permute-start.25) | collective-permute-done | bytes 16416 | tf_op jit(solution)/shard_map/ppermute | solution.py:32
  157.3 11.0 %all_to_all.27.refs_0_ = f32[8,32,128]{2,1,0:T(8,128)S(1)} all-to-all(f32[8,32,128]{2,1,0:T(8,128)S(1)} %broadcast_in_dim.3), channel_id=1, replica_groups=mesh['row'=4,'col'=8] {'col'}, dimensions={0} | all-to-all | bytes 262144 | tf_op jit(solution)/shard_map/all_to_all | solution.py:595
  168.2 3.8 %finish.1 = (f32[64,512]{1,0:T(8,128)}, f32[64,512]{1,0:T(8,128)}) custom-call(f32[8,32,128]{2,1,0:T(8,128)S(1)} %all_to_all.27.refs_0_, f32[64,64]{1,0:T(8,128)S(1)} %get-tuple-element.64.refs_1_, f32[64,512]{1,0:T(8,128)S(1)} %get-tuple-element.65.refs_2_, f32[64,512]{1,0:T(8,128)S(1)} %get-tuple-element.66.refs_3_, ...), custom_call_target="tpu_custom_call" | custom-call | tf_op jit(solution)/shard_map/finish/pallas_call | solution.py:250
  (96 shorter events, 34.7 us)
Async XLA Ops:
  0.6 46.0 %copy-start = (bf16[64,256,32]{1,2,0:T(8,128)(2,1)S(1)}, bf16[64,256,32]{1,2,0:T(8,128)(2,1)}, u32[]{:S(2)}) copy-start(bf16[64,256,32]{1,2,0:T(8,128)(2,1)} %param.18) | copy-start | bytes 3145732
  4.5 42.2 %copy-start.1 = (bf16[64,256,32]{1,2,0:T(8,128)(2,1)S(1)}, bf16[64,256,32]{1,2,0:T(8,128)(2,1)}, u32[]{:S(2)}) copy-start(bf16[64,256,32]{1,2,0:T(8,128)(2,1)} %param.19) | copy-start | bytes 3145732
  4.5 15.1 %all-to-all-start = ((f32[32,4,256]{2,1,0:T(4,128)}), f32[32,4,256]{2,1,0:T(4,128)S(1)}, u32[]{:S(2)}, u32[]{:S(2)}) async-start(f32[32,4,256]{2,1,0:T(4,128)} %project.1), calls=%async_computation | async-start | bytes 262144 | tf_op jit(solution)/shard_map/all_to_all | solution.py:69
  20.3 10.3 %all-to-all-start.1 = ((f32[32,4,256]{2,1,0:T(4,128)}), f32[32,4,256]{2,1,0:T(4,128)S(1)}, u32[]{:S(2)}, u32[]{:S(2)}) async-start(f32[32,4,256]{2,1,0:T(4,128)} %total.2), calls=%async_computation.1 | async-start | bytes 262144 | tf_op jit(solution)/shard_map/all_to_all | solution.py:71
  22.9 1.2 copy-start.5
  32.5 6.5 %collective-permute-start.2 = (bf16[2,64,256]{2,1,0:T(8,128)(2,1)S(1)}, bf16[2,64,256]{2,1,0:T(8,128)(2,1)S(1)}, u32[]{:S(2)}, u32[]{:S(2)}) collective-permute-start(bf16[2,64,256]{2,1,0:T(8,128)(2,1)S(1)} %get-tuple-element.40), channel_id=1, source_target_pairs={{0,4},{1,5},{2,6},{3,7},{4,0},{5,1},{6,2},{7,3},{8,12},{9,13},{10,... | collective-permute-start | bytes 196616 | tf_op jit(solution)/shard_map/ppermute | solution.py:32
  34.0 5.1 %collective-permute-start = (bf16[2,64,256]{2,1,0:T(8,128)(2,1)S(1)}, bf16[2,64,256]{2,1,0:T(8,128)(2,1)S(1)}, u32[]{:S(2)}, u32[]{:S(2)}) collective-permute-start(bf16[2,64,256]{2,1,0:T(8,128)(2,1)S(1)} %get-tuple-element.40), channel_id=1, source_target_pairs={{0,16},{8,24},{16,0},{24,8},{1,17},{9,25},{17,1},{25,9},{2,18},{10... | collective-permute-start | bytes 196616 | tf_op jit(solution)/shard_map/ppermute | solution.py:32
  39.0 1.4 collective-permute-start.1
  39.1 6.2 %collective-permute-start.3 = (bf16[4,64,256]{2,1,0:T(8,128)(2,1)S(1)}, bf16[4,64,256]{2,1,0:T(8,128)(2,1)S(1)}, u32[]{:S(2)}, u32[]{:S(2)}) collective-permute-start(bf16[4,64,256]{2,1,0:T(8,128)(2,1)S(1)} %get-tuple-element.90), channel_id=1, source_target_pairs={{0,2},{1,3},{2,0},{3,1},{4,6},{5,7},{6,4},{7,5},{8,10},{9,11},{10,... | collective-permute-start | bytes 393224 | tf_op jit(solution)/shard_map/ppermute | solution.py:32
  45.4 9.2 %collective-permute-start.4 = (bf16[8,64,256]{2,1,0:T(8,128)(2,1)S(1)}, bf16[8,64,256]{2,1,0:T(8,128)(2,1)S(1)}, u32[]{:S(2)}, u32[]{:S(2)}) collective-permute-start(bf16[8,64,256]{2,1,0:T(8,128)(2,1)S(1)} %gathered.2.refs_0_), channel_id=1, source_target_pairs={{0,1},{1,0},{2,3},{3,2},{4,5},{5,4},{6,7},{7,6},{8,9},{9,8},{10,11... | collective-permute-start | bytes 786440 | tf_op jit(solution)/shard_map/ppermute | solution.py:32
  49.5 27.2 %copy-start.4 = (f32[512,512]{1,0:T(8,128)S(1)}, f32[512,512]{1,0:T(8,128)}, u32[]{:S(2)}) copy-start(f32[512,512]{1,0:T(8,128)} %copy-done.2) | copy-start | bytes 3145732
  49.6 10.6 %collective-permute-start.6 = (f32[4,64,256]{2,1,0:T(8,128)S(1)}, f32[4,64,256]{2,1,0:T(8,128)S(1)}, u32[]{:S(2)}, u32[]{:S(2)}) collective-permute-start(f32[4,64,256]{2,1,0:T(8,128)S(1)} %get-tuple-element.80), channel_id=1, source_target_pairs={{0,1},{1,0},{2,3},{3,2},{4,5},{5,4},{6,7},{7,6},{8,9},{9,8},{10,11... | collective-permute-start | bytes 786440 | tf_op jit(solution)/shard_map/ppermute | solution.py:32
  50.4 9.7 %collective-permute-start.5 = (f32[4,64,256]{2,1,0:T(8,128)S(1)}, f32[4,64,256]{2,1,0:T(8,128)S(1)}, u32[]{:S(2)}, u32[]{:S(2)}) collective-permute-start(f32[4,64,256]{2,1,0:T(8,128)S(1)} %get-tuple-element.81), channel_id=1, source_target_pairs={{0,2},{1,3},{2,0},{3,1},{4,6},{5,7},{6,4},{7,5},{8,10},{9,11},{10,... | collective-permute-start | bytes 786440 | tf_op jit(solution)/shard_map/ppermute | solution.py:32
  60.2 5.6 %collective-permute-start.8 = (f32[2,64,256]{2,1,0:T(8,128)S(1)}, f32[2,64,256]{2,1,0:T(8,128)S(1)}, u32[]{:S(2)}, u32[]{:S(2)}) collective-permute-start(f32[2,64,256]{2,1,0:T(8,128)S(1)} %get-tuple-element.46), channel_id=1, source_target_pairs={{0,2},{1,3},{2,0},{3,1},{4,6},{5,7},{6,4},{7,5},{8,10},{9,11},{10,... | collective-permute-start | bytes 393224 | tf_op jit(solution)/shard_map/ppermute | solution.py:32
  61.7 5.2 %collective-permute-start.7 = (f32[2,64,256]{2,1,0:T(8,128)S(1)}, f32[2,64,256]{2,1,0:T(8,128)S(1)}, u32[]{:S(2)}, u32[]{:S(2)}) collective-permute-start(f32[2,64,256]{2,1,0:T(8,128)S(1)} %get-tuple-element.43.refs_0_), channel_id=1, source_target_pairs={{0,1},{1,0},{2,3},{3,2},{4,5},{5,4},{6,7},{7,6},{8,9},{9,8},{10,11... | collective-permute-start | bytes 393224 | tf_op jit(solution)/shard_map/ppermute | solution.py:32
  67.0 1.6 collective-permute-start.10
  67.1 9.6 %collective-permute-start.9 = (f32[2,64,256]{2,1,0:T(8,128)S(1)}, f32[2,64,256]{2,1,0:T(8,128)S(1)}, u32[]{:S(2)}, u32[]{:S(2)}) collective-permute-start(f32[2,64,256]{2,1,0:T(8,128)S(1)} %get-tuple-element.48), channel_id=1, source_target_pairs={{0,4},{1,5},{2,6},{3,7},{4,0},{5,1},{6,2},{7,3},{8,12},{9,13},{10,... | collective-permute-start | bytes 393224 | tf_op jit(solution)/shard_map/ppermute | solution.py:32
  68.7 8.0 %collective-permute-start.11 = (f32[2,64,256]{2,1,0:T(8,128)S(1)}, f32[2,64,256]{2,1,0:T(8,128)S(1)}, u32[]{:S(2)}, u32[]{:S(2)}) collective-permute-start(f32[2,64,256]{2,1,0:T(8,128)S(1)} %get-tuple-element.86), channel_id=1, source_target_pairs={{0,16},{8,24},{16,0},{24,8},{1,17},{9,25},{17,1},{25,9},{2,18},{10... | collective-permute-start | bytes 393224 | tf_op jit(solution)/shard_map/ppermute | solution.py:32
  106.5 6.6 %collective-permute-start.14 = (bf16[2,64,256]{2,1,0:T(8,128)(2,1)S(1)}, bf16[2,64,256]{2,1,0:T(8,128)(2,1)S(1)}, u32[]{:S(2)}, u32[]{:S(2)}) collective-permute-start(bf16[2,64,256]{2,1,0:T(8,128)(2,1)S(1)} %get-tuple-element.54), channel_id=1, source_target_pairs={{0,4},{1,5},{2,6},{3,7},{4,0},{5,1},{6,2},{7,3},{8,12},{9,13},{10,... | collective-permute-start | bytes 196616 | tf_op jit(solution)/shard_map/ppermute | solution.py:32
  108.1 5.0 %collective-permute-start.12 = (bf16[2,64,256]{2,1,0:T(8,128)(2,1)S(1)}, bf16[2,64,256]{2,1,0:T(8,128)(2,1)S(1)}, u32[]{:S(2)}, u32[]{:S(2)}) collective-permute-start(bf16[2,64,256]{2,1,0:T(8,128)(2,1)S(1)} %get-tuple-element.54), channel_id=1, source_target_pairs={{0,16},{8,24},{16,0},{24,8},{1,17},{9,25},{17,1},{25,9},{2,18},{10... | collective-permute-start | bytes 196616 | tf_op jit(solution)/shard_map/ppermute | solution.py:32
  113.2 1.4 collective-permute-start.13
  113.3 5.9 %collective-permute-start.15 = (bf16[4,64,256]{2,1,0:T(8,128)(2,1)S(1)}, bf16[4,64,256]{2,1,0:T(8,128)(2,1)S(1)}, u32[]{:S(2)}, u32[]{:S(2)}) collective-permute-start(bf16[4,64,256]{2,1,0:T(8,128)(2,1)S(1)} %get-tuple-element.88), channel_id=1, source_target_pairs={{0,2},{1,3},{2,0},{3,1},{4,6},{5,7},{6,4},{7,5},{8,10},{9,11},{10,... | collective-permute-start | bytes 393224 | tf_op jit(solution)/shard_map/ppermute | solution.py:32
  122.1 9.2 %collective-permute-start.16 = (bf16[8,64,256]{2,1,0:T(8,128)(2,1)S(1)}, bf16[8,64,256]{2,1,0:T(8,128)(2,1)S(1)}, u32[]{:S(2)}, u32[]{:S(2)}) collective-permute-start(bf16[8,64,256]{2,1,0:T(8,128)(2,1)S(1)} %gathered.3.refs_0_), channel_id=1, source_target_pairs={{0,1},{1,0},{2,3},{3,2},{4,5},{5,4},{6,7},{7,6},{8,9},{9,8},{10,11... | collective-permute-start | bytes 786440 | tf_op jit(solution)/shard_map/ppermute | solution.py:32
  123.6 13.1 %collective-permute-start.18 = (f32[4,64,256]{2,1,0:T(8,128)S(1)}, f32[4,64,256]{2,1,0:T(8,128)S(1)}, u32[]{:S(2)}, u32[]{:S(2)}) collective-permute-start(f32[4,64,256]{2,1,0:T(8,128)S(1)} %get-tuple-element.76), channel_id=1, source_target_pairs={{0,1},{1,0},{2,3},{3,2},{4,5},{5,4},{6,7},{7,6},{8,9},{9,8},{10,11... | collective-permute-start | bytes 786440 | tf_op jit(solution)/shard_map/ppermute | solution.py:32
  124.3 12.4 %collective-permute-start.17 = (f32[4,64,256]{2,1,0:T(8,128)S(1)}, f32[4,64,256]{2,1,0:T(8,128)S(1)}, u32[]{:S(2)}, u32[]{:S(2)}) collective-permute-start(f32[4,64,256]{2,1,0:T(8,128)S(1)} %get-tuple-element.77), channel_id=1, source_target_pairs={{0,2},{1,3},{2,0},{3,1},{4,6},{5,7},{6,4},{7,5},{8,10},{9,11},{10,... | collective-permute-start | bytes 786440 | tf_op jit(solution)/shard_map/ppermute | solution.py:32
  136.8 5.3 %collective-permute-start.20 = (f32[2,64,256]{2,1,0:T(8,128)S(1)}, f32[2,64,256]{2,1,0:T(8,128)S(1)}, u32[]{:S(2)}, u32[]{:S(2)}) collective-permute-start(f32[2,64,256]{2,1,0:T(8,128)S(1)} %get-tuple-element.58), channel_id=1, source_target_pairs={{0,2},{1,3},{2,0},{3,1},{4,6},{5,7},{6,4},{7,5},{8,10},{9,11},{10,... | collective-permute-start | bytes 393224 | tf_op jit(solution)/shard_map/ppermute | solution.py:32
  136.9 5.3 %collective-permute-start.19 = (f32[2,64,256]{2,1,0:T(8,128)S(1)}, f32[2,64,256]{2,1,0:T(8,128)S(1)}, u32[]{:S(2)}, u32[]{:S(2)}) collective-permute-start(f32[2,64,256]{2,1,0:T(8,128)S(1)} %get-tuple-element.55.refs_0_), channel_id=1, source_target_pairs={{0,1},{1,0},{2,3},{3,2},{4,5},{5,4},{6,7},{7,6},{8,9},{9,8},{10,11... | collective-permute-start | bytes 393224 | tf_op jit(solution)/shard_map/ppermute | solution.py:32
  142.3 2.4 %collective-permute-start.22 = (f32[4,64,256]{2,1,0:T(8,128)S(1)}, f32[4,64,256]{2,1,0:T(8,128)S(1)}, u32[]{:S(2)}, u32[]{:S(2)}) collective-permute-start(f32[4,64,256]{2,1,0:T(8,128)S(1)} %get-tuple-element.62), channel_id=1, source_target_pairs={{0,8},{8,0},{16,24},{24,16},{1,9},{9,1},{17,25},{25,17},{2,10},{10... | collective-permute-start | bytes 786440 | tf_op jit(solution)/shard_map/ppermute | solution.py:32
  142.3 9.6 %collective-permute-start.21 = (f32[2,64,256]{2,1,0:T(8,128)S(1)}, f32[2,64,256]{2,1,0:T(8,128)S(1)}, u32[]{:S(2)}, u32[]{:S(2)}) collective-permute-start(f32[2,64,256]{2,1,0:T(8,128)S(1)} %get-tuple-element.60), channel_id=1, source_target_pairs={{0,4},{1,5},{2,6},{3,7},{4,0},{5,1},{6,2},{7,3},{8,12},{9,13},{10,... | collective-permute-start | bytes 393224 | tf_op jit(solution)/shard_map/ppermute | solution.py:32
  144.7 7.2 %collective-permute-start.23 = (f32[2,64,256]{2,1,0:T(8,128)S(1)}, f32[2,64,256]{2,1,0:T(8,128)S(1)}, u32[]{:S(2)}, u32[]{:S(2)}) collective-permute-start(f32[2,64,256]{2,1,0:T(8,128)S(1)} %get-tuple-element.84), channel_id=1, source_target_pairs={{0,16},{8,24},{16,0},{24,8},{1,17},{9,25},{17,1},{25,9},{2,18},{10... | collective-permute-start | bytes 393224 | tf_op jit(solution)/shard_map/ppermute | solution.py:32
  152.3 1.2 collective-permute-start.24
  153.5 3.7 %collective-permute-start.25 = (f32[32,128]{1,0:T(8,128)S(1)}, f32[32,128]{1,0:T(8,128)S(1)}, u32[]{:S(2)}, u32[]{:S(2)}) collective-permute-start(f32[32,128]{1,0:T(8,128)S(1)} %add.140), channel_id=1, source_target_pairs={{0,16},{8,24},{16,0},{24,8},{1,17},{9,25},{17,1},{25,9},{2,18},{10... | collective-permute-start | bytes 49160 | tf_op jit(solution)/shard_map/ppermute | solution.py:32
  (5 other events, 4.5 us)

commit v4 on v3

--- a/solution.py
+++ b/solution.py
@@ -1,5 +1,3 @@
-import functools
-
 import jax
 import jax.numpy as jnp
 from jax import lax
@@ -14,7 +12,6 @@
 VMEM_LIMIT = 18 * 2**20
 PROJECT_LIMIT = 62 * 2**20
 STREAM_LIMIT = 36 * 2**20
-GROUP = 8
 
 
 def exact(left, right, dims):
@@ -119,19 +116,14 @@
 
 
 def near_products(
-    forward, v, tiles, count, src, dst, part=(0, 1), out_blocks=None, start=None, stream=False, after=(),
-    far=(),
+    forward, v, tiles, count, src, dst, part=(0, 1), out_blocks=None, start=None, stream=False, after=()
 ):
     slots, width, _ = tiles.shape
     rhs = v.shape[1]
     chunk = 32
 
     def body(*refs):
-        far_refs, refs = refs[len(after) : len(after) + len(far)], refs[len(after) + len(far) :]
-        near_kernel(forward, chunk, stream, part, *refs)
-        if far:
-            src, dst, inner, outer = far_refs
-            add_far(GROUP, src, dst, refs[3], inner, outer, refs[-1])
+        near_kernel(forward, chunk, stream, part, *refs[len(after) :])
 
     extra = [] if start is None else [start]
     total = jax.ShapeDtypeStruct((out_blocks, rhs, width) if start is None else start.shape, F32)
@@ -142,7 +134,6 @@
         body,
         out_shape=[total, jax.ShapeDtypeStruct(tiles.shape, tiles.dtype)] if stream else [total],
         in_specs=[pl.BlockSpec(memory_space=pl.ANY)] * len(after)
-        + ([smem] * 2 + [vmem] * 2 if far else [])
         + [smem] * 3
         + [vmem]
         + [hbm if stream else vmem]
@@ -156,11 +147,16 @@
             transcendentals=0,
         ),
         name="near_forward" if forward else "near_transposed",
-    )(*after, *far, count, src, dst, v, tiles, *extra)
-
-
-def add_far(group, src_ref, dst_ref, v_ref, inner_ref, outer_ref, out_ref):
+    )(*after, count, src, dst, v, tiles, *extra)
+
+
+def far_kernel(group, src_ref, dst_ref, v_ref, inner_ref, outer_ref, *refs):
     rhs = v_ref.shape[1]
+    out_ref = refs[-1]
+    if len(refs) == 2:
+        out_ref[...] = refs[0][...]
+    else:
+        out_ref[...] = jnp.zeros_like(out_ref)
     panels = src_ref.shape[0]
     prank = inner_ref.shape[0] // panels
     shape = (group * rhs, group * prank)
@@ -177,28 +173,32 @@
             out_ref[dst_ref[start + g]] += prod[g * rhs : (g + 1) * rhs]
 
 
-def far_kernel(group, src_ref, dst_ref, v_ref, inner_ref, outer_ref, out_ref):
-    out_ref[...] = jnp.zeros_like(out_ref)
-    add_far(group, src_ref, dst_ref, v_ref, inner_ref, outer_ref, out_ref)
-
-
-def far_products(v, src, dst, inner, outer, out_blocks):
+def far_products(forward, v, src, dst, inner, outer, out_blocks=None, start=None, after=()):
+    panels = src.shape[0]
     _, rhs, width = v.shape
     smem = pl.BlockSpec(memory_space=pltpu.SMEM)
     vmem = pl.BlockSpec(memory_space=pltpu.VMEM)
+    extra = [] if start is None else [start]
+    total = (out_blocks, rhs, width) if start is None else start.shape
+
+    def body(*refs):
+        far_kernel(8, *refs[len(after) :])
+
     return pl.pallas_call(
-        functools.partial(far_kernel, GROUP),
-        out_shape=jax.ShapeDtypeStruct((out_blocks, rhs, width), F32),
-        in_specs=[smem] * 2 + [vmem] * 3,
+        body,
+        out_shape=jax.ShapeDtypeStruct(total, F32),
+        in_specs=[pl.BlockSpec(memory_space=pl.ANY)] * len(after)
+        + [smem] * 2
+        + [vmem] * (3 + len(extra)),
         out_specs=vmem,
         compiler_params=pltpu.CompilerParams(vmem_limit_bytes=VMEM_LIMIT),
         cost_estimate=pl.CostEstimate(
-            flops=4 * rhs * width * inner.shape[0],
+            flops=2 * panels * rhs * width * inner.shape[0] // panels,
             bytes_accessed=2 * inner.size,
             transcendentals=0,
         ),
-        name="far_transposed",
-    )(src, dst, v, inner, outer)
+        name="far_forward" if forward else "far_transposed",
+    )(*after, src, dst, v, inner, outer, *extra)
 
 
 def eliminate(systems, block=8):
@@ -523,10 +523,12 @@
             copy_kernel, [(row_side.shape, BF16)], "gathered", [row_side], [forward]
         )
         (forward,) = near_products(
-            True, col_side, held, *near, part=(1, 2), start=forward, after=[row_side],
-            far=(far_col_src, far_row_dst, right, left),
+            True, col_side, held, *near, part=(1, 2), start=forward, after=[row_side]
         )
         other_side = swap(row_side, "col", gather_col[-1])
+        forward = far_products(
+            True, col_side, far_col_src, far_row_dst, right, left, start=forward
+        )
         row_side = jnp.concatenate([row_side, other_side], axis=0)
 
         half = n_col // 2
@@ -534,7 +536,7 @@
         paths = [path_a if b % 2 == 0 else path_b for b in range(blocks)]
         got = [swap(sends[b], "col", paths[b][0]) for b in range(blocks)]
         transposed = far_products(
-            row_side, far_row_src, far_col_dst, left, right, n_row * blocks
+            False, row_side, far_row_src, far_col_dst, left, right, out_blocks=n_row * blocks
         )
         own = [forward[b * n_col : b * n_col + half] for b in range(blocks)]
         for step in range(1, len(col_masks) - 1):

time: 173 us -> 171 us (0.988)
  waiting for transfers between devices: 59.2 us -> 52.2 us
  starting transfers between devices: 29.4 us -> 34.2 us
  local copies, waits for them, and re-layouts: 7.27 us -> 5 us
    ppermute x26, waiting for transfers between devices: 50.6 us -> 42.5 us  [swap(): return lax.ppermute(value, axis, pairs)]
    ppermute x26, starting transfers between devices: 19.5 us -> 24.3 us  [swap(): return lax.ppermute(value, axis, pairs)]
    pallas_call x2 -> x4, Pallas kernels: 4.18 us -> 8.36 us  [far_products(): pl.pallas_call(body, out_shape=jax.ShapeDtypeStruct(total, F32), in_specs...]
    pallas_call x6, Pallas kernels: 17.3 us -> 14.3 us  [near_products(): pl.pallas_call(body, out_shape=[total, jax.ShapeDtypeStruct(tiles.shape,...]
    unnamed x22 -> x16, local copies, waits for them, and re-layouts: 5.77 us -> 3.52 us
  transfers between devices with their start and end apart: 28 -> 28, of which waited for: 20 -> 19; matrix products, arithmetic and copies ran while one was open for 3% -> 3% of each run, Pallas kernels for 11% -> 13%
where the time goes in v4:
time: 171 us; the launch traced here: 170 us
  waiting for transfers between devices  52.2 us (31%)
  Pallas kernels  39.9 us (23%)
  blocking collectives  34.9 us (20%)
  starting transfers between devices  34.2 us (20%)
  local copies, waits for them, and re-layouts  5 us (3%)
  other arithmetic  2.97 us (2%)
    ppermute x26, waiting for transfers between devices, swap(): return lax.ppermute(value, axis, pairs)  42.5 us
    ppermute x26, starting transfers between devices, swap(): return lax.ppermute(value, axis, pairs)  24.3 us
    pallas_call x6, Pallas kernels, near_products(): pl.pallas_call(body, out_shape=[total, jax.ShapeDtypeStruct(tiles.shape,...  14.3 us
    pallas_call x13, Pallas kernels, call(): pl.pallas_call(body, out_shape=[jax.ShapeDtypeStruct(shape, dtype) for sh...  13.3 us
    all_to_all x1, blocking collectives, local(): lax.all_to_all(jnp.broadcast_to(partial, (n_col, *partial.shape)), 'col',...  11.8 us
    all_to_all x1, blocking collectives, spread_sum(): got = lax.all_to_all(pieces, axes, 0, 0, tiled=True)  11.8 us
    all_to_all x1, blocking collectives, spread_sum(): return lax.all_to_all(same, axes, 0, 0, tiled=True)  11.4 us
    pallas_call x4, Pallas kernels, far_products(): pl.pallas_call(body, out_shape=jax.ShapeDtypeStruct(total, F32), in_specs...  8.36 us
  transfers between devices with their start and end apart: 28, of which 19 were waited for; matrix products, arithmetic and copies ran while one was open for 3% of the time, Pallas kernels for 13%

profile of v4, /device:TPU:0, one launch (start us, length us, event | category | flops | bytes accessed | tf_op | source)
XLA Modules:
  0.0 170.2 jit_solution(8713081699751846260)
XLA Ops:
  0.6 3.8 %project.1 = f32[32,4,256]{2,1,0:T(4,128)} custom-call(f32[64,512]{1,0:T(8,128)} %rhs_hbm.1, f32[512,512]{1,0:T(8,128)} %factor_hbm.1), custom_call_target="tpu_custom_call" | custom-call | tf_op jit(solution)/shard_map/project/pallas_call | solution.py:288
  4.4 7.3 %all-to-all-start = ((f32[32,4,256]{2,1,0:T(4,128)}), f32[32,4,256]{2,1,0:T(4,128)S(1)}, u32[]{:S(2)}, u32[]{:S(2)}) async-start(f32[32,4,256]{2,1,0:T(4,128)} %project.1), calls=%async_computation | async-start | bytes 262144 | tf_op jit(solution)/shard_map/all_to_all | solution.py:66
  13.1 6.4 %all-to-all-done.refs_0_ = f32[32,4,256]{2,1,0:T(4,128)S(1)} async-done(((f32[32,4,256]{2,1,0:T(4,128)}), f32[32,4,256]{2,1,0:T(4,128)S(1)}, u32[]{:S(2)}, u32[]{:S(2)}) %all-to-all-start) | async-done | bytes 131104 | tf_op jit(solution)/shard_map/all_to_all | solution.py:66
  20.2 2.6 %all-to-all-start.1 = ((f32[32,4,256]{2,1,0:T(4,128)}), f32[32,4,256]{2,1,0:T(4,128)S(1)}, u32[]{:S(2)}, u32[]{:S(2)}) async-start(f32[32,4,256]{2,1,0:T(4,128)} %total.2), calls=%async_computation.1 | async-start | bytes 262144 | tf_op jit(solution)/shard_map/all_to_all | solution.py:68
  27.2 3.3 %all-to-all-done.1.refs_3_.refs_4_ = f32[32,4,256]{2,1,0:T(4,128)S(1)} async-done(((f32[32,4,256]{2,1,0:T(4,128)}), f32[32,4,256]{2,1,0:T(4,128)S(1)}, u32[]{:S(2)}, u32[]{:S(2)}) %all-to-all-start.1) | async-done | bytes 131104 | tf_op jit(solution)/shard_map/all_to_all | solution.py:68
  35.1 2.6 %collective-permute-done.2 = bf16[2,64,256]{2,1,0:T(8,128)(2,1)S(1)} collective-permute-done((bf16[2,64,256]{2,1,0:T(8,128)(2,1)S(1)}, bf16[2,64,256]{2,1,0:T(8,128)(2,1)S(1)}, u32[]{:S(2)}, u32[]{:S(2)}) %collective-permute-start.2) | collective-permute-done | bytes 65568 | tf_op jit(solution)/shard_map/ppermute | solution.py:29
  39.2 5.0 %near_forward.4 = (f32[16,64,256]{2,1,0:T(8,128)S(1)}, bf16[128,256,256]{2,1,0:T(8,128)(2,1)S(1)}) custom-call(s32[1]{0:T(128)} %dynamic_slice.3.refs_0_.refs_1_, s32[128]{0:T(128)S(1)} %get-tuple-element.92.refs_1_.refs_2_.refs_3_, s32[128]{0:T(128)S(1)} %get-tuple-element.93.refs_2_.refs_3_, ...), custom_call_target="tpu_custom_call" | custom-call | flops 2147483648 | bytes 16777216 | tf_op jit(solution)/shard_map/near_forward/pallas_call | solution.py:133
  44.2 2.7 %collective-permute-start.4 = (bf16[8,64,256]{2,1,0:T(8,128)(2,1)S(1)}, bf16[8,64,256]{2,1,0:T(8,128)(2,1)S(1)}, u32[]{:S(2)}, u32[]{:S(2)}) collective-permute-start(bf16[8,64,256]{2,1,0:T(8,128)(2,1)S(1)} %gathered.2.refs_0_), channel_id=1, source_target_pairs={{0,1},{1,0},{2,3},{3,2},{4,5},{5,4},{6,7},{7,6},{8,9},{9,8},{10,11... | collective-permute-start | bytes 786440 | tf_op jit(solution)/shard_map/ppermute | solution.py:29
  48.2 2.1 %far_forward.2 = f32[16,64,256]{2,1,0:T(8,128)S(1)} custom-call(s32[64]{0:T(128)S(1)} %fusion.refs_1_.refs_0_, s32[64]{0:T(128)S(1)} %get-tuple-element.72.refs_1_, bf16[8,64,256]{2,1,0:T(8,128)(2,1)S(1)} %constant_dynamic-update-slice_fusion.refs_3_.refs_4_.refs_2_, bf16[2048,256]{1,0:T(8,128)(2,1)S(1)} %bitcast.12, bf16[2048,256]{1,0:T(8,128)(2,1)S(1)} %bitcast.8, ...), custom_call_target="tpu_custom_call" | custom-call | flops 67108864 | bytes 1048576 | tf_op jit(solution)/shard_map/far_forward/pallas_call | solution.py:187
  52.0 2.0 %collective-permute-done.4 = bf16[8,64,256]{2,1,0:T(8,128)(2,1)S(1)} collective-permute-done((bf16[8,64,256]{2,1,0:T(8,128)(2,1)S(1)}, bf16[8,64,256]{2,1,0:T(8,128)(2,1)S(1)}, u32[]{:S(2)}, u32[]{:S(2)}) %collective-permute-start.4) | collective-permute-done | bytes 262176 | tf_op jit(solution)/shard_map/ppermute | solution.py:29
  54.1 2.1 %far_transposed.2.refs_0_.refs_6_ = f32[8,64,256]{2,1,0:T(8,128)S(1)} custom-call(s32[64]{0:T(128)S(1)} %multiply_add_fusion.3.refs_0_, s32[64]{0:T(128)S(1)} %fusion.refs_1_.refs_0_, bf16[16,64,256]{2,1,0:T(8,128)(2,1)S(1)} %pad_maximum_fusion.refs_2_.refs_4_, bf16[2048,256]{1,0:T(8,128)(2,1)S(1)} %bitcast.9, bf16[2048,256]{1,0:T(8,128)(2,1)S(1)} %bitcast.13), custom_call_target="tpu_custom_call" | custom-call | flops 67108864 | bytes 1048576 | tf_op jit(solution)/shard_map/far_transposed/pallas_call | solution.py:187
  56.2 3.4 %collective-permute-done.6.refs_4_ = f32[4,64,256]{2,1,0:T(8,128)S(1)} collective-permute-done((f32[4,64,256]{2,1,0:T(8,128)S(1)}, f32[4,64,256]{2,1,0:T(8,128)S(1)}, u32[]{:S(2)}, u32[]{:S(2)}) %collective-permute-start.6) | collective-permute-done | bytes 262176 | tf_op jit(solution)/shard_map/ppermute | solution.py:29
  60.4 2.1 %near_transposed.2.refs_0_ = f32[8,64,256]{2,1,0:T(8,128)S(1)} custom-call(f32[2,64,256]{2,1,0:T(8,128)S(1)} %get-tuple-element.43.refs_0_, s32[1]{0:T(128)} %dynamic_slice.3.refs_0_.refs_1_, s32[128]{0:T(128)S(1)} %get-tuple-element.68.refs_2_, s32[128]{0:T(128)S(1)} %get-tuple-element.92.refs_1_.refs_2_.refs_3_, ...), custom_call_target="tpu_custom_call" | custom-call | flops 2147483648 | bytes 16777216 | tf_op jit(solution)/shard_map/near_transposed/pallas_call | solution.py:133
  62.5 2.8 %collective-permute-done.8.refs_4_ = f32[2,64,256]{2,1,0:T(8,128)S(1)} collective-permute-done((f32[2,64,256]{2,1,0:T(8,128)S(1)}, f32[2,64,256]{2,1,0:T(8,128)S(1)}, u32[]{:S(2)}, u32[]{:S(2)}) %collective-permute-start.8) | collective-permute-done | bytes 131104 | tf_op jit(solution)/shard_map/ppermute | solution.py:29
  65.5 2.4 %collective-permute-start.9 = (f32[2,64,256]{2,1,0:T(8,128)S(1)}, f32[2,64,256]{2,1,0:T(8,128)S(1)}, u32[]{:S(2)}, u32[]{:S(2)}) collective-permute-start(f32[2,64,256]{2,1,0:T(8,128)S(1)} %get-tuple-element.48), channel_id=1, source_target_pairs={{0,4},{1,5},{2,6},{3,7},{4,0},{5,1},{6,2},{7,3},{8,12},{9,13},{10,... | collective-permute-start | bytes 393224 | tf_op jit(solution)/shard_map/ppermute | solution.py:29
  68.8 6.4 %collective-permute-done.9.refs_5_ = f32[2,64,256]{2,1,0:T(8,128)S(1)} collective-permute-done((f32[2,64,256]{2,1,0:T(8,128)S(1)}, f32[2,64,256]{2,1,0:T(8,128)S(1)}, u32[]{:S(2)}, u32[]{:S(2)}) %collective-permute-start.9) | collective-permute-done | bytes 131104 | tf_op jit(solution)/shard_map/ppermute | solution.py:29
  76.7 11.8 %all_to_all.25.refs_0_ = f32[32,4,384]{2,1,0:T(4,128)S(1)} all-to-all(f32[32,4,384]{2,1,0:T(4,128)S(1)} %get-tuple-element.51), channel_id=1, replica_groups=mesh['row'=4,'col'=8] {'row','col'}, dimensions={0} | all-to-all | bytes 393216 | tf_op jit(solution)/shard_map/all_to_all | solution.py:66
  88.5 11.4 %all_to_all.26.refs_3_ = f32[32,4,384]{2,1,0:T(4,128)S(1)} all-to-all(f32[32,4,384]{2,1,0:T(4,128)S(1)} %total.3), channel_id=1, replica_groups=mesh['row'=4,'col'=8] {'row','col'}, dimensions={0} | all-to-all | bytes 393216 | tf_op jit(solution)/shard_map/all_to_all | solution.py:68
  99.9 5.8 %advance.1 = (f32[64,512]{1,0:T(8,128)S(1)}, f32[64,512]{1,0:T(8,128)S(1)}, f32[64,512]{1,0:T(8,128)S(1)}, bf16[2,64,256]{2,1,0:T(8,128)(2,1)S(1)}, f32[64,64]{1,0:T(8,128)S(1)}) custom-call(f32[1,512]{1,0:T(1,128)S(1)} %get-tuple-element.36.refs_1_.refs_0_, f32[512,512]{1,0:T(8,128)S(1)} %get-tuple-element.37.refs_2_.refs_1_, ...), custom_call_target="tpu_custom_call" | custom-call | tf_op jit(solution)/shard_map/advance/pallas_call | solution.py:250
  107.9 4.5 %collective-permute-done.14 = bf16[2,64,256]{2,1,0:T(8,128)(2,1)S(1)} collective-permute-done((bf16[2,64,256]{2,1,0:T(8,128)(2,1)S(1)}, bf16[2,64,256]{2,1,0:T(8,128)(2,1)S(1)}, u32[]{:S(2)}, u32[]{:S(2)}) %collective-permute-start.14) | collective-permute-done | bytes 65568 | tf_op jit(solution)/shard_map/ppermute | solution.py:29
  113.8 2.7 %near_forward.6.refs_0_.refs_6_ = f32[16,64,256]{2,1,0:T(8,128)S(1)} custom-call(s32[1]{0:T(128)} %dynamic_slice.3.refs_0_.refs_1_, s32[128]{0:T(128)S(1)} %get-tuple-element.92.refs_1_.refs_2_.refs_3_, s32[128]{0:T(128)S(1)} %get-tuple-element.93.refs_2_.refs_3_, bf16[8,64,256]{2,1,0:T(8,128)(2,1)S(1)} %constant_dynamic-update-slice_fusion.3.refs_3_.refs_4_.refs_2_, ...), custom_call_target="tpu_custom_call" | custom-call | flops 2147483648 | bytes 16777216 | tf_op jit(solution)/shard_map/near_forward/pallas_call | solution.py:133
  116.5 1.9 %collective-permute-done.15 = bf16[4,64,256]{2,1,0:T(8,128)(2,1)S(1)} collective-permute-done((bf16[4,64,256]{2,1,0:T(8,128)(2,1)S(1)}, bf16[4,64,256]{2,1,0:T(8,128)(2,1)S(1)}, u32[]{:S(2)}, u32[]{:S(2)}) %collective-permute-start.15) | collective-permute-done | bytes 131104 | tf_op jit(solution)/shard_map/ppermute | solution.py:29
  121.1 2.1 %far_forward.3 = f32[16,64,256]{2,1,0:T(8,128)S(1)} custom-call(s32[64]{0:T(128)S(1)} %fusion.refs_1_.refs_0_, s32[64]{0:T(128)S(1)} %get-tuple-element.72.refs_1_, bf16[8,64,256]{2,1,0:T(8,128)(2,1)S(1)} %constant_dynamic-update-slice_fusion.3.refs_3_.refs_4_.refs_2_, bf16[2048,256]{1,0:T(8,128)(2,1)S(1)} %bitcast.14, bf16[2048,256]{1,0:T(8,128)(2,1)S(1)} %bitcast.10, ...), custom_call_target="tpu_custom_call" | custom-call | flops 67108864 | bytes 1048576 | tf_op jit(solution)/shard_map/far_forward/pallas_call | solution.py:187
  124.4 4.6 %collective-permute-done.16 = bf16[8,64,256]{2,1,0:T(8,128)(2,1)S(1)} collective-permute-done((bf16[8,64,256]{2,1,0:T(8,128)(2,1)S(1)}, bf16[8,64,256]{2,1,0:T(8,128)(2,1)S(1)}, u32[]{:S(2)}, u32[]{:S(2)}) %collective-permute-start.16) | collective-permute-done | bytes 262176 | tf_op jit(solution)/shard_map/ppermute | solution.py:29
  129.0 2.1 %far_transposed.3.refs_0_.refs_6_ = f32[8,64,256]{2,1,0:T(8,128)S(1)} custom-call(s32[64]{0:T(128)S(1)} %multiply_add_fusion.3.refs_0_, s32[64]{0:T(128)S(1)} %fusion.refs_1_.refs_0_, bf16[16,64,256]{2,1,0:T(8,128)(2,1)S(1)} %pad_maximum_fusion.1.refs_2_.refs_4_, bf16[2048,256]{1,0:T(8,128)(2,1)S(1)} %bitcast.11, bf16[2048,256]{1,0:T(8,128)(2,1)S(1)} %bitcast.15), custom_call_target="tpu_custom_call" | custom-call | flops 67108864 | bytes 1048576 | tf_op jit(solution)/shard_map/far_transposed/pallas_call | solution.py:187
  131.1 2.1 %collective-permute-done.18.refs_4_ = f32[4,64,256]{2,1,0:T(8,128)S(1)} collective-permute-done((f32[4,64,256]{2,1,0:T(8,128)S(1)}, f32[4,64,256]{2,1,0:T(8,128)S(1)}, u32[]{:S(2)}, u32[]{:S(2)}) %collective-permute-start.18) | collective-permute-done | bytes 262176 | tf_op jit(solution)/shard_map/ppermute | solution.py:29
  135.1 2.1 %near_transposed.3.refs_0_ = f32[8,64,256]{2,1,0:T(8,128)S(1)} custom-call(f32[2,64,256]{2,1,0:T(8,128)S(1)} %get-tuple-element.55.refs_0_, s32[1]{0:T(128)} %dynamic_slice.3.refs_0_.refs_1_, s32[128]{0:T(128)S(1)} %get-tuple-element.68.refs_2_, s32[128]{0:T(128)S(1)} %get-tuple-element.92.refs_1_.refs_2_.refs_3_, ...), custom_call_target="tpu_custom_call" | custom-call | flops 2147483648 | bytes 16777216 | tf_op jit(solution)/shard_map/near_transposed/pallas_call | solution.py:133
  138.8 3.1 %collective-permute-start.21 = (f32[2,64,256]{2,1,0:T(8,128)S(1)}, f32[2,64,256]{2,1,0:T(8,128)S(1)}, u32[]{:S(2)}, u32[]{:S(2)}) collective-permute-start(f32[2,64,256]{2,1,0:T(8,128)S(1)} %get-tuple-element.60), channel_id=1, source_target_pairs={{0,4},{1,5},{2,6},{3,7},{4,0},{5,1},{6,2},{7,3},{8,12},{9,13},{10,... | collective-permute-start | bytes 393224 | tf_op jit(solution)/shard_map/ppermute | solution.py:29
  143.4 5.4 %collective-permute-done.21.refs_3_ = f32[2,64,256]{2,1,0:T(8,128)S(1)} collective-permute-done((f32[2,64,256]{2,1,0:T(8,128)S(1)}, f32[2,64,256]{2,1,0:T(8,128)S(1)}, u32[]{:S(2)}, u32[]{:S(2)}) %collective-permute-start.21) | collective-permute-done | bytes 131104 | tf_op jit(solution)/shard_map/ppermute | solution.py:29
  150.4 2.5 %collective-permute-start.25 = (f32[32,128]{1,0:T(8,128)S(1)}, f32[32,128]{1,0:T(8,128)S(1)}, u32[]{:S(2)}, u32[]{:S(2)}) collective-permute-start(f32[32,128]{1,0:T(8,128)S(1)} %add.140), channel_id=1, source_target_pairs={{0,16},{8,24},{16,0},{24,8},{1,17},{9,25},{17,1},{25,9},{2,18},{10... | collective-permute-start | bytes 49160 | tf_op jit(solution)/shard_map/ppermute | solution.py:29
  154.7 11.8 %all_to_all.27.refs_0_ = f32[8,32,128]{2,1,0:T(8,128)S(1)} all-to-all(f32[8,32,128]{2,1,0:T(8,128)S(1)} %broadcast_in_dim.3), channel_id=1, replica_groups=mesh['row'=4,'col'=8] {'col'}, dimensions={0} | all-to-all | bytes 262144 | tf_op jit(solution)/shard_map/all_to_all | solution.py:597
  166.4 3.8 %finish.1 = (f32[64,512]{1,0:T(8,128)}, f32[64,512]{1,0:T(8,128)}) custom-call(f32[8,32,128]{2,1,0:T(8,128)S(1)} %all_to_all.27.refs_0_, f32[64,64]{1,0:T(8,128)S(1)} %get-tuple-element.64.refs_1_, f32[64,512]{1,0:T(8,128)S(1)} %get-tuple-element.65.refs_2_, f32[64,512]{1,0:T(8,128)S(1)} %get-tuple-element.66.refs_3_, ...), custom_call_target="tpu_custom_call" | custom-call | tf_op jit(solution)/shard_map/finish/pallas_call | solution.py:250
  (92 shorter events, 34.6 us)
Async XLA Ops:
  4.4 15.1 %all-to-all-start = ((f32[32,4,256]{2,1,0:T(4,128)}), f32[32,4,256]{2,1,0:T(4,128)S(1)}, u32[]{:S(2)}, u32[]{:S(2)}) async-start(f32[32,4,256]{2,1,0:T(4,128)} %project.1), calls=%async_computation | async-start | bytes 262144 | tf_op jit(solution)/shard_map/all_to_all | solution.py:66
  20.2 10.3 %all-to-all-start.1 = ((f32[32,4,256]{2,1,0:T(4,128)}), f32[32,4,256]{2,1,0:T(4,128)S(1)}, u32[]{:S(2)}, u32[]{:S(2)}) async-start(f32[32,4,256]{2,1,0:T(4,128)} %total.2), calls=%async_computation.1 | async-start | bytes 262144 | tf_op jit(solution)/shard_map/all_to_all | solution.py:68
  22.8 1.2 copy-start.2
  24.0 0.9 copy-start.3
  31.2 6.5 %collective-permute-start.2 = (bf16[2,64,256]{2,1,0:T(8,128)(2,1)S(1)}, bf16[2,64,256]{2,1,0:T(8,128)(2,1)S(1)}, u32[]{:S(2)}, u32[]{:S(2)}) collective-permute-start(bf16[2,64,256]{2,1,0:T(8,128)(2,1)S(1)} %get-tuple-element.40), channel_id=1, source_target_pairs={{0,4},{1,5},{2,6},{3,7},{4,0},{5,1},{6,2},{7,3},{8,12},{9,13},{10,... | collective-permute-start | bytes 196616 | tf_op jit(solution)/shard_map/ppermute | solution.py:29
  32.6 5.1 %collective-permute-start = (bf16[2,64,256]{2,1,0:T(8,128)(2,1)S(1)}, bf16[2,64,256]{2,1,0:T(8,128)(2,1)S(1)}, u32[]{:S(2)}, u32[]{:S(2)}) collective-permute-start(bf16[2,64,256]{2,1,0:T(8,128)(2,1)S(1)} %get-tuple-element.40), channel_id=1, source_target_pairs={{0,16},{8,24},{16,0},{24,8},{1,17},{9,25},{17,1},{25,9},{2,18},{10... | collective-permute-start | bytes 196616 | tf_op jit(solution)/shard_map/ppermute | solution.py:29
  37.7 1.4 collective-permute-start.1
  37.8 6.3 %collective-permute-start.3 = (bf16[4,64,256]{2,1,0:T(8,128)(2,1)S(1)}, bf16[4,64,256]{2,1,0:T(8,128)(2,1)S(1)}, u32[]{:S(2)}, u32[]{:S(2)}) collective-permute-start(bf16[4,64,256]{2,1,0:T(8,128)(2,1)S(1)} %get-tuple-element.90), channel_id=1, source_target_pairs={{0,2},{1,3},{2,0},{3,1},{4,6},{5,7},{6,4},{7,5},{8,10},{9,11},{10,... | collective-permute-start | bytes 393224 | tf_op jit(solution)/shard_map/ppermute | solution.py:29
  39.1 9.0 %copy-start = (bf16[64,256,32]{1,2,0:T(8,128)(2,1)S(1)}, bf16[64,256,32]{1,2,0:T(8,128)(2,1)}, u32[]{:S(2)}) copy-start(bf16[64,256,32]{1,2,0:T(8,128)(2,1)} %param.18) | copy-start | bytes 3145732
  39.2 9.0 %copy-start.1 = (bf16[64,256,32]{1,2,0:T(8,128)(2,1)S(1)}, bf16[64,256,32]{1,2,0:T(8,128)(2,1)}, u32[]{:S(2)}) copy-start(bf16[64,256,32]{1,2,0:T(8,128)(2,1)} %param.19) | copy-start | bytes 3145732
  44.2 9.9 %collective-permute-start.4 = (bf16[8,64,256]{2,1,0:T(8,128)(2,1)S(1)}, bf16[8,64,256]{2,1,0:T(8,128)(2,1)S(1)}, u32[]{:S(2)}, u32[]{:S(2)}) collective-permute-start(bf16[8,64,256]{2,1,0:T(8,128)(2,1)S(1)} %gathered.2.refs_0_), channel_id=1, source_target_pairs={{0,1},{1,0},{2,3},{3,2},{4,5},{5,4},{6,7},{7,6},{8,9},{9,8},{10,11... | collective-permute-start | bytes 786440 | tf_op jit(solution)/shard_map/ppermute | solution.py:29
  50.4 9.3 %collective-permute-start.6 = (f32[4,64,256]{2,1,0:T(8,128)S(1)}, f32[4,64,256]{2,1,0:T(8,128)S(1)}, u32[]{:S(2)}, u32[]{:S(2)}) collective-permute-start(f32[4,64,256]{2,1,0:T(8,128)S(1)} %get-tuple-element.80), channel_id=1, source_target_pairs={{0,1},{1,0},{2,3},{3,2},{4,5},{5,4},{6,7},{7,6},{8,9},{9,8},{10,11... | collective-permute-start | bytes 786440 | tf_op jit(solution)/shard_map/ppermute | solution.py:29
  50.5 9.2 %collective-permute-start.5 = (f32[4,64,256]{2,1,0:T(8,128)S(1)}, f32[4,64,256]{2,1,0:T(8,128)S(1)}, u32[]{:S(2)}, u32[]{:S(2)}) collective-permute-start(f32[4,64,256]{2,1,0:T(8,128)S(1)} %get-tuple-element.81), channel_id=1, source_target_pairs={{0,2},{1,3},{2,0},{3,1},{4,6},{5,7},{6,4},{7,5},{8,10},{9,11},{10,... | collective-permute-start | bytes 786440 | tf_op jit(solution)/shard_map/ppermute | solution.py:29
  59.7 5.5 %collective-permute-start.8 = (f32[2,64,256]{2,1,0:T(8,128)S(1)}, f32[2,64,256]{2,1,0:T(8,128)S(1)}, u32[]{:S(2)}, u32[]{:S(2)}) collective-permute-start(f32[2,64,256]{2,1,0:T(8,128)S(1)} %get-tuple-element.46), channel_id=1, source_target_pairs={{0,2},{1,3},{2,0},{3,1},{4,6},{5,7},{6,4},{7,5},{8,10},{9,11},{10,... | collective-permute-start | bytes 393224 | tf_op jit(solution)/shard_map/ppermute | solution.py:29
  59.8 5.5 %collective-permute-start.7 = (f32[2,64,256]{2,1,0:T(8,128)S(1)}, f32[2,64,256]{2,1,0:T(8,128)S(1)}, u32[]{:S(2)}, u32[]{:S(2)}) collective-permute-start(f32[2,64,256]{2,1,0:T(8,128)S(1)} %get-tuple-element.43.refs_0_), channel_id=1, source_target_pairs={{0,1},{1,0},{2,3},{3,2},{4,5},{5,4},{6,7},{7,6},{8,9},{9,8},{10,11... | collective-permute-start | bytes 393224 | tf_op jit(solution)/shard_map/ppermute | solution.py:29
  65.4 2.5 %collective-permute-start.10 = (f32[4,64,256]{2,1,0:T(8,128)S(1)}, f32[4,64,256]{2,1,0:T(8,128)S(1)}, u32[]{:S(2)}, u32[]{:S(2)}) collective-permute-start(f32[4,64,256]{2,1,0:T(8,128)S(1)} %get-tuple-element.50), channel_id=1, source_target_pairs={{0,8},{8,0},{16,24},{24,16},{1,9},{9,1},{17,25},{25,17},{2,10},{10... | collective-permute-start | bytes 786440 | tf_op jit(solution)/shard_map/ppermute | solution.py:29
  65.5 9.6 %collective-permute-start.9 = (f32[2,64,256]{2,1,0:T(8,128)S(1)}, f32[2,64,256]{2,1,0:T(8,128)S(1)}, u32[]{:S(2)}, u32[]{:S(2)}) collective-permute-start(f32[2,64,256]{2,1,0:T(8,128)S(1)} %get-tuple-element.48), channel_id=1, source_target_pairs={{0,4},{1,5},{2,6},{3,7},{4,0},{5,1},{6,2},{7,3},{8,12},{9,13},{10,... | collective-permute-start | bytes 393224 | tf_op jit(solution)/shard_map/ppermute | solution.py:29
  68.0 7.2 %collective-permute-start.11 = (f32[2,64,256]{2,1,0:T(8,128)S(1)}, f32[2,64,256]{2,1,0:T(8,128)S(1)}, u32[]{:S(2)}, u32[]{:S(2)}) collective-permute-start(f32[2,64,256]{2,1,0:T(8,128)S(1)} %get-tuple-element.86), channel_id=1, source_target_pairs={{0,16},{8,24},{16,0},{24,8},{1,17},{9,25},{17,1},{25,9},{2,18},{10... | collective-permute-start | bytes 393224 | tf_op jit(solution)/shard_map/ppermute | solution.py:29
  105.7 6.6 %collective-permute-start.14 = (bf16[2,64,256]{2,1,0:T(8,128)(2,1)S(1)}, bf16[2,64,256]{2,1,0:T(8,128)(2,1)S(1)}, u32[]{:S(2)}, u32[]{:S(2)}) collective-permute-start(bf16[2,64,256]{2,1,0:T(8,128)(2,1)S(1)} %get-tuple-element.54), channel_id=1, source_target_pairs={{0,4},{1,5},{2,6},{3,7},{4,0},{5,1},{6,2},{7,3},{8,12},{9,13},{10,... | collective-permute-start | bytes 196616 | tf_op jit(solution)/shard_map/ppermute | solution.py:29
  107.3 5.0 %collective-permute-start.12 = (bf16[2,64,256]{2,1,0:T(8,128)(2,1)S(1)}, bf16[2,64,256]{2,1,0:T(8,128)(2,1)S(1)}, u32[]{:S(2)}, u32[]{:S(2)}) collective-permute-start(bf16[2,64,256]{2,1,0:T(8,128)(2,1)S(1)} %get-tuple-element.54), channel_id=1, source_target_pairs={{0,16},{8,24},{16,0},{24,8},{1,17},{9,25},{17,1},{25,9},{2,18},{10... | collective-permute-start | bytes 196616 | tf_op jit(solution)/shard_map/ppermute | solution.py:29
  112.4 1.4 collective-permute-start.13
  112.5 5.9 %collective-permute-start.15 = (bf16[4,64,256]{2,1,0:T(8,128)(2,1)S(1)}, bf16[4,64,256]{2,1,0:T(8,128)(2,1)S(1)}, u32[]{:S(2)}, u32[]{:S(2)}) collective-permute-start(bf16[4,64,256]{2,1,0:T(8,128)(2,1)S(1)} %get-tuple-element.88), channel_id=1, source_target_pairs={{0,2},{1,3},{2,0},{3,1},{4,6},{5,7},{6,4},{7,5},{8,10},{9,11},{10,... | collective-permute-start | bytes 393224 | tf_op jit(solution)/shard_map/ppermute | solution.py:29
  119.7 9.3 %collective-permute-start.16 = (bf16[8,64,256]{2,1,0:T(8,128)(2,1)S(1)}, bf16[8,64,256]{2,1,0:T(8,128)(2,1)S(1)}, u32[]{:S(2)}, u32[]{:S(2)}) collective-permute-start(bf16[8,64,256]{2,1,0:T(8,128)(2,1)S(1)} %gathered.3.refs_0_), channel_id=1, source_target_pairs={{0,1},{1,0},{2,3},{3,2},{4,5},{5,4},{6,7},{7,6},{8,9},{9,8},{10,11... | collective-permute-start | bytes 786440 | tf_op jit(solution)/shard_map/ppermute | solution.py:29
  123.3 10.0 %collective-permute-start.18 = (f32[4,64,256]{2,1,0:T(8,128)S(1)}, f32[4,64,256]{2,1,0:T(8,128)S(1)}, u32[]{:S(2)}, u32[]{:S(2)}) collective-permute-start(f32[4,64,256]{2,1,0:T(8,128)S(1)} %get-tuple-element.76), channel_id=1, source_target_pairs={{0,1},{1,0},{2,3},{3,2},{4,5},{5,4},{6,7},{7,6},{8,9},{9,8},{10,11... | collective-permute-start | bytes 786440 | tf_op jit(solution)/shard_map/ppermute | solution.py:29
  124.1 9.2 %collective-permute-start.17 = (f32[4,64,256]{2,1,0:T(8,128)S(1)}, f32[4,64,256]{2,1,0:T(8,128)S(1)}, u32[]{:S(2)}, u32[]{:S(2)}) collective-permute-start(f32[4,64,256]{2,1,0:T(8,128)S(1)} %get-tuple-element.77), channel_id=1, source_target_pairs={{0,2},{1,3},{2,0},{3,1},{4,6},{5,7},{6,4},{7,5},{8,10},{9,11},{10,... | collective-permute-start | bytes 786440 | tf_op jit(solution)/shard_map/ppermute | solution.py:29
  133.4 5.0 %collective-permute-start.20 = (f32[2,64,256]{2,1,0:T(8,128)S(1)}, f32[2,64,256]{2,1,0:T(8,128)S(1)}, u32[]{:S(2)}, u32[]{:S(2)}) collective-permute-start(f32[2,64,256]{2,1,0:T(8,128)S(1)} %get-tuple-element.58), channel_id=1, source_target_pairs={{0,2},{1,3},{2,0},{3,1},{4,6},{5,7},{6,4},{7,5},{8,10},{9,11},{10,... | collective-permute-start | bytes 393224 | tf_op jit(solution)/shard_map/ppermute | solution.py:29
  133.7 5.0 %collective-permute-start.19 = (f32[2,64,256]{2,1,0:T(8,128)S(1)}, f32[2,64,256]{2,1,0:T(8,128)S(1)}, u32[]{:S(2)}, u32[]{:S(2)}) collective-permute-start(f32[2,64,256]{2,1,0:T(8,128)S(1)} %get-tuple-element.55.refs_0_), channel_id=1, source_target_pairs={{0,1},{1,0},{2,3},{3,2},{4,5},{5,4},{6,7},{7,6},{8,9},{9,8},{10,11... | collective-permute-start | bytes 393224 | tf_op jit(solution)/shard_map/ppermute | solution.py:29
  138.7 3.2 %collective-permute-start.22 = (f32[4,64,256]{2,1,0:T(8,128)S(1)}, f32[4,64,256]{2,1,0:T(8,128)S(1)}, u32[]{:S(2)}, u32[]{:S(2)}) collective-permute-start(f32[4,64,256]{2,1,0:T(8,128)S(1)} %get-tuple-element.62), channel_id=1, source_target_pairs={{0,8},{8,0},{16,24},{24,16},{1,9},{9,1},{17,25},{25,17},{2,10},{10... | collective-permute-start | bytes 786440 | tf_op jit(solution)/shard_map/ppermute | solution.py:29
  138.8 10.0 %collective-permute-start.21 = (f32[2,64,256]{2,1,0:T(8,128)S(1)}, f32[2,64,256]{2,1,0:T(8,128)S(1)}, u32[]{:S(2)}, u32[]{:S(2)}) collective-permute-start(f32[2,64,256]{2,1,0:T(8,128)S(1)} %get-tuple-element.60), channel_id=1, source_target_pairs={{0,4},{1,5},{2,6},{3,7},{4,0},{5,1},{6,2},{7,3},{8,12},{9,13},{10,... | collective-permute-start | bytes 393224 | tf_op jit(solution)/shard_map/ppermute | solution.py:29
  142.0 6.8 %collective-permute-start.23 = (f32[2,64,256]{2,1,0:T(8,128)S(1)}, f32[2,64,256]{2,1,0:T(8,128)S(1)}, u32[]{:S(2)}, u32[]{:S(2)}) collective-permute-start(f32[2,64,256]{2,1,0:T(8,128)S(1)} %get-tuple-element.84), channel_id=1, source_target_pairs={{0,16},{8,24},{16,0},{24,8},{1,17},{9,25},{17,1},{25,9},{2,18},{10... | collective-permute-start | bytes 393224 | tf_op jit(solution)/shard_map/ppermute | solution.py:29
  149.2 1.2 collective-permute-start.24
  150.4 4.2 %collective-permute-start.25 = (f32[32,128]{1,0:T(8,128)S(1)}, f32[32,128]{1,0:T(8,128)S(1)}, u32[]{:S(2)}, u32[]{:S(2)}) collective-permute-start(f32[32,128]{1,0:T(8,128)S(1)} %add.140), channel_id=1, source_target_pairs={{0,16},{8,24},{16,0},{24,8},{1,17},{9,25},{17,1},{25,9},{2,18},{10... | collective-permute-start | bytes 49160 | tf_op jit(solution)/shard_map/ppermute | solution.py:29
  (2 other events, 1.4 us)

commit v5 on v4

--- a/solution.py
+++ b/solution.py
@@ -512,7 +512,8 @@
         col_side = row_side = packed
         for mask in gather_row:
             col_side = jnp.concatenate([col_side, swap(col_side, "row", mask)], axis=0)
-        for mask in gather_col[:-1]:
+        (row_side,) = call(copy_kernel, [(packed.shape, BF16)], "gathered", [packed], [col_side])
+        for mask in gather_col[:-2]:
             row_side = jnp.concatenate([row_side, swap(row_side, "col", mask)], axis=0)
         near = (count, col_src, row_dst)
         forward, *streamed = near_products(
@@ -522,12 +523,17 @@
         (row_side,) = call(
             copy_kernel, [(row_side.shape, BF16)], "gathered", [row_side], [forward]
         )
+        other_side = swap(row_side, "col", gather_col[-2])
         (forward,) = near_products(
             True, col_side, held, *near, part=(1, 2), start=forward, after=[row_side]
         )
+        row_side = jnp.concatenate([row_side, other_side], axis=0)
+        (row_side,) = call(
+            copy_kernel, [(row_side.shape, BF16)], "gathered", [row_side], [forward]
+        )
         other_side = swap(row_side, "col", gather_col[-1])
         forward = far_products(
-            True, col_side, far_col_src, far_row_dst, right, left, start=forward
+            True, col_side, far_col_src, far_row_dst, right, left, start=forward, after=[row_side]
         )
         row_side = jnp.concatenate([row_side, other_side], axis=0)
 

time: 171 us -> 179 us (1.047)
  Pallas kernels: 39.9 us -> 49.3 us
  starting transfers between devices: 34.2 us -> 30.5 us
  waiting for transfers between devices: 52.2 us -> 55 us
    pallas_call x6, Pallas kernels: 14.3 us -> 23.6 us  [near_products(): pl.pallas_call(body, out_shape=[total, jax.ShapeDtypeStruct(tiles.shape,...]
    ppermute x26, starting transfers between devices: 24.3 us -> 20.6 us  [swap(): return lax.ppermute(value, axis, pairs)]
    ppermute x26, waiting for transfers between devices: 42.5 us -> 45.3 us  [swap(): return lax.ppermute(value, axis, pairs)]
    pallas_call x13 -> x17, Pallas kernels: 13.3 us -> 13.3 us  [call(): pl.pallas_call(body, out_shape=[jax.ShapeDtypeStruct(shape, dtype) for sh...]
  transfers between devices with their start and end apart: 28 -> 28, of which waited for: 19 -> 18; matrix products, arithmetic and copies ran while one was open for 3% -> 2% of each run, Pallas kernels for 13% -> 17%
where the time goes in v5:
time: 179 us; the launch traced here: 178 us
  waiting for transfers between devices  55 us (31%)
  Pallas kernels  49.3 us (28%)
  blocking collectives  34 us (19%)
  starting transfers between devices  30.5 us (17%)
  local copies, waits for them, and re-layouts  4.99 us (3%)
  other arithmetic  2.98 us (2%)
    ppermute x26, waiting for transfers between devices, swap(): return lax.ppermute(value, axis, pairs)  45.3 us
    pallas_call x6, Pallas kernels, near_products(): pl.pallas_call(body, out_shape=[total, jax.ShapeDtypeStruct(tiles.shape,...  23.6 us
    ppermute x26, starting transfers between devices, swap(): return lax.ppermute(value, axis, pairs)  20.6 us
    pallas_call x17, Pallas kernels, call(): pl.pallas_call(body, out_shape=[jax.ShapeDtypeStruct(shape, dtype) for sh...  13.3 us
    all_to_all x1, blocking collectives, spread_sum(): got = lax.all_to_all(pieces, axes, 0, 0, tiled=True)  12.3 us
    all_to_all x1, blocking collectives, spread_sum(): return lax.all_to_all(same, axes, 0, 0, tiled=True)  11.4 us
    all_to_all x1, blocking collectives, local(): lax.all_to_all(jnp.broadcast_to(partial, (n_col, *partial.shape)), 'col',...  10.3 us
    pallas_call x4, Pallas kernels, far_products(): pl.pallas_call(body, out_shape=jax.ShapeDtypeStruct(total, F32), in_specs...  8.36 us
  transfers between devices with their start and end apart: 28, of which 18 were waited for; matrix products, arithmetic and copies ran while one was open for 2% of the time, Pallas kernels for 17%

profile of v5, /device:TPU:0, one launch (start us, length us, event | category | flops | bytes accessed | tf_op | source)
XLA Modules:
  0.0 177.8 jit_solution(17752068964181462553)
XLA Ops:
  0.6 3.8 %project.1 = f32[32,4,256]{2,1,0:T(4,128)} custom-call(f32[64,512]{1,0:T(8,128)} %rhs_hbm.1, f32[512,512]{1,0:T(8,128)} %factor_hbm.1), custom_call_target="tpu_custom_call" | custom-call | tf_op jit(solution)/shard_map/project/pallas_call | solution.py:288
  4.4 7.3 %all-to-all-start = ((f32[32,4,256]{2,1,0:T(4,128)}), f32[32,4,256]{2,1,0:T(4,128)S(1)}, u32[]{:S(2)}, u32[]{:S(2)}) async-start(f32[32,4,256]{2,1,0:T(4,128)} %project.1), calls=%async_computation | async-start | bytes 262144 | tf_op jit(solution)/shard_map/all_to_all | solution.py:66
  13.1 6.4 %all-to-all-done.refs_0_ = f32[32,4,256]{2,1,0:T(4,128)S(1)} async-done(((f32[32,4,256]{2,1,0:T(4,128)}), f32[32,4,256]{2,1,0:T(4,128)S(1)}, u32[]{:S(2)}, u32[]{:S(2)}) %all-to-all-start) | async-done | bytes 131104 | tf_op jit(solution)/shard_map/all_to_all | solution.py:66
  20.2 2.6 %all-to-all-start.1 = ((f32[32,4,256]{2,1,0:T(4,128)}), f32[32,4,256]{2,1,0:T(4,128)S(1)}, u32[]{:S(2)}, u32[]{:S(2)}) async-start(f32[32,4,256]{2,1,0:T(4,128)} %total.2), calls=%async_computation.1 | async-start | bytes 262144 | tf_op jit(solution)/shard_map/all_to_all | solution.py:68
  27.2 3.3 %all-to-all-done.1.refs_3_.refs_4_ = f32[32,4,256]{2,1,0:T(4,128)S(1)} async-done(((f32[32,4,256]{2,1,0:T(4,128)}), f32[32,4,256]{2,1,0:T(4,128)S(1)}, u32[]{:S(2)}, u32[]{:S(2)}) %all-to-all-start.1) | async-done | bytes 131104 | tf_op jit(solution)/shard_map/all_to_all | solution.py:68
  38.4 6.4 %near_forward.4 = (f32[16,64,256]{2,1,0:T(8,128)S(1)}, bf16[128,256,256]{2,1,0:T(8,128)(2,1)S(1)}) custom-call(s32[1]{0:T(128)} %dynamic_slice.3.refs_0_.refs_1_, s32[128]{0:T(128)S(1)} %get-tuple-element.88.refs_1_.refs_2_.refs_3_, s32[128]{0:T(128)S(1)} %get-tuple-element.89.refs_2_.refs_3_, ...), custom_call_target="tpu_custom_call" | custom-call | flops 2147483648 | bytes 16777216 | tf_op jit(solution)/shard_map/near_forward/pallas_call | solution.py:133
  44.9 2.7 %near_forward.5.refs_0_.refs_6_ = f32[16,64,256]{2,1,0:T(8,128)S(1)} custom-call(bf16[4,64,256]{2,1,0:T(8,128)(2,1)S(1)} %gathered.7.refs_0_, s32[1]{0:T(128)} %dynamic_slice.3.refs_0_.refs_1_, s32[128]{0:T(128)S(1)} %get-tuple-element.88.refs_1_.refs_2_.refs_3_, s32[128]{0:T(128)S(1)} %get-tuple-element.89.refs_2_.refs_3_, ...), custom_call_target="tpu_custom_call" | custom-call | flops 2147483648 | bytes 16777216 | tf_op jit(solution)/shard_map/near_forward/pallas_call | solution.py:133
  47.6 2.3 %collective-permute-done.3 = bf16[4,64,256]{2,1,0:T(8,128)(2,1)S(1)} collective-permute-done((bf16[4,64,256]{2,1,0:T(8,128)(2,1)S(1)}, bf16[4,64,256]{2,1,0:T(8,128)(2,1)S(1)}, u32[]{:S(2)}, u32[]{:S(2)}) %collective-permute-start.3) | collective-permute-done | bytes 131104 | tf_op jit(solution)/shard_map/ppermute | solution.py:29
  50.3 2.1 %far_forward.2 = f32[16,64,256]{2,1,0:T(8,128)S(1)} custom-call(bf16[8,64,256]{2,1,0:T(8,128)(2,1)S(1)} %gathered.8.refs_0_, s32[64]{0:T(128)S(1)} %fusion.refs_1_, s32[64]{0:T(128)S(1)} %get-tuple-element.72.refs_2_, bf16[8,64,256]{2,1,0:T(8,128)(2,1)S(1)} %constant_dynamic-update-slice_fusion.refs_3_.refs_0_.refs_4_, bf16[2048,256]{1,0:T(8,128)(2,1)S(1)} %bitcast.12, ...), custom_call_target="tpu_custom_call" | custom-call | flops 67108864 | bytes 1048576 | tf_op jit(solution)/shard_map/far_forward/pallas_call | solution.py:187
  52.5 1.8 %collective-permute-start.6 = (f32[4,64,256]{2,1,0:T(8,128)S(1)}, f32[4,64,256]{2,1,0:T(8,128)S(1)}, u32[]{:S(2)}, u32[]{:S(2)}) collective-permute-start(f32[4,64,256]{2,1,0:T(8,128)S(1)} %get-tuple-element.80), channel_id=1, source_target_pairs={{0,1},{1,0},{2,3},{3,2},{4,5},{5,4},{6,7},{7,6},{8,9},{9,8},{10,11... | collective-permute-start | bytes 786440 | tf_op jit(solution)/shard_map/ppermute | solution.py:29
  54.3 4.6 %collective-permute-done.4 = bf16[8,64,256]{2,1,0:T(8,128)(2,1)S(1)} collective-permute-done((bf16[8,64,256]{2,1,0:T(8,128)(2,1)S(1)}, bf16[8,64,256]{2,1,0:T(8,128)(2,1)S(1)}, u32[]{:S(2)}, u32[]{:S(2)}) %collective-permute-start.4) | collective-permute-done | bytes 262176 | tf_op jit(solution)/shard_map/ppermute | solution.py:29
  59.0 2.1 %far_transposed.2.refs_0_.refs_6_ = f32[8,64,256]{2,1,0:T(8,128)S(1)} custom-call(s32[64]{0:T(128)S(1)} %multiply_add_fusion.3.refs_0_, s32[64]{0:T(128)S(1)} %fusion.refs_1_, bf16[16,64,256]{2,1,0:T(8,128)(2,1)S(1)} %pad_maximum_fusion.refs_2_.refs_4_, bf16[2048,256]{1,0:T(8,128)(2,1)S(1)} %bitcast.9, bf16[2048,256]{1,0:T(8,128)(2,1)S(1)} %bitcast.13), custom_call_target="tpu_custom_call" | custom-call | flops 67108864 | bytes 1048576 | tf_op jit(solution)/shard_map/far_transposed/pallas_call | solution.py:187
  63.4 3.9 %near_transposed.2.refs_0_ = f32[8,64,256]{2,1,0:T(8,128)S(1)} custom-call(f32[2,64,256]{2,1,0:T(8,128)S(1)} %get-tuple-element.43.refs_0_, s32[1]{0:T(128)} %dynamic_slice.3.refs_0_.refs_1_, s32[128]{0:T(128)S(1)} %get-tuple-element.68.refs_2_, s32[128]{0:T(128)S(1)} %get-tuple-element.88.refs_1_.refs_2_.refs_3_, ...), custom_call_target="tpu_custom_call" | custom-call | flops 2147483648 | bytes 16777216 | tf_op jit(solution)/shard_map/near_transposed/pallas_call | solution.py:133
  67.4 4.0 %collective-permute-start.9 = (f32[2,64,256]{2,1,0:T(8,128)S(1)}, f32[2,64,256]{2,1,0:T(8,128)S(1)}, u32[]{:S(2)}, u32[]{:S(2)}) collective-permute-start(f32[2,64,256]{2,1,0:T(8,128)S(1)} %get-tuple-element.48), channel_id=1, source_target_pairs={{0,4},{1,5},{2,6},{3,7},{4,0},{5,1},{6,2},{7,3},{8,12},{9,13},{10,... | collective-permute-start | bytes 393224 | tf_op jit(solution)/shard_map/ppermute | solution.py:29
  71.7 6.6 %collective-permute-done.9.refs_5_ = f32[2,64,256]{2,1,0:T(8,128)S(1)} collective-permute-done((f32[2,64,256]{2,1,0:T(8,128)S(1)}, f32[2,64,256]{2,1,0:T(8,128)S(1)}, u32[]{:S(2)}, u32[]{:S(2)}) %collective-permute-start.9) | collective-permute-done | bytes 131104 | tf_op jit(solution)/shard_map/ppermute | solution.py:29
  79.9 12.3 %all_to_all.25.refs_0_ = f32[32,4,384]{2,1,0:T(4,128)S(1)} all-to-all(f32[32,4,384]{2,1,0:T(4,128)S(1)} %get-tuple-element.51), channel_id=1, replica_groups=mesh['row'=4,'col'=8] {'row','col'}, dimensions={0} | all-to-all | bytes 393216 | tf_op jit(solution)/shard_map/all_to_all | solution.py:66
  92.2 11.4 %all_to_all.26.refs_3_ = f32[32,4,384]{2,1,0:T(4,128)S(1)} all-to-all(f32[32,4,384]{2,1,0:T(4,128)S(1)} %total.3), channel_id=1, replica_groups=mesh['row'=4,'col'=8] {'row','col'}, dimensions={0} | all-to-all | bytes 393216 | tf_op jit(solution)/shard_map/all_to_all | solution.py:68
  103.6 5.8 %advance.1 = (f32[64,512]{1,0:T(8,128)S(1)}, f32[64,512]{1,0:T(8,128)S(1)}, f32[64,512]{1,0:T(8,128)S(1)}, bf16[2,64,256]{2,1,0:T(8,128)(2,1)S(1)}, f32[64,64]{1,0:T(8,128)S(1)}) custom-call(f32[1,512]{1,0:T(1,128)S(1)} %get-tuple-element.36.refs_1_.refs_0_, f32[512,512]{1,0:T(8,128)S(1)} %get-tuple-element.37.refs_2_.refs_1_, ...), custom_call_target="tpu_custom_call" | custom-call | tf_op jit(solution)/shard_map/advance/pallas_call | solution.py:250
  110.4 3.4 %collective-permute-done.12 = bf16[2,64,256]{2,1,0:T(8,128)(2,1)S(1)} collective-permute-done((bf16[2,64,256]{2,1,0:T(8,128)(2,1)S(1)}, bf16[2,64,256]{2,1,0:T(8,128)(2,1)S(1)}, u32[]{:S(2)}, u32[]{:S(2)}) %collective-permute-start.12) | collective-permute-done | bytes 65568 | tf_op jit(solution)/shard_map/ppermute | solution.py:29
  116.9 4.1 %near_forward.6.refs_0_.refs_6_ = f32[16,64,256]{2,1,0:T(8,128)S(1)} custom-call(s32[1]{0:T(128)} %dynamic_slice.3.refs_0_.refs_1_, s32[128]{0:T(128)S(1)} %get-tuple-element.88.refs_1_.refs_2_.refs_3_, s32[128]{0:T(128)S(1)} %get-tuple-element.89.refs_2_.refs_3_, bf16[8,64,256]{2,1,0:T(8,128)(2,1)S(1)} %constant_dynamic-update-slice_fusion.3.refs_3_.refs_0_.refs_4_, ...), custom_call_target="tpu_custom_call" | custom-call | flops 2147483648 | bytes 16777216 | tf_op jit(solution)/shard_map/near_forward/pallas_call | solution.py:133
  122.2 2.7 %near_forward.7.refs_0_.refs_6_ = f32[16,64,256]{2,1,0:T(8,128)S(1)} custom-call(bf16[4,64,256]{2,1,0:T(8,128)(2,1)S(1)} %gathered.10.refs_0_, s32[1]{0:T(128)} %dynamic_slice.3.refs_0_.refs_1_, s32[128]{0:T(128)S(1)} %get-tuple-element.88.refs_1_.refs_2_.refs_3_, s32[128]{0:T(128)S(1)} %get-tuple-element.89.refs_2_.refs_3_, ...), custom_call_target="tpu_custom_call" | custom-call | flops 2147483648 | bytes 16777216 | tf_op jit(solution)/shard_map/near_forward/pallas_call | solution.py:133
  124.9 2.1 %collective-permute-done.15 = bf16[4,64,256]{2,1,0:T(8,128)(2,1)S(1)} collective-permute-done((bf16[4,64,256]{2,1,0:T(8,128)(2,1)S(1)}, bf16[4,64,256]{2,1,0:T(8,128)(2,1)S(1)}, u32[]{:S(2)}, u32[]{:S(2)}) %collective-permute-start.15) | collective-permute-done | bytes 131104 | tf_op jit(solution)/shard_map/ppermute | solution.py:29
  127.0 2.1 %far_forward.3 = f32[16,64,256]{2,1,0:T(8,128)S(1)} custom-call(bf16[8,64,256]{2,1,0:T(8,128)(2,1)S(1)} %gathered.11.refs_0_, s32[64]{0:T(128)S(1)} %fusion.refs_1_, s32[64]{0:T(128)S(1)} %get-tuple-element.72.refs_2_, bf16[8,64,256]{2,1,0:T(8,128)(2,1)S(1)} %constant_dynamic-update-slice_fusion.3.refs_3_.refs_0_.refs_4_, bf16[2048,256]{1,0:T(8,128)(2,1)S(1)} %bitcast.14, ...), custom_call_target="tpu_custom_call" | custom-call | flops 67108864 | bytes 1048576 | tf_op jit(solution)/shard_map/far_forward/pallas_call | solution.py:187
  129.1 1.9 %collective-permute-start.16 = (bf16[8,64,256]{2,1,0:T(8,128)(2,1)S(1)}, bf16[8,64,256]{2,1,0:T(8,128)(2,1)S(1)}, u32[]{:S(2)}, u32[]{:S(2)}) collective-permute-start(bf16[8,64,256]{2,1,0:T(8,128)(2,1)S(1)} %gathered.11.refs_0_), channel_id=1, source_target_pairs={{0,1},{1,0},{2,3},{3,2},{4,5},{5,4},{6,7},{7,6},{8,9},{9,8},{10,11... | collective-permute-start | bytes 786440 | tf_op jit(solution)/shard_map/ppermute | solution.py:29
  131.6 6.8 %collective-permute-done.16 = bf16[8,64,256]{2,1,0:T(8,128)(2,1)S(1)} collective-permute-done((bf16[8,64,256]{2,1,0:T(8,128)(2,1)S(1)}, bf16[8,64,256]{2,1,0:T(8,128)(2,1)S(1)}, u32[]{:S(2)}, u32[]{:S(2)}) %collective-permute-start.16) | collective-permute-done | bytes 262176 | tf_op jit(solution)/shard_map/ppermute | solution.py:29
  138.5 2.1 %far_transposed.3.refs_0_.refs_6_ = f32[8,64,256]{2,1,0:T(8,128)S(1)} custom-call(s32[64]{0:T(128)S(1)} %multiply_add_fusion.3.refs_0_, s32[64]{0:T(128)S(1)} %fusion.refs_1_, bf16[16,64,256]{2,1,0:T(8,128)(2,1)S(1)} %pad_maximum_fusion.1.refs_2_.refs_4_, bf16[2048,256]{1,0:T(8,128)(2,1)S(1)} %bitcast.11, bf16[2048,256]{1,0:T(8,128)(2,1)S(1)} %bitcast.15), custom_call_target="tpu_custom_call" | custom-call | flops 67108864 | bytes 1048576 | tf_op jit(solution)/shard_map/far_transposed/pallas_call | solution.py:187
  143.0 1.7 collective-permute-start.19
  144.7 3.9 %near_transposed.3.refs_0_ = f32[8,64,256]{2,1,0:T(8,128)S(1)} custom-call(f32[2,64,256]{2,1,0:T(8,128)S(1)} %get-tuple-element.55.refs_0_, s32[1]{0:T(128)} %dynamic_slice.3.refs_0_.refs_1_, s32[128]{0:T(128)S(1)} %get-tuple-element.68.refs_2_, s32[128]{0:T(128)S(1)} %get-tuple-element.88.refs_1_.refs_2_.refs_3_, ...), custom_call_target="tpu_custom_call" | custom-call | flops 2147483648 | bytes 16777216 | tf_op jit(solution)/shard_map/near_transposed/pallas_call | solution.py:133
  151.4 7.0 %collective-permute-done.21.refs_3_ = f32[2,64,256]{2,1,0:T(8,128)S(1)} collective-permute-done((f32[2,64,256]{2,1,0:T(8,128)S(1)}, f32[2,64,256]{2,1,0:T(8,128)S(1)}, u32[]{:S(2)}, u32[]{:S(2)}) %collective-permute-start.21) | collective-permute-done | bytes 131104 | tf_op jit(solution)/shard_map/ppermute | solution.py:29
  160.4 3.3 %collective-permute-done.25 = f32[32,128]{1,0:T(8,128)S(1)} collective-permute-done((f32[32,128]{1,0:T(8,128)S(1)}, f32[32,128]{1,0:T(8,128)S(1)}, u32[]{:S(2)}, u32[]{:S(2)}) %collective-permute-start.25) | collective-permute-done | bytes 16416 | tf_op jit(solution)/shard_map/ppermute | solution.py:29
  163.7 10.3 %all_to_all.27.refs_0_ = f32[8,32,128]{2,1,0:T(8,128)S(1)} all-to-all(f32[8,32,128]{2,1,0:T(8,128)S(1)} %broadcast_in_dim.3), channel_id=1, replica_groups=mesh['row'=4,'col'=8] {'col'}, dimensions={0} | all-to-all | bytes 262144 | tf_op jit(solution)/shard_map/all_to_all | solution.py:603
  174.0 3.8 %finish.1 = (f32[64,512]{1,0:T(8,128)}, f32[64,512]{1,0:T(8,128)}) custom-call(f32[8,32,128]{2,1,0:T(8,128)S(1)} %all_to_all.27.refs_0_, f32[64,64]{1,0:T(8,128)S(1)} %get-tuple-element.64.refs_1_, f32[64,512]{1,0:T(8,128)S(1)} %get-tuple-element.65.refs_2_, f32[64,512]{1,0:T(8,128)S(1)} %get-tuple-element.66.refs_3_, ...), custom_call_target="tpu_custom_call" | custom-call | tf_op jit(solution)/shard_map/finish/pallas_call | solution.py:250
  (98 shorter events, 32.3 us)
Async XLA Ops:
  4.4 15.1 %all-to-all-start = ((f32[32,4,256]{2,1,0:T(4,128)}), f32[32,4,256]{2,1,0:T(4,128)S(1)}, u32[]{:S(2)}, u32[]{:S(2)}) async-start(f32[32,4,256]{2,1,0:T(4,128)} %project.1), calls=%async_computation | async-start | bytes 262144 | tf_op jit(solution)/shard_map/all_to_all | solution.py:66
  20.2 10.3 %all-to-all-start.1 = ((f32[32,4,256]{2,1,0:T(4,128)}), f32[32,4,256]{2,1,0:T(4,128)S(1)}, u32[]{:S(2)}, u32[]{:S(2)}) async-start(f32[32,4,256]{2,1,0:T(4,128)} %total.2), calls=%async_computation.1 | async-start | bytes 262144 | tf_op jit(solution)/shard_map/all_to_all | solution.py:68
  22.8 1.2 copy-start.2
  24.0 0.9 copy-start.3
  31.2 4.3 %collective-permute-start = (bf16[2,64,256]{2,1,0:T(8,128)(2,1)S(1)}, bf16[2,64,256]{2,1,0:T(8,128)(2,1)S(1)}, u32[]{:S(2)}, u32[]{:S(2)}) collective-permute-start(bf16[2,64,256]{2,1,0:T(8,128)(2,1)S(1)} %get-tuple-element.40.refs_1_), channel_id=1, source_target_pairs={{0,16},{8,24},{16,0},{24,8},{1,17},{9,25},{17,1},{25,9},{2,18},{10... | collective-permute-start | bytes 196616 | tf_op jit(solution)/shard_map/ppermute | solution.py:29
  35.6 1.4 collective-permute-start.1
  37.0 7.8 %collective-permute-start.2 = (bf16[2,64,256]{2,1,0:T(8,128)(2,1)S(1)}, bf16[2,64,256]{2,1,0:T(8,128)(2,1)S(1)}, u32[]{:S(2)}, u32[]{:S(2)}) collective-permute-start(bf16[2,64,256]{2,1,0:T(8,128)(2,1)S(1)} %gathered.6), channel_id=1, source_target_pairs={{0,4},{1,5},{2,6},{3,7},{4,0},{5,1},{6,2},{7,3},{8,12},{9,13},{10,... | collective-permute-start | bytes 196616 | tf_op jit(solution)/shard_map/ppermute | solution.py:29
  38.4 11.8 %copy-start = (bf16[64,256,32]{1,2,0:T(8,128)(2,1)S(1)}, bf16[64,256,32]{1,2,0:T(8,128)(2,1)}, u32[]{:S(2)}) copy-start(bf16[64,256,32]{1,2,0:T(8,128)(2,1)} %param.18) | copy-start | bytes 3145732
  38.4 11.8 %copy-start.1 = (bf16[64,256,32]{1,2,0:T(8,128)(2,1)S(1)}, bf16[64,256,32]{1,2,0:T(8,128)(2,1)}, u32[]{:S(2)}) copy-start(bf16[64,256,32]{1,2,0:T(8,128)(2,1)} %param.19) | copy-start | bytes 3145732
  44.9 5.0 %collective-permute-start.3 = (bf16[4,64,256]{2,1,0:T(8,128)(2,1)S(1)}, bf16[4,64,256]{2,1,0:T(8,128)(2,1)S(1)}, u32[]{:S(2)}, u32[]{:S(2)}) collective-permute-start(bf16[4,64,256]{2,1,0:T(8,128)(2,1)S(1)} %gathered.7.refs_0_), channel_id=1, source_target_pairs={{0,2},{1,3},{2,0},{3,1},{4,6},{5,7},{6,4},{7,5},{8,10},{9,11},{10,... | collective-permute-start | bytes 393224 | tf_op jit(solution)/shard_map/ppermute | solution.py:29
  50.0 9.0 %collective-permute-start.4 = (bf16[8,64,256]{2,1,0:T(8,128)(2,1)S(1)}, bf16[8,64,256]{2,1,0:T(8,128)(2,1)S(1)}, u32[]{:S(2)}, u32[]{:S(2)}) collective-permute-start(bf16[8,64,256]{2,1,0:T(8,128)(2,1)S(1)} %gathered.8.refs_0_), channel_id=1, source_target_pairs={{0,1},{1,0},{2,3},{3,2},{4,5},{5,4},{6,7},{7,6},{8,9},{9,8},{10,11... | collective-permute-start | bytes 786440 | tf_op jit(solution)/shard_map/ppermute | solution.py:29
  52.5 9.6 %collective-permute-start.6 = (f32[4,64,256]{2,1,0:T(8,128)S(1)}, f32[4,64,256]{2,1,0:T(8,128)S(1)}, u32[]{:S(2)}, u32[]{:S(2)}) collective-permute-start(f32[4,64,256]{2,1,0:T(8,128)S(1)} %get-tuple-element.80), channel_id=1, source_target_pairs={{0,1},{1,0},{2,3},{3,2},{4,5},{5,4},{6,7},{7,6},{8,9},{9,8},{10,11... | collective-permute-start | bytes 786440 | tf_op jit(solution)/shard_map/ppermute | solution.py:29
  54.3 7.7 %collective-permute-start.5 = (f32[4,64,256]{2,1,0:T(8,128)S(1)}, f32[4,64,256]{2,1,0:T(8,128)S(1)}, u32[]{:S(2)}, u32[]{:S(2)}) collective-permute-start(f32[4,64,256]{2,1,0:T(8,128)S(1)} %get-tuple-element.81), channel_id=1, source_target_pairs={{0,2},{1,3},{2,0},{3,1},{4,6},{5,7},{6,4},{7,5},{8,10},{9,11},{10,... | collective-permute-start | bytes 786440 | tf_op jit(solution)/shard_map/ppermute | solution.py:29
  62.1 5.2 %collective-permute-start.8 = (f32[2,64,256]{2,1,0:T(8,128)S(1)}, f32[2,64,256]{2,1,0:T(8,128)S(1)}, u32[]{:S(2)}, u32[]{:S(2)}) collective-permute-start(f32[2,64,256]{2,1,0:T(8,128)S(1)} %get-tuple-element.46), channel_id=1, source_target_pairs={{0,2},{1,3},{2,0},{3,1},{4,6},{5,7},{6,4},{7,5},{8,10},{9,11},{10,... | collective-permute-start | bytes 393224 | tf_op jit(solution)/shard_map/ppermute | solution.py:29
  62.2 5.1 %collective-permute-start.7 = (f32[2,64,256]{2,1,0:T(8,128)S(1)}, f32[2,64,256]{2,1,0:T(8,128)S(1)}, u32[]{:S(2)}, u32[]{:S(2)}) collective-permute-start(f32[2,64,256]{2,1,0:T(8,128)S(1)} %get-tuple-element.43.refs_0_), channel_id=1, source_target_pairs={{0,1},{1,0},{2,3},{3,2},{4,5},{5,4},{6,7},{7,6},{8,9},{9,8},{10,11... | collective-permute-start | bytes 393224 | tf_op jit(solution)/shard_map/ppermute | solution.py:29
  67.4 4.1 %collective-permute-start.10 = (f32[4,64,256]{2,1,0:T(8,128)S(1)}, f32[4,64,256]{2,1,0:T(8,128)S(1)}, u32[]{:S(2)}, u32[]{:S(2)}) collective-permute-start(f32[4,64,256]{2,1,0:T(8,128)S(1)} %get-tuple-element.50), channel_id=1, source_target_pairs={{0,8},{8,0},{16,24},{24,16},{1,9},{9,1},{17,25},{25,17},{2,10},{10... | collective-permute-start | bytes 786440 | tf_op jit(solution)/shard_map/ppermute | solution.py:29
  67.4 10.9 %collective-permute-start.9 = (f32[2,64,256]{2,1,0:T(8,128)S(1)}, f32[2,64,256]{2,1,0:T(8,128)S(1)}, u32[]{:S(2)}, u32[]{:S(2)}) collective-permute-start(f32[2,64,256]{2,1,0:T(8,128)S(1)} %get-tuple-element.48), channel_id=1, source_target_pairs={{0,4},{1,5},{2,6},{3,7},{4,0},{5,1},{6,2},{7,3},{8,12},{9,13},{10,... | collective-permute-start | bytes 393224 | tf_op jit(solution)/shard_map/ppermute | solution.py:29
  71.5 6.8 %collective-permute-start.11 = (f32[2,64,256]{2,1,0:T(8,128)S(1)}, f32[2,64,256]{2,1,0:T(8,128)S(1)}, u32[]{:S(2)}, u32[]{:S(2)}) collective-permute-start(f32[2,64,256]{2,1,0:T(8,128)S(1)} %get-tuple-element.86), channel_id=1, source_target_pairs={{0,16},{8,24},{16,0},{24,8},{1,17},{9,25},{17,1},{25,9},{2,18},{10... | collective-permute-start | bytes 393224 | tf_op jit(solution)/shard_map/ppermute | solution.py:29
  109.5 4.3 %collective-permute-start.12 = (bf16[2,64,256]{2,1,0:T(8,128)(2,1)S(1)}, bf16[2,64,256]{2,1,0:T(8,128)(2,1)S(1)}, u32[]{:S(2)}, u32[]{:S(2)}) collective-permute-start(bf16[2,64,256]{2,1,0:T(8,128)(2,1)S(1)} %get-tuple-element.54.refs_1_), channel_id=1, source_target_pairs={{0,16},{8,24},{16,0},{24,8},{1,17},{9,25},{17,1},{25,9},{2,18},{10... | collective-permute-start | bytes 196616 | tf_op jit(solution)/shard_map/ppermute | solution.py:29
  113.8 1.4 collective-permute-start.13
  115.3 6.6 %collective-permute-start.14 = (bf16[2,64,256]{2,1,0:T(8,128)(2,1)S(1)}, bf16[2,64,256]{2,1,0:T(8,128)(2,1)S(1)}, u32[]{:S(2)}, u32[]{:S(2)}) collective-permute-start(bf16[2,64,256]{2,1,0:T(8,128)(2,1)S(1)} %gathered.9), channel_id=1, source_target_pairs={{0,4},{1,5},{2,6},{3,7},{4,0},{5,1},{6,2},{7,3},{8,12},{9,13},{10,... | collective-permute-start | bytes 196616 | tf_op jit(solution)/shard_map/ppermute | solution.py:29
  121.9 5.0 %collective-permute-start.15 = (bf16[4,64,256]{2,1,0:T(8,128)(2,1)S(1)}, bf16[4,64,256]{2,1,0:T(8,128)(2,1)S(1)}, u32[]{:S(2)}, u32[]{:S(2)}) collective-permute-start(bf16[4,64,256]{2,1,0:T(8,128)(2,1)S(1)} %gathered.10.refs_0_), channel_id=1, source_target_pairs={{0,2},{1,3},{2,0},{3,1},{4,6},{5,7},{6,4},{7,5},{8,10},{9,11},{10,... | collective-permute-start | bytes 393224 | tf_op jit(solution)/shard_map/ppermute | solution.py:29
  129.1 9.3 %collective-permute-start.16 = (bf16[8,64,256]{2,1,0:T(8,128)(2,1)S(1)}, bf16[8,64,256]{2,1,0:T(8,128)(2,1)S(1)}, u32[]{:S(2)}, u32[]{:S(2)}) collective-permute-start(bf16[8,64,256]{2,1,0:T(8,128)(2,1)S(1)} %gathered.11.refs_0_), channel_id=1, source_target_pairs={{0,1},{1,0},{2,3},{3,2},{4,5},{5,4},{6,7},{7,6},{8,9},{9,8},{10,11... | collective-permute-start | bytes 786440 | tf_op jit(solution)/shard_map/ppermute | solution.py:29
  131.1 11.1 %collective-permute-start.18 = (f32[4,64,256]{2,1,0:T(8,128)S(1)}, f32[4,64,256]{2,1,0:T(8,128)S(1)}, u32[]{:S(2)}, u32[]{:S(2)}) collective-permute-start(f32[4,64,256]{2,1,0:T(8,128)S(1)} %get-tuple-element.76), channel_id=1, source_target_pairs={{0,1},{1,0},{2,3},{3,2},{4,5},{5,4},{6,7},{7,6},{8,9},{9,8},{10,11... | collective-permute-start | bytes 786440 | tf_op jit(solution)/shard_map/ppermute | solution.py:29
  131.4 10.9 %collective-permute-start.17 = (f32[4,64,256]{2,1,0:T(8,128)S(1)}, f32[4,64,256]{2,1,0:T(8,128)S(1)}, u32[]{:S(2)}, u32[]{:S(2)}) collective-permute-start(f32[4,64,256]{2,1,0:T(8,128)S(1)} %get-tuple-element.77), channel_id=1, source_target_pairs={{0,2},{1,3},{2,0},{3,1},{4,6},{5,7},{6,4},{7,5},{8,10},{9,11},{10,... | collective-permute-start | bytes 786440 | tf_op jit(solution)/shard_map/ppermute | solution.py:29
  142.3 6.3 %collective-permute-start.20 = (f32[2,64,256]{2,1,0:T(8,128)S(1)}, f32[2,64,256]{2,1,0:T(8,128)S(1)}, u32[]{:S(2)}, u32[]{:S(2)}) collective-permute-start(f32[2,64,256]{2,1,0:T(8,128)S(1)} %get-tuple-element.58), channel_id=1, source_target_pairs={{0,2},{1,3},{2,0},{3,1},{4,6},{5,7},{6,4},{7,5},{8,10},{9,11},{10,... | collective-permute-start | bytes 393224 | tf_op jit(solution)/shard_map/ppermute | solution.py:29
  143.0 5.6 %collective-permute-start.19 = (f32[2,64,256]{2,1,0:T(8,128)S(1)}, f32[2,64,256]{2,1,0:T(8,128)S(1)}, u32[]{:S(2)}, u32[]{:S(2)}) collective-permute-start(f32[2,64,256]{2,1,0:T(8,128)S(1)} %get-tuple-element.55.refs_0_), channel_id=1, source_target_pairs={{0,1},{1,0},{2,3},{3,2},{4,5},{5,4},{6,7},{7,6},{8,9},{9,8},{10,11... | collective-permute-start | bytes 393224 | tf_op jit(solution)/shard_map/ppermute | solution.py:29
  148.7 1.6 collective-permute-start.22
  148.8 9.6 %collective-permute-start.21 = (f32[2,64,256]{2,1,0:T(8,128)S(1)}, f32[2,64,256]{2,1,0:T(8,128)S(1)}, u32[]{:S(2)}, u32[]{:S(2)}) collective-permute-start(f32[2,64,256]{2,1,0:T(8,128)S(1)} %get-tuple-element.60), channel_id=1, source_target_pairs={{0,4},{1,5},{2,6},{3,7},{4,0},{5,1},{6,2},{7,3},{8,12},{9,13},{10,... | collective-permute-start | bytes 393224 | tf_op jit(solution)/shard_map/ppermute | solution.py:29
  150.4 8.0 %collective-permute-start.23 = (f32[2,64,256]{2,1,0:T(8,128)S(1)}, f32[2,64,256]{2,1,0:T(8,128)S(1)}, u32[]{:S(2)}, u32[]{:S(2)}) collective-permute-start(f32[2,64,256]{2,1,0:T(8,128)S(1)} %get-tuple-element.84), channel_id=1, source_target_pairs={{0,16},{8,24},{16,0},{24,8},{1,17},{9,25},{17,1},{25,9},{2,18},{10... | collective-permute-start | bytes 393224 | tf_op jit(solution)/shard_map/ppermute | solution.py:29
  158.7 1.2 collective-permute-start.24
  159.9 3.7 %collective-permute-start.25 = (f32[32,128]{1,0:T(8,128)S(1)}, f32[32,128]{1,0:T(8,128)S(1)}, u32[]{:S(2)}, u32[]{:S(2)}) collective-permute-start(f32[32,128]{1,0:T(8,128)S(1)} %add.140), channel_id=1, source_target_pairs={{0,16},{8,24},{16,0},{24,8},{1,17},{9,25},{17,1},{25,9},{2,18},{10... | collective-permute-start | bytes 49160 | tf_op jit(solution)/shard_map/ppermute | solution.py:29
  (2 other events, 1.4 us)
